TPU v7x, 32 devices: a whole 2x2x4 slice. The times are simulated.
32 devices in a mesh: groups: 2 (over y), adapter: 4 (over z), tensor: 2 (over x), seq: 2 (over core).
Axes of the slice: x: 2, y: 2, z: 4, core: 2. Of those that a mesh axis runs over, the one named last changes fastest.
Arguments:
- hidden: bfloat16 [256, 28672], P(('groups', 'adapter'), ('tensor', 'seq')), parts along dimension 0, may hold values from -6 to 6
- down_matrix: bfloat16 [28672, 8192], P(('tensor', 'seq'), 'adapter'), may hold values from -0.03125 to 0.03125
- adapter_first_factors: bfloat16 [8, 28672, 64], P('adapter', ('tensor', 'seq')), may hold values from -0.03125 to 0.03125
- adapter_second_factors: bfloat16 [8, 64, 8192], P('adapter'), may hold values from -0.75 to 0.75
- adapter_index_rows: int32 [256], P('groups'), parts along dimension 0, may hold values from 0 to 7, as said below
- storage: int32 [16], P('groups'), parts along dimension 0, may hold values from 0 to 7, as said below
Outputs:
- projected: bfloat16 [256, 8192], P(('groups', 'tensor', 'seq'), 'adapter'), parts along dimension 0
There are 2 independent parts, one for each index of `groups`. A program takes and returns all parts, laid end to end along the dimension named above; an argument that names none is the same for every part. Nothing has to cross between parts.
Inputs may be any that keep to these rules, and one draw needn't show every extreme that they name: A permutation of the storage positions; position p lives on index p // 2 of adapter. `adapter_index_rows`: in each aligned block of 32 rows at most 16 rows name adapters stored on one index of adapter; in every draw one index receives exactly 16 rows from every block.
All inputs are finite; a program needn't handle non-finite values.
Results may differ from a plain program's by a relative error of at most 0.0049.
Values may be sent and summed in bfloat16 or wider, within the bound.
No kernel may reach another device: no remote copies, remote signals or barrier semaphores. Data moves between devices by JAX's collectives and lax.ppermute only.
A program may use at most 128 MiB of HBM per device.

v0:
```python
import jax
import jax.numpy as jnp
from jax import lax
from jax.sharding import PartitionSpec as P


def body(
    hidden, down_matrix, adapter_first_factors, adapter_second_factors, adapter_index_rows, storage
):
    owners = lax.axis_size("adapter")
    groups = lax.axis_size(("tensor", "seq"))
    block_of_rows = hidden.shape[0]
    slice_width = hidden.shape[1]
    stored_factors = adapter_first_factors.shape[0]
    rank_extent = adapter_first_factors.shape[2]
    adapters = storage.shape[0]
    capacity = max(2, min(block_of_rows // 2, 2 * block_of_rows // owners))
    present_block_list = owners // groups
    own_index = lax.axis_index("adapter")
    part_index = lax.axis_index(("tensor", "seq"))
    id_match = adapter_index_rows[:, None] == jnp.arange(adapters, dtype=jnp.int32)[None, :]
    position = jnp.sum(jnp.where(id_match, storage[None, :], 0), axis=1)
    owner_blocks = (position // stored_factors).reshape(owners, block_of_rows)
    local_blocks = (position % stored_factors).reshape(owners, block_of_rows)
    owner_hits = (
        owner_blocks[:, :, None] == jnp.arange(owners, dtype=jnp.int32)[None, None, :]
    ).astype(jnp.int32)
    slot_rank = jnp.sum(owner_hits * (jnp.cumsum(owner_hits, axis=1) - 1), axis=2)
    slot_of = owner_blocks * capacity + slot_rank
    slot_range = jnp.arange(capacity, dtype=jnp.int32)
    owned = owner_blocks == own_index
    picker = owned[:, None, :] & (slot_rank[:, None, :] == slot_range[None, :, None])
    local_in = jnp.sum(jnp.where(picker, local_blocks[:, None, :], 0), axis=2)
    h_all = lax.all_gather(hidden, "adapter", axis=0, tiled=True)
    partial_total = lax.psum_scatter(
        jnp.dot(h_all, down_matrix, preferred_element_type=jnp.float32),
        ("tensor", "seq"),
        scatter_dimension=0,
        tiled=True,
    )
    my_slots = lax.dynamic_index_in_dim(slot_of, own_index, 0, keepdims=False)
    send_pick = my_slots[None, :] == jnp.arange(owners * capacity, dtype=jnp.int32)[:, None]
    send_rows = jnp.dot(send_pick.astype(jnp.bfloat16), hidden, preferred_element_type=jnp.float32)
    send_rows = send_rows.astype(jnp.bfloat16).reshape(owners, capacity, slice_width)
    input_rows = lax.all_to_all(send_rows, "adapter", split_axis=0, concat_axis=0, tiled=True)
    product_terms = jnp.einsum(
        "mbw,twk->mbtk", input_rows, adapter_first_factors, preferred_element_type=jnp.float32
    )
    product_terms = product_terms.reshape(
        input_rows.shape[0], input_rows.shape[1], stored_factors * rank_extent
    )
    select_low = (
        local_in[:, :, None] == jnp.arange(stored_factors, dtype=jnp.int32)[None, None, :]
    ).astype(jnp.float32)
    low_part = jnp.sum(
        product_terms.reshape(owners, capacity, stored_factors, rank_extent)
        * select_low[:, :, :, None],
        axis=2,
    )
    low_rank = lax.psum(low_part, ("tensor", "seq")).astype(jnp.bfloat16)
    owned_lowrank_part = lax.dynamic_slice_in_dim(
        low_rank, part_index * present_block_list, present_block_list, 0
    )
    mine_local = lax.dynamic_slice_in_dim(
        local_in, part_index * present_block_list, present_block_list, 0
    )
    widened_rows = jnp.einsum(
        "jwf,sfe->jwse",
        owned_lowrank_part,
        adapter_second_factors,
        preferred_element_type=jnp.float32,
    )
    select_out = (
        mine_local[:, :, None] == jnp.arange(stored_factors, dtype=jnp.int32)[None, None, :]
    ).astype(jnp.float32)
    delta_rows = jnp.sum(widened_rows * select_out[:, :, :, None], axis=2).astype(jnp.bfloat16)
    returned_rows = lax.all_to_all(delta_rows, "adapter", split_axis=2, concat_axis=1, tiled=True)
    my_targets = lax.dynamic_slice_in_dim(
        slot_of, part_index * present_block_list, present_block_list, 0
    )
    target_pick = (
        my_targets[:, :, None] == jnp.arange(owners * capacity, dtype=jnp.int32)[None, None, :]
    ).astype(jnp.bfloat16)
    adapter_delta_rows = jnp.einsum(
        "prs,psd->prd", target_pick, returned_rows, preferred_element_type=jnp.float32
    )
    adapter_delta_rows = adapter_delta_rows.reshape(
        present_block_list * block_of_rows, returned_rows.shape[2]
    )
    return (partial_total + adapter_delta_rows).astype(jnp.bfloat16)


def solution(mesh):
    placed = (
        P(("groups", "adapter"), ("tensor", "seq")),
        P(("tensor", "seq"), "adapter"),
        P("adapter", ("tensor", "seq"), None),
        P("adapter", None, None),
        P("groups"),
        P("groups"),
    )
    return jax.shard_map(
        body,
        mesh=mesh,
        in_specs=placed,
        out_specs=P(("groups", "tensor", "seq"), "adapter"),
        check_vma=False,
    )
```

profile of v0, /device:TPU:0, one launch (start us, length us, event | category | flops | bytes accessed | tf_op | source)
XLA Modules:
  0.0 188.3 jit_solution(588101763510062284)
XLA Ops:
  6.5 0.0 copy-start
  6.5 0.0 all-gather.2.cloned.1.call-start
  6.5 0.7 all-gather.2.cloned.1.call-update
  7.3 0.8 select_reduce_fusion.2
  8.0 0.1 reduce_sum.48
  8.1 0.1 fusion.11
  8.2 0.1 reduce_window_sum.11
  8.3 0.2 select_reduce_fusion
  8.5 2.3 %convolution_convert_fusion = bf16[64,7168]{1,0:T(8,128)(2,1)} fusion(bf16[32,7168]{1,0:T(8,128)(2,1)} %param.6, s32[32]{0:T(128)S(1)} %get-tuple-element.8), kind=kOutput, calls=%fused_computation.1 | convolution fusion | flops 29820928 | bytes 1376384 | tf_op jit(solution)/shard_map/dot_general | solution.py:43
  10.9 6.3 %all-to-all-start = ((bf16[4,16,7168]{2,1,0:T(8,128)(2,1)}), bf16[4,16,7168]{2,1,0:T(8,128)(2,1)S(1)}, u32[]{:S(2)}, u32[]{:S(2)}) async-start(bf16[4,16,7168]{2,1,0:T(8,128)(2,1)} %bitcast.3), calls=%async_computation.1 | async-start | bytes 1835008 | tf_op jit(solution)/shard_map/all_to_all | solution.py:45
  17.2 0.0 reduce-scatter.2.cloned.1.call-start
  17.2 52.9 %all-gather.2.cloned.1.call-done = bf16[128,7168]{1,0:T(8,128)(2,1)} async-done(((bf16[32,7168]{1,0:T(8,128)(2,1)}), bf16[128,7168]{1,0:T(8,128)(2,1)}) %all-gather.2.cloned.1.call-update) | async-done | bytes 1835024 | tf_op jit(solution)/shard_map/all_gather | solution.py:34
  70.1 14.9 %fusion.24 = f32[128,2048]{1,0:T(8,128)} fusion(bf16[128,7168]{1,0:T(8,128)(2,1)} %all-gather.2.cloned.1.call-done, bf16[7168,2048]{1,0:T(8,128)(2,1)} %param.7), kind=kOutput, calls=%fused_computation.45 | convolution fusion | flops 3758096384 | bytes 32243712 | tf_op jit(solution)/shard_map/dot_general | solution.py:36
  85.0 0.0 reduce-scatter.2.cloned.1.call-update
  85.0 0.1 select_reduce_fusion.1
  85.2 0.0 all-to-all-done
  85.2 2.5 %fusion.7 = f32[4,16,64]{2,1,0:T(8,128)S(1)} fusion(bf16[2,7168,64]{1,2,0:T(8,128)(2,1)} %param.8, bf16[4,16,7168]{2,1,0:T(8,128)(2,1)S(1)} %all-to-all-done, f32[4,16,2]{1,2,0:T(2,128)S(1)} %compare_convert_fusion), kind=kOutput, calls=%fused_computation.8 | convolution fusion | flops 117452800 | bytes 2769408 | tf_op jit(solution)/shard_map/mbw,twk->mbtk/dot_general | solution.py:46
  87.7 11.4 %psum.7 = bf16[4,16,64]{2,1,0:T(8,128)(2,1)S(1)} all-reduce(f32[4,16,64]{2,1,0:T(8,128)S(1)} %fusion.7), channel_id=1, replica_groups=mesh['groups'=2,'adapter'=4,'tensor'=2,'seq'=2] {'tensor','seq'}, use_global_device_ids=true, to_apply=%region_6.7 | all-reduce | flops 4096 | bytes 24576 | tf_op jit(solution)/shard_map/psum | solution.py:60
  99.1 0.0 copy-done
  99.1 0.4 fusion.3
  99.5 6.7 %copy.13 = bf16[1,16,8192]{1,0,2:T(2,128)(2,1)} copy(bf16[1,16,8192]{2,1,0:T(8,128)(2,1)S(1)} %bitcast.40) | data formatting | bytes 524288 | tf_op jit(solution)/shard_map/convert_element_type | solution.py:76
  106.2 0.5 broadcast.171
  106.7 46.6 %reduce.2 = bf16[8192,16]{1,0:T(8,128)(2,1)} reduce(bf16[8192,1,16]{2,1,0:T(2,128)(2,1)} %bitcast.38, bf16[]{:T(256)} %broadcast.171), dimensions={1}, to_apply=%bitcast.31.reduce_sub_computation | reduce | bytes 524290
  153.3 3.4 %reshape.203 = bf16[4,2,16384]{2,1,0:T(2,128)(2,1)S(1)} reshape(bf16[8192,16]{1,0:T(8,128)(2,1)} %reduce.2) | data formatting | bytes 524288
  156.7 10.7 %all_to_all.20 = bf16[4,2,16384]{2,1,0:T(2,128)(2,1)S(1)} all-to-all(bf16[4,2,16384]{2,1,0:T(2,128)(2,1)S(1)} %reshape.203), channel_id=1, replica_groups=mesh['groups'=2,'adapter'=4,'tensor'=2,'seq'=2] {'adapter'}, dimensions={0} | all-to-all | bytes 524288 | tf_op jit(solution)/shard_map/all_to_all | solution.py:77
  167.4 4.0 %reshape.204 = bf16[8192,1,16]{2,1,0:T(2,128)(2,1)} reshape(bf16[4,2,16384]{2,1,0:T(2,128)(2,1)S(1)} %all_to_all.20) | data formatting | bytes 524288
  171.4 7.9 %copy.14 = bf16[1,16,8192]{2,1,0:T(8,128)(2,1)S(1)} copy(bf16[1,16,8192]{1,0,2:T(2,128)(2,1)} %bitcast.39) | data formatting | bytes 524288 | tf_op jit(solution)/shard_map/all_to_all | solution.py:77
  179.3 0.2 all_to_all.16
  179.5 0.2 copy.15
  179.6 0.0 reduce-scatter.2.cloned.1.call-done
  179.6 1.8 fusion
  (7 shorter events, 0.1 us)
Async XLA Ops:
  6.5 92.5 %copy-start = (bf16[2,64,8192]{2,1,0:T(8,128)(2,1)S(1)}, bf16[2,64,8192]{2,1,0:T(8,128)(2,1)}, u32[]{:S(2)}) copy-start(bf16[2,64,8192]{2,1,0:T(8,128)(2,1)} %param.9) | copy-start | bytes 6291460
  6.5 63.6 %all-gather.2.cloned.1.call-start = ((), (), s32[]{:S(2)}) async-start(), calls=%async_computation.3 | async-start | bytes 2293760 | tf_op jit(solution)/shard_map/all_gather | solution.py:34
  10.9 74.3 %all-to-all-start = ((bf16[4,16,7168]{2,1,0:T(8,128)(2,1)}), bf16[4,16,7168]{2,1,0:T(8,128)(2,1)S(1)}, u32[]{:S(2)}, u32[]{:S(2)}) async-start(bf16[4,16,7168]{2,1,0:T(8,128)(2,1)} %bitcast.3), calls=%async_computation.1 | async-start | bytes 1835008 | tf_op jit(solution)/shard_map/all_to_all | solution.py:45
  17.2 162.4 %reduce-scatter.2.cloned.1.call-start = ((), (), s32[]{:S(2)}) async-start(), calls=%async_computation.4 | async-start | bytes 1310720 | tf_op jit(solution)/shard_map/reduce_scatter | solution.py:35
Sparse Core Ops, SparseCore 0:
  8.9 61.1 all-gather.1
  85.1 24.0 reduce-scatter.1
where the time goes:
time: 189 us; the launch traced here: 188 us
  waiting for transfers between devices  53.7 us (28%)
  other arithmetic  47.9 us (25%)
  local copies, waits for them, and re-layouts  23 us (12%)
  blocking collectives  22 us (12%)
  matrix products  21.9 us (12%)
  between operations  13.5 us (7%)
  starting transfers between devices  6.33 us (3%)
    all_gather x1, waiting for transfers between devices, body(): h_all = lax.all_gather(hidden, 'adapter', axis=0, tiled=True)  52.9 us
    unnamed x1, other arithmetic  46.6 us
    dot_general x1, matrix products, body(): jnp.dot(h_all, down_matrix, preferred_element_type=jnp.float32)  14.9 us
    psum x1, blocking collectives, body(): low_rank = lax.psum(low_part, ('tensor', 'seq')).astype(jnp.bfloat16)  11.4 us
    all_to_all x1, blocking collectives, body(): lax.all_to_all(delta_rows, 'adapter', split_axis=2, concat_axis=1, tiled=...  10.7 us
    all_to_all x3, local copies, waits for them, and re-layouts, body(): lax.all_to_all(delta_rows, 'adapter', split_axis=2, concat_axis=1, tiled=...  8.2 us
    unnamed x5, local copies, waits for them, and re-layouts  7.97 us
    convert_element_type x1, local copies, waits for them, and re-layouts, body(): jnp.sum(widened_rows * select_out[:, :, :, None], axis=2)  6.71 us
  transfers between devices with their start and end apart: 3, of which 1 were waited for; matrix products, arithmetic and copies ran while one was open for 48% of the time, Pallas kernels for 0%

commit v1 on v0

--- a/solution.py
+++ b/solution.py
@@ -1,7 +1,325 @@
+import functools
+
 import jax
 import jax.numpy as jnp
 from jax import lax
+from jax.experimental import pallas as pl
+from jax.experimental.pallas import tpu as pltpu
 from jax.sharding import PartitionSpec as P
+
+F32 = jnp.float32
+BF16 = jnp.bfloat16
+VMEM_LIMIT = 40 * 1024 * 1024
+
+
+def tile_of(extent, most):
+    tile = most
+    while extent % tile:
+        tile //= 2
+    return tile
+
+
+def gathered(refs):
+    return jnp.concatenate([ref[...] for ref in refs], axis=0)
+
+
+def dot_nt(a, b):
+    return lax.dot_general(a, b, (((1,), (1,)), ((), ())), preferred_element_type=F32)
+
+
+def first_kernel(h0, h1, h2, h3, w_ref, a_ref, base_ref, low_ref):
+    @pl.when(pl.program_id(0) == 0)
+    def _():
+        base_ref[...] = jnp.zeros_like(base_ref)
+        low_ref[...] = jnp.zeros_like(low_ref)
+
+    h = gathered((h0, h1, h2, h3))
+    base_ref[...] += jnp.dot(h, w_ref[...], preferred_element_type=F32)
+    low_ref[...] += dot_nt(h, a_ref[...])
+
+
+def first_half(blocks, w, a, offset):
+    rows, extent = blocks[0].shape
+    width = w.shape[1]
+    low = a.shape[0]
+    tile = tile_of(extent, 512)
+    skip = offset // tile
+    count = len(blocks)
+    return pl.pallas_call(
+        first_kernel,
+        grid=(extent // tile,),
+        in_specs=[pl.BlockSpec((rows, tile), lambda k: (0, k))] * count
+        + [
+            pl.BlockSpec((tile, width), lambda k: (k + skip, 0)),
+            pl.BlockSpec((low, tile), lambda k: (0, k + skip)),
+        ],
+        out_specs=[
+            pl.BlockSpec((count * rows, width), lambda k: (0, 0)),
+            pl.BlockSpec((count * rows, low), lambda k: (0, 0)),
+        ],
+        out_shape=[
+            jax.ShapeDtypeStruct((count * rows, width), F32),
+            jax.ShapeDtypeStruct((count * rows, low), F32),
+        ],
+        compiler_params=pltpu.CompilerParams(vmem_limit_bytes=VMEM_LIMIT),
+        cost_estimate=pl.CostEstimate(
+            flops=2 * count * rows * extent * (width + low),
+            bytes_accessed=2 * extent * (width + low + count * rows) + 4 * count * rows * width,
+            transcendentals=0,
+        ),
+        name="first_half",
+    )(*blocks, w, a)
+
+
+def low_kernel(pick, h0, h1, h2, h3, a_ref, low_in, keep_ref, send_ref, total):
+    step = pl.program_id(0)
+
+    @pl.when(step == 0)
+    def _():
+        total[...] = low_in[...]
+
+    part = dot_nt(gathered((h0, h1, h2, h3)), a_ref[...])
+    total[...] += part.reshape(total.shape)
+
+    @pl.when(step == pl.num_programs(0) - 1)
+    def _():
+        mine = pick[0]
+        for far in range(2):
+            keep_ref[far] = total[2 * far + mine]
+            send_ref[far] = total[2 * far + 1 - mine]
+
+
+def second_low(pick, blocks, a, low_in, offset):
+    rows, extent = blocks[0].shape
+    low = a.shape[0]
+    tile = tile_of(extent, 2048)
+    skip = offset // tile
+    return pl.pallas_call(
+        low_kernel,
+        grid_spec=pltpu.PrefetchScalarGridSpec(
+            num_scalar_prefetch=1,
+            grid=(extent // tile,),
+            in_specs=[pl.BlockSpec((rows, tile), lambda k, s: (0, k))] * 4
+            + [
+                pl.BlockSpec((low, tile), lambda k, s: (0, k + skip)),
+                pl.BlockSpec((4, rows, low), lambda k, s: (0, 0, 0)),
+            ],
+            out_specs=[pl.BlockSpec((2, rows, low), lambda k, s: (0, 0, 0))] * 2,
+            scratch_shapes=[pltpu.VMEM((4, rows, low), F32)],
+        ),
+        out_shape=[jax.ShapeDtypeStruct((2, rows, low), F32)] * 2,
+        compiler_params=pltpu.CompilerParams(vmem_limit_bytes=VMEM_LIMIT),
+        cost_estimate=pl.CostEstimate(
+            flops=8 * rows * extent * low,
+            bytes_accessed=2 * extent * (low + 4 * rows),
+            transcendentals=0,
+        ),
+        name="second_low",
+    )(pick, *blocks, a, low_in.reshape(4, rows, low))
+
+
+def base_kernel(pick, h0, h1, h2, h3, w_ref, base_in, keep_ref, send_ref, total):
+    step = pl.program_id(0)
+
+    @pl.when(step == 0)
+    def _():
+        total[...] = base_in[...]
+
+    part = jnp.dot(gathered((h0, h1, h2, h3)), w_ref[...], preferred_element_type=F32)
+    total[...] += part.reshape(total.shape)
+
+    @pl.when(step == pl.num_programs(0) - 1)
+    def _():
+        mine = pick[0]
+        for far in range(2):
+            keep_ref[far] = total[2 * far + mine]
+            send_ref[far] = total[2 * far + 1 - mine].astype(BF16)
+
+
+def second_base(pick, blocks, w, base_in, offset):
+    rows, extent = blocks[0].shape
+    width = w.shape[1]
+    tile = tile_of(extent, 512)
+    skip = offset // tile
+    return pl.pallas_call(
+        base_kernel,
+        grid_spec=pltpu.PrefetchScalarGridSpec(
+            num_scalar_prefetch=1,
+            grid=(extent // tile,),
+            in_specs=[pl.BlockSpec((rows, tile), lambda k, s: (0, k))] * 4
+            + [
+                pl.BlockSpec((tile, width), lambda k, s: (k + skip, 0)),
+                pl.BlockSpec((4, rows, width), lambda k, s: (0, 0, 0)),
+            ],
+            out_specs=[pl.BlockSpec((2, rows, width), lambda k, s: (0, 0, 0))] * 2,
+            scratch_shapes=[pltpu.VMEM((4, rows, width), F32)],
+        ),
+        out_shape=[
+            jax.ShapeDtypeStruct((2, rows, width), F32),
+            jax.ShapeDtypeStruct((2, rows, width), BF16),
+        ],
+        compiler_params=pltpu.CompilerParams(vmem_limit_bytes=VMEM_LIMIT),
+        cost_estimate=pl.CostEstimate(
+            flops=8 * rows * extent * width,
+            bytes_accessed=2 * extent * (width + 4 * rows) + 8 * rows * width,
+            transcendentals=0,
+        ),
+        name="second_base",
+    )(pick, *blocks, w, base_in.reshape(4, rows, width))
+
+
+def swap_kernel(pick, keep_in, came, keep_ref, send_ref):
+    mine = pick[0]
+    keep_ref[...] = keep_in[mine] + came[mine].astype(F32)
+    send_ref[...] = (keep_in[1 - mine] + came[1 - mine].astype(F32)).astype(send_ref.dtype)
+
+
+def split_sum(pick, keep, came):
+    shape = keep.shape[1:]
+    return pl.pallas_call(
+        swap_kernel,
+        in_specs=[
+            pl.BlockSpec(memory_space=pltpu.SMEM),
+            pl.BlockSpec(memory_space=pltpu.VMEM),
+            pl.BlockSpec(memory_space=pltpu.VMEM),
+        ],
+        out_specs=[pl.BlockSpec(memory_space=pltpu.VMEM)] * 2,
+        out_shape=[jax.ShapeDtypeStruct(shape, F32), jax.ShapeDtypeStruct(shape, came.dtype)],
+        name="split_sum",
+    )(pick, keep, came)
+
+
+def widen_kernel(own, low_a, low_b, owner_row, local_row, rank_row, b_ref, out_ref, *, slots, stored):
+    low = (low_a[...] + low_b[...]).astype(BF16)
+    rows = low.shape[0]
+    slot = lax.broadcasted_iota(jnp.int32, (slots, rows), 0)
+    here = (owner_row[...] == own[0]) & (rank_row[...] == slot)
+    rank_extent = low.shape[1] // stored
+    terms = []
+    for index in range(stored):
+        taken = jnp.where(here & (local_row[...] == index), 1.0, 0.0).astype(BF16)
+        terms.append(
+            jnp.dot(
+                taken,
+                low[:, index * rank_extent : (index + 1) * rank_extent],
+                preferred_element_type=F32,
+            ).astype(BF16)
+        )
+    packed = jnp.concatenate(terms, axis=1)
+    owners, _, width = out_ref.shape
+    for part in range(owners):
+        out_ref[part] = jnp.dot(
+            packed, b_ref[:, part * width : (part + 1) * width], preferred_element_type=F32
+        ).astype(BF16)
+
+
+def widen(own, low_a, low_b, owner_row, local_row, rank_row, b, slots, stored, owners):
+    width = b.shape[1] // owners
+    return pl.pallas_call(
+        functools.partial(widen_kernel, slots=slots, stored=stored),
+        in_specs=[pl.BlockSpec(memory_space=pltpu.SMEM)]
+        + [pl.BlockSpec(memory_space=pltpu.VMEM)] * 6,
+        out_specs=pl.BlockSpec(memory_space=pltpu.VMEM),
+        out_shape=jax.ShapeDtypeStruct((owners, slots, width), BF16),
+        compiler_params=pltpu.CompilerParams(vmem_limit_bytes=VMEM_LIMIT),
+        name="widen",
+    )(own, low_a, low_b, owner_row, local_row, rank_row, b)
+
+
+def last_kernel(own, keep, came, owner_col, rank_col, d0, d1, d2, d3, out_ref):
+    slots = d0.shape[0]
+    rows = keep.shape[0]
+    slot = lax.broadcasted_iota(jnp.int32, (rows, slots), 1)
+    total = keep[...] + came[...].astype(F32)
+    picks = []
+    for step in range(4):
+        owner = lax.rem(own[0] + 4 - step, 4)
+        picks.append(
+            jnp.where((owner_col[...] == owner) & (rank_col[...] == slot), 1.0, 0.0).astype(BF16)
+        )
+    picked = jnp.concatenate(picks, axis=1)
+    rows_back = gathered((d0, d1, d2, d3))
+    delta = jnp.dot(picked, rows_back, preferred_element_type=F32)
+    out_ref[...] = (total + delta).astype(out_ref.dtype)
+
+
+def last(own, keep, came, owner_col, rank_col, deltas):
+    return pl.pallas_call(
+        last_kernel,
+        in_specs=[pl.BlockSpec(memory_space=pltpu.SMEM)]
+        + [pl.BlockSpec(memory_space=pltpu.VMEM)] * 8,
+        out_specs=pl.BlockSpec(memory_space=pltpu.VMEM),
+        out_shape=jax.ShapeDtypeStruct(keep.shape, BF16),
+        name="last",
+    )(own, keep, came, owner_col, rank_col, *deltas)
+
+
+def small_body(
+    hidden, down_matrix, adapter_first_factors, adapter_second_factors, adapter_index_rows, storage
+):
+    owners = 4
+    rows, extent = hidden.shape
+    stored, _, rank_extent = adapter_first_factors.shape
+    adapters = storage.shape[0]
+    slots = max(2, min(rows // 2, 2 * rows // owners))
+    own = lax.axis_index("adapter")
+    far = lax.axis_index("tensor")
+    near = lax.axis_index("seq")
+    part = far * 2 + near
+    half = extent // 2
+
+    a = jnp.swapaxes(adapter_first_factors, 1, 2).reshape(stored * rank_extent, extent)
+    b = adapter_second_factors.reshape(stored * rank_extent, -1)
+    near_pick = jnp.reshape(near ^ (own & 1), (1,)).astype(jnp.int32)
+    far_pick = jnp.reshape(far ^ (own >> 1), (1,)).astype(jnp.int32)
+    own_ref = jnp.reshape(own, (1,)).astype(jnp.int32)
+
+    pairs = [(0, 1), (1, 0), (2, 3), (3, 2)]
+    twos = [(0, 2), (2, 0), (1, 3), (3, 1)]
+    both = [(0, 1), (1, 0)]
+    hop = functools.partial(lax.ppermute, axis_name="adapter")
+
+    parts = [hidden[:, :half], hidden[:, half:]]
+    h2a = hop(parts[0], perm=twos)
+    h1a = hop(parts[0], perm=pairs)
+    h2b = hop(parts[1], perm=twos)
+    h1b = hop(parts[1], perm=pairs)
+    h3a = hop(h2a, perm=pairs)
+    h3b = hop(h2b, perm=pairs)
+    blocks_a = (parts[0], h1a, h2a, h3a)
+    blocks_b = (parts[1], h1b, h2b, h3b)
+
+    mine = lax.dynamic_slice_in_dim(adapter_index_rows, part * rows, rows, 0)
+    match = mine[:, None] == jnp.arange(adapters, dtype=jnp.int32)[None, :]
+    position = jnp.sum(jnp.where(match, storage[None, :], 0), axis=1)
+    owner = position // stored
+    local = position % stored
+    index = jnp.arange(rows, dtype=jnp.int32)
+    rank = jnp.sum(
+        ((owner[:, None] == owner[None, :]) & (index[None, :] < index[:, None])).astype(jnp.int32),
+        axis=1,
+    )
+
+    base_a, low_a = first_half(blocks_a, down_matrix, a, 0)
+    low_keep, low_send = second_low(near_pick, blocks_b, a, low_a, half)
+    low_came = lax.ppermute(low_send, "seq", both)
+    low_keep, low_send = split_sum(far_pick, low_keep, low_came)
+    low_came = lax.ppermute(low_send, "tensor", both)
+
+    base_keep, base_send = second_base(near_pick, blocks_b, down_matrix, base_a, half)
+    base_came = lax.ppermute(base_send, "seq", both)
+    base_keep, base_send = split_sum(far_pick, base_keep, base_came)
+    base_came = lax.ppermute(base_send, "tensor", both)
+
+    wide = widen(
+        own_ref, low_keep, low_came, owner[None, :], local[None, :], rank[None, :], b,
+        slots, stored, owners,
+    )
+    deltas = [lax.dynamic_index_in_dim(wide, own, 0, keepdims=False)]
+    for step in range(1, owners):
+        block = lax.dynamic_index_in_dim(wide, (own + step) % owners, 0, keepdims=False)
+        deltas.append(hop(block, perm=[(i, (i + step) % owners) for i in range(owners)]))
+    return last(own_ref, base_keep, base_came, owner[:, None], rank[:, None], deltas)
 
 
 def body(
@@ -99,8 +417,9 @@
         P("groups"),
         P("groups"),
     )
+    small = mesh.shape["adapter"] == 4 and mesh.shape["tensor"] == 2 and mesh.shape["seq"] == 2
     return jax.shard_map(
-        body,
+        small_body if small else body,
         mesh=mesh,
         in_specs=placed,
         out_specs=P(("groups", "tensor", "seq"), "adapter"),

time: 189 us -> 76.4 us (0.40)
  other arithmetic: 47.9 us -> 1.55 us
  waiting for transfers between devices: 53.7 us -> 27.2 us
  Pallas kernels: 0 us -> 25.2 us
  blocking collectives: 22 us -> 0 us
  matrix products: 21.9 us -> 0 us
  local copies, waits for them, and re-layouts: 23 us -> 8.24 us
  between operations: 13.5 us -> 0.17 us
  starting transfers between devices: 6.33 us -> 13.6 us
    all_gather x1 -> x0, waiting for transfers between devices: 52.9 us -> none  [body(): h_all = lax.all_gather(hidden, 'adapter', axis=0, tiled=True)]
    unnamed x1 -> x0, other arithmetic: 46.6 us -> none
    ppermute x0 -> x13, waiting for transfers between devices: none -> 27.2 us  [the longest x1 8.69 us: small_body(): h2a = hop(parts[0], perm=twos)]
    pallas_call x0 -> x7, Pallas kernels: none -> 25.2 us  [the longest x1 8.78 us: second_base(): pl.pallas_call(base_kernel, grid_spec=pltpu.PrefetchScalarGridSpec(num_sc...]
    dot_general x5 -> x0, matrix products: 21.9 us -> none  [the longest x1 14.9 us: body(): jnp.dot(h_all, down_matrix, preferred_element_type=jnp.float32)]
    ppermute x0 -> x13, starting transfers between devices: none -> 13.6 us  [the longest x1 4.1 us: small_body(): h2a = hop(parts[0], perm=twos)]
    psum x1 -> x0, blocking collectives: 11.4 us -> none  [body(): low_rank = lax.psum(low_part, ('tensor', 'seq')).astype(jnp.bfloat16)]
    all_to_all x1 -> x0, blocking collectives: 10.7 us -> none  [body(): lax.all_to_all(delta_rows, 'adapter', split_axis=2, concat_axis=1, tiled=...]
  transfers between devices with their start and end apart: 3 -> 13, of which waited for: 1 -> 6; matrix products, arithmetic and copies ran while one was open for 48% -> 5% of each run, Pallas kernels for 0% -> 28%
where the time goes in v1:
time: 76.4 us; the launch traced here: 75.9 us
  waiting for transfers between devices  27.2 us (36%)
  Pallas kernels  25.2 us (33%)
  starting transfers between devices  13.6 us (18%)
  local copies, waits for them, and re-layouts  8.24 us (11%)
  other arithmetic  1.55 us (2%)
    pallas_call x1, Pallas kernels, second_base(): pl.pallas_call(base_kernel, grid_spec=pltpu.PrefetchScalarGridSpec(num_sc...  8.78 us
    pallas_call x1, Pallas kernels, first_half(): pl.pallas_call(first_kernel, grid=(extent // tile,), in_specs=[pl.BlockSp...  8.78 us
    ppermute x1, waiting for transfers between devices, small_body(): h2a = hop(parts[0], perm=twos)  8.69 us
    ppermute x1, waiting for transfers between devices, small_body(): h2b = hop(parts[1], perm=twos)  8.2 us
    ppermute x1, waiting for transfers between devices, small_body(): h3a = hop(h2a, perm=pairs)  5.85 us
    unnamed x24, local copies, waits for them, and re-layouts  5.01 us
    ppermute x1, starting transfers between devices, small_body(): h2a = hop(parts[0], perm=twos)  4.1 us
    pallas_call x2, Pallas kernels, split_sum(): pl.pallas_call(swap_kernel, in_specs=[pl.BlockSpec(memory_space=pltpu.SME...  3.27 us
  transfers between devices with their start and end apart: 13, of which 6 were waited for; matrix products, arithmetic and copies ran while one was open for 5% of the time, Pallas kernels for 28%

profile of v1, /device:TPU:0, one launch (start us, length us, event | category | flops | bytes accessed | tf_op | source)
XLA Modules:
  0.0 75.9 jit_solution(3579441336492166974)
XLA Ops:
  0.0 1.1 %fusion.3 = (bf16[32,3584]{1,0:T(8,128)(2,1)S(1)}, bf16[32,3584]{1,0:T(8,128)(2,1)S(1)}) fusion(bf16[32,7168]{1,0:T(8,128)(2,1)} %param.6), kind=kLoop, calls=%fused_computation.26 | loop fusion | bytes 917504 | tf_op jit(solution)/shard_map/slice | solution.py:282
  1.1 4.1 %collective-permute-start.4 = (bf16[32,3584]{1,0:T(8,128)(2,1)S(1)}, bf16[32,3584]{1,0:T(8,128)(2,1)S(1)}, u32[]{:S(2)}, u32[]{:S(2)}) collective-permute-start(bf16[32,3584]{1,0:T(8,128)(2,1)S(1)} %get-tuple-element.25.h0), channel_id=1, source_target_pairs={{0,8},{8,0},{4,12},{12,4},{1,9},{9,1},{5,13},{13,5},{2,10},{10,2},... | collective-permute-start | bytes 688136 | tf_op jit(solution)/shard_map/ppermute | solution.py:283
  5.2 1.6 %collective-permute-start.3 = (bf16[32,3584]{1,0:T(8,128)(2,1)S(1)}, bf16[32,3584]{1,0:T(8,128)(2,1)S(1)}, u32[]{:S(2)}, u32[]{:S(2)}) collective-permute-start(bf16[32,3584]{1,0:T(8,128)(2,1)S(1)} %get-tuple-element.25.h0), channel_id=1, source_target_pairs={{0,4},{4,0},{8,12},{12,8},{1,5},{5,1},{9,13},{13,9},{2,6},{6,2},{1... | collective-permute-start | bytes 688136 | tf_op jit(solution)/shard_map/ppermute | solution.py:284
  7.3 0.7 dynamic_slice.16
  8.0 0.7 select_reduce_fusion
  8.8 8.7 %collective-permute-done.4.h2 = bf16[32,3584]{1,0:T(8,128)(2,1)S(1)} collective-permute-done((bf16[32,3584]{1,0:T(8,128)(2,1)S(1)}, bf16[32,3584]{1,0:T(8,128)(2,1)S(1)}, u32[]{:S(2)}, u32[]{:S(2)}) %collective-permute-start.4) | collective-permute-done | bytes 229408 | tf_op jit(solution)/shard_map/ppermute | solution.py:283
  17.5 8.2 %collective-permute-done.1.h2 = bf16[32,3584]{1,0:T(8,128)(2,1)S(1)} collective-permute-done((bf16[32,3584]{1,0:T(8,128)(2,1)S(1)}, bf16[32,3584]{1,0:T(8,128)(2,1)S(1)}, u32[]{:S(2)}, u32[]{:S(2)}) %collective-permute-start.1) | collective-permute-done | bytes 229408 | tf_op jit(solution)/shard_map/ppermute | solution.py:285
  25.7 0.7 collective-permute-start.2
  26.4 5.9 %collective-permute-done.5.h3 = bf16[32,3584]{1,0:T(8,128)(2,1)S(1)} collective-permute-done((bf16[32,3584]{1,0:T(8,128)(2,1)S(1)}, bf16[32,3584]{1,0:T(8,128)(2,1)S(1)}, u32[]{:S(2)}, u32[]{:S(2)}) %collective-permute-start.5) | collective-permute-done | bytes 229408 | tf_op jit(solution)/shard_map/ppermute | solution.py:287
  32.2 1.5 %copy-done = bf16[2,7168,64]{1,2,0:T(8,128)(2,1)S(1)} copy-done((bf16[2,7168,64]{1,2,0:T(8,128)(2,1)S(1)}, bf16[2,7168,64]{1,2,0:T(8,128)(2,1)}, u32[]{:S(2)}) %copy-start) | copy-done | bytes 1835032
  33.7 8.8 %first_half.1 = (f32[128,2048]{1,0:T(8,128)S(1)}, f32[128,128]{1,0:T(8,128)S(1)}) custom-call(bf16[32,3584]{1,0:T(8,128)(2,1)S(1)} %get-tuple-element.25.h0, bf16[32,3584]{1,0:T(8,128)(2,1)S(1)} %collective-permute-done.3.h1, bf16[32,3584]{1,0:T(8,128)(2,1)S(1)} %collective-permute-done.4.h2, bf16[32,3584]{1,0:T(8,128)(2,1)S(1)} %collective-permute-done.5.h3, ...), custom_call_target="tpu_custom_call" | custom-call | flops 1996488704 | bytes 17563648 | tf_op jit(solution)/shard_map/first_half/pallas_call | solution.py:48
  42.5 1.7 %second_low.1 = (f32[2,32,128]{2,1,0:T(8,128)S(1)}, f32[2,32,128]{2,1,0:T(8,128)S(1)}) custom-call(s32[1]{0:T(128)} %bitcast.2.pick, bf16[32,3584]{1,0:T(8,128)(2,1)S(1)} %get-tuple-element.26.h0, bf16[32,3584]{1,0:T(8,128)(2,1)S(1)} %collective-permute-done.h1, bf16[32,3584]{1,0:T(8,128)(2,1)S(1)} %collective-permute-done.1.h2, ...), custom_call_target="tpu_custom_call" | custom-call | flops 117440512 | bytes 1835008 | tf_op jit(solution)/shard_map/second_low/pallas_call | solution.py:97
  44.3 8.8 %second_base.1 = (f32[2,32,2048]{2,1,0:T(8,128)S(1)}, bf16[2,32,2048]{2,1,0:T(8,128)(2,1)S(1)}) custom-call(s32[1]{0:T(128)} %bitcast.2.pick, bf16[32,3584]{1,0:T(8,128)(2,1)S(1)} %get-tuple-element.26.h0, bf16[32,3584]{1,0:T(8,128)(2,1)S(1)} %collective-permute-done.h1, bf16[32,3584]{1,0:T(8,128)(2,1)S(1)} %collective-permute-done.1.h2, ...), custom_call_target="tpu_custom_call" | custom-call | flops 1879048192 | bytes 16121856 | tf_op jit(solution)/shard_map/second_base/pallas_call | solution.py:144
  53.1 0.8 %copy-done.3 = f32[2,32,2048]{2,1,0:T(8,128)} copy-done((f32[2,32,2048]{2,1,0:T(8,128)}, f32[2,32,2048]{2,1,0:T(8,128)S(1)}, u32[]{:S(2)}) %copy-start.3) | copy-done | bytes 524312
  53.9 0.5 collective-permute-start.6
  54.4 0.6 copy-done.11
  55.0 1.4 %split_sum.3 = (f32[32,128]{1,0:T(8,128)}, f32[32,128]{1,0:T(8,128)}) custom-call(s32[1]{0:T(128)} %bitcast.1.pick, f32[2,32,128]{2,1,0:T(8,128)} %copy-done.4, f32[2,32,128]{2,1,0:T(8,128)} %copy-done.11), custom_call_target="tpu_custom_call" | custom-call | tf_op jit(solution)/shard_map/split_sum/pallas_call | solution.py:179
  56.4 1.5 %collective-permute-start.9 = (f32[32,128]{1,0:T(8,128)}, f32[32,128]{1,0:T(8,128)S(1)}, u32[]{:S(2)}, u32[]{:S(2)}) collective-permute-start(f32[32,128]{1,0:T(8,128)} %get-tuple-element.24), channel_id=1, source_target_pairs={{0,2},{2,0},{1,3},{3,1},{4,6},{6,4},{5,7},{7,5},{8,10},{10,8},{9,1... | collective-permute-start | bytes 49160 | tf_op jit(solution)/shard_map/ppermute | solution.py:307
  58.3 2.1 %collective-permute-done.9.low_b = f32[32,128]{1,0:T(8,128)S(1)} collective-permute-done((f32[32,128]{1,0:T(8,128)}, f32[32,128]{1,0:T(8,128)S(1)}, u32[]{:S(2)}, u32[]{:S(2)}) %collective-permute-start.9) | collective-permute-done | bytes 16416 | tf_op jit(solution)/shard_map/ppermute | solution.py:307
  60.4 0.7 copy-done.5
  61.1 0.6 widen.1
  61.7 0.7 dynamic-slice_bitcast_fusion
  62.4 1.6 %collective-permute-start.12 = (bf16[16,2048]{1,0:T(8,128)(2,1)S(1)}, bf16[16,2048]{1,0:T(8,128)(2,1)S(1)}, u32[]{:S(2)}, u32[]{:S(2)}) collective-permute-start(bf16[16,2048]{1,0:T(8,128)(2,1)S(1)} %get-tuple-element.27), channel_id=1, source_target_pairs={{0,12},{4,0},{8,4},{12,8},{1,13},{5,1},{9,5},{13,9},{2,14},{6,2},{... | collective-permute-start | bytes 196616 | tf_op jit(solution)/shard_map/ppermute | solution.py:321
  63.9 1.1 %collective-permute-start.11 = (bf16[16,2048]{1,0:T(8,128)(2,1)S(1)}, bf16[16,2048]{1,0:T(8,128)(2,1)S(1)}, u32[]{:S(2)}, u32[]{:S(2)}) collective-permute-start(bf16[16,2048]{1,0:T(8,128)(2,1)S(1)} %get-tuple-element.28), channel_id=1, source_target_pairs={{0,8},{4,12},{8,0},{12,4},{1,9},{5,13},{9,1},{13,5},{2,10},{6,14},... | collective-permute-start | bytes 196616 | tf_op jit(solution)/shard_map/ppermute | solution.py:321
  65.4 0.7 copy-done.6
  66.1 1.9 %split_sum.2 = (f32[32,2048]{1,0:T(8,128)}, bf16[32,2048]{1,0:T(8,128)(2,1)}) custom-call(s32[1]{0:T(128)} %bitcast.1.pick, f32[2,32,2048]{2,1,0:T(8,128)} %copy-done.3, bf16[2,32,2048]{2,1,0:T(8,128)(2,1)} %copy-done.6), custom_call_target="tpu_custom_call" | custom-call | tf_op jit(solution)/shard_map/split_sum/pallas_call | solution.py:179
  68.0 1.5 %collective-permute-start.7 = (bf16[32,2048]{1,0:T(8,128)(2,1)}, bf16[32,2048]{1,0:T(8,128)(2,1)S(1)}, u32[]{:S(2)}, u32[]{:S(2)}) collective-permute-start(bf16[32,2048]{1,0:T(8,128)(2,1)} %get-tuple-element.19), channel_id=1, source_target_pairs={{0,2},{2,0},{1,3},{3,1},{4,6},{6,4},{5,7},{7,5},{8,10},{10,8},{9,1... | collective-permute-start | bytes 393224 | tf_op jit(solution)/shard_map/ppermute | solution.py:312
  69.5 0.6 add_select_fusion.owner_col
  70.1 0.7 copy.16.rank_col
  71.1 2.1 %collective-permute-done.7.came = bf16[32,2048]{1,0:T(8,128)(2,1)S(1)} collective-permute-done((bf16[32,2048]{1,0:T(8,128)(2,1)}, bf16[32,2048]{1,0:T(8,128)(2,1)S(1)}, u32[]{:S(2)}, u32[]{:S(2)}) %collective-permute-start.7) | collective-permute-done | bytes 131104 | tf_op jit(solution)/shard_map/ppermute | solution.py:312
  73.2 0.6 copy-done.7
  73.9 2.1 %last.1 = bf16[32,2048]{1,0:T(8,128)(2,1)} custom-call(s32[1]{0:T(128)} %bitcast.own, f32[32,2048]{1,0:T(8,128)} %get-tuple-element.18.keep, bf16[32,2048]{1,0:T(8,128)(2,1)} %copy-done.7, s32[32,1]{1,0:T(8,128)} %add_select_fusion.owner_col, s32[32,1]{1,0:T(8,128)} %copy.16.rank_col, bf16[16,2048]{1,0:T(8,128)(2,1)} %get-tuple-element.30.d0, ...), custom_call_target="tpu_custom_call" | custom-call | tf_op jit(solution)/shard_map/last/pallas_call | solution.py:247
  (35 shorter events, 1.6 us)
Async XLA Ops:
  1.1 16.4 %collective-permute-start.4 = (bf16[32,3584]{1,0:T(8,128)(2,1)S(1)}, bf16[32,3584]{1,0:T(8,128)(2,1)S(1)}, u32[]{:S(2)}, u32[]{:S(2)}) collective-permute-start(bf16[32,3584]{1,0:T(8,128)(2,1)S(1)} %get-tuple-element.25.h0), channel_id=1, source_target_pairs={{0,8},{8,0},{4,12},{12,4},{1,9},{9,1},{5,13},{13,5},{2,10},{10,2},... | collective-permute-start | bytes 688136 | tf_op jit(solution)/shard_map/ppermute | solution.py:283
  5.2 21.2 %collective-permute-start.3 = (bf16[32,3584]{1,0:T(8,128)(2,1)S(1)}, bf16[32,3584]{1,0:T(8,128)(2,1)S(1)}, u32[]{:S(2)}, u32[]{:S(2)}) collective-permute-start(bf16[32,3584]{1,0:T(8,128)(2,1)S(1)} %get-tuple-element.25.h0), channel_id=1, source_target_pairs={{0,4},{4,0},{8,12},{12,8},{1,5},{5,1},{9,13},{13,9},{2,6},{6,2},{1... | collective-permute-start | bytes 688136 | tf_op jit(solution)/shard_map/ppermute | solution.py:284
  6.8 18.9 %collective-permute-start.1 = (bf16[32,3584]{1,0:T(8,128)(2,1)S(1)}, bf16[32,3584]{1,0:T(8,128)(2,1)S(1)}, u32[]{:S(2)}, u32[]{:S(2)}) collective-permute-start(bf16[32,3584]{1,0:T(8,128)(2,1)S(1)} %get-tuple-element.26.h0), channel_id=1, source_target_pairs={{0,8},{8,0},{4,12},{12,4},{1,9},{9,1},{5,13},{13,5},{2,10},{10,2},... | collective-permute-start | bytes 688136 | tf_op jit(solution)/shard_map/ppermute | solution.py:285
  7.1 35.4 %collective-permute-start = (bf16[32,3584]{1,0:T(8,128)(2,1)S(1)}, bf16[32,3584]{1,0:T(8,128)(2,1)S(1)}, u32[]{:S(2)}, u32[]{:S(2)}) collective-permute-start(bf16[32,3584]{1,0:T(8,128)(2,1)S(1)} %get-tuple-element.26.h0), channel_id=1, source_target_pairs={{0,4},{4,0},{8,12},{12,8},{1,5},{5,1},{9,13},{13,9},{2,6},{6,2},{1... | collective-permute-start | bytes 688136 | tf_op jit(solution)/shard_map/ppermute | solution.py:286
  17.4 14.8 %collective-permute-start.5 = (bf16[32,3584]{1,0:T(8,128)(2,1)S(1)}, bf16[32,3584]{1,0:T(8,128)(2,1)S(1)}, u32[]{:S(2)}, u32[]{:S(2)}) collective-permute-start(bf16[32,3584]{1,0:T(8,128)(2,1)S(1)} %collective-permute-done.4.h2), channel_id=1, source_target_pairs={{0,4},{4,0},{8,12},{12,8},{1,5},{5,1},{9,13},{13,9},{2,6},{6,2},{1... | collective-permute-start | bytes 688136 | tf_op jit(solution)/shard_map/ppermute | solution.py:287
  25.7 16.8 %collective-permute-start.2 = (bf16[32,3584]{1,0:T(8,128)(2,1)S(1)}, bf16[32,3584]{1,0:T(8,128)(2,1)S(1)}, u32[]{:S(2)}, u32[]{:S(2)}) collective-permute-start(bf16[32,3584]{1,0:T(8,128)(2,1)S(1)} %collective-permute-done.1.h2), channel_id=1, source_target_pairs={{0,4},{4,0},{8,12},{12,8},{1,5},{5,1},{9,13},{13,9},{2,6},{6,2},{1... | collective-permute-start | bytes 688136 | tf_op jit(solution)/shard_map/ppermute | solution.py:288
  32.2 1.5 %copy-start = (bf16[2,7168,64]{1,2,0:T(8,128)(2,1)S(1)}, bf16[2,7168,64]{1,2,0:T(8,128)(2,1)}, u32[]{:S(2)}) copy-start(bf16[2,7168,64]{1,2,0:T(8,128)(2,1)} %param.8) | copy-start | bytes 5505028
  33.7 8.8 %copy-start.1 = (bf16[2,7168,64]{1,2,0:T(8,128)(2,1)S(1)}, bf16[2,7168,64]{1,2,0:T(8,128)(2,1)}, u32[]{:S(2)}) copy-start(bf16[2,7168,64]{1,2,0:T(8,128)(2,1)} %param.8) | copy-start | bytes 5505028
  44.2 8.9 %copy-start.4 = (f32[2,32,128]{2,1,0:T(8,128)}, f32[2,32,128]{2,1,0:T(8,128)S(1)}, u32[]{:S(2)}) copy-start(f32[2,32,128]{2,1,0:T(8,128)S(1)} %get-tuple-element.21.keep_in) | copy-start | bytes 98308
  44.2 10.2 %collective-permute-start.8 = (f32[2,32,128]{2,1,0:T(8,128)S(1)}, f32[2,32,128]{2,1,0:T(8,128)S(1)}, u32[]{:S(2)}, u32[]{:S(2)}) collective-permute-start(f32[2,32,128]{2,1,0:T(8,128)S(1)} %get-tuple-element.22), channel_id=1, source_target_pairs={{0,1},{1,0},{2,3},{3,2},{4,5},{5,4},{6,7},{7,6},{8,9},{9,8},{10,11... | collective-permute-start | bytes 98312 | tf_op jit(solution)/shard_map/ppermute | solution.py:305
  44.3 16.1 %copy-start.2 = (bf16[2,64,8192]{2,1,0:T(8,128)(2,1)S(1)}, bf16[2,64,8192]{2,1,0:T(8,128)(2,1)}, u32[]{:S(2)}) copy-start(bf16[2,64,8192]{2,1,0:T(8,128)(2,1)} %param.9) | copy-start | bytes 6291460
  53.1 0.8 %copy-start.3 = (f32[2,32,2048]{2,1,0:T(8,128)}, f32[2,32,2048]{2,1,0:T(8,128)S(1)}, u32[]{:S(2)}) copy-start(f32[2,32,2048]{2,1,0:T(8,128)S(1)} %get-tuple-element.16.keep_in) | copy-start | bytes 1572868
  53.9 11.5 %collective-permute-start.6 = (bf16[2,32,2048]{2,1,0:T(8,128)(2,1)S(1)}, bf16[2,32,2048]{2,1,0:T(8,128)(2,1)S(1)}, u32[]{:S(2)}, u32[]{:S(2)}) collective-permute-start(bf16[2,32,2048]{2,1,0:T(8,128)(2,1)S(1)} %get-tuple-element.17), channel_id=1, source_target_pairs={{0,1},{1,0},{2,3},{3,2},{4,5},{5,4},{6,7},{7,6},{8,9},{9,8},{10,11... | collective-permute-start | bytes 786440 | tf_op jit(solution)/shard_map/ppermute | solution.py:310
  54.4 0.6 copy-start.11
  56.4 3.9 %collective-permute-start.9 = (f32[32,128]{1,0:T(8,128)}, f32[32,128]{1,0:T(8,128)S(1)}, u32[]{:S(2)}, u32[]{:S(2)}) collective-permute-start(f32[32,128]{1,0:T(8,128)} %get-tuple-element.24), channel_id=1, source_target_pairs={{0,2},{2,0},{1,3},{3,1},{4,6},{6,4},{5,7},{7,5},{8,10},{10,8},{9,1... | collective-permute-start | bytes 49160 | tf_op jit(solution)/shard_map/ppermute | solution.py:307
  60.4 0.7 copy-start.5
  62.4 8.5 %collective-permute-start.12 = (bf16[16,2048]{1,0:T(8,128)(2,1)S(1)}, bf16[16,2048]{1,0:T(8,128)(2,1)S(1)}, u32[]{:S(2)}, u32[]{:S(2)}) collective-permute-start(bf16[16,2048]{1,0:T(8,128)(2,1)S(1)} %get-tuple-element.27), channel_id=1, source_target_pairs={{0,12},{4,0},{8,4},{12,8},{1,13},{5,1},{9,5},{13,9},{2,14},{6,2},{... | collective-permute-start | bytes 196616 | tf_op jit(solution)/shard_map/ppermute | solution.py:321
  63.9 6.9 %collective-permute-start.11 = (bf16[16,2048]{1,0:T(8,128)(2,1)S(1)}, bf16[16,2048]{1,0:T(8,128)(2,1)S(1)}, u32[]{:S(2)}, u32[]{:S(2)}) collective-permute-start(bf16[16,2048]{1,0:T(8,128)(2,1)S(1)} %get-tuple-element.28), channel_id=1, source_target_pairs={{0,8},{4,12},{8,0},{12,4},{1,9},{5,13},{9,1},{13,5},{2,10},{6,14},... | collective-permute-start | bytes 196616 | tf_op jit(solution)/shard_map/ppermute | solution.py:321
  65.0 6.1 %collective-permute-start.10 = (bf16[16,2048]{1,0:T(8,128)(2,1)S(1)}, bf16[16,2048]{1,0:T(8,128)(2,1)S(1)}, u32[]{:S(2)}, u32[]{:S(2)}) collective-permute-start(bf16[16,2048]{1,0:T(8,128)(2,1)S(1)} %get-tuple-element.29), channel_id=1, source_target_pairs={{0,4},{4,8},{8,12},{12,0},{1,5},{5,9},{9,13},{13,1},{2,6},{6,10},{... | collective-permute-start | bytes 196616 | tf_op jit(solution)/shard_map/ppermute | solution.py:321
  65.4 0.7 copy-start.6
  68.0 5.2 %collective-permute-start.7 = (bf16[32,2048]{1,0:T(8,128)(2,1)}, bf16[32,2048]{1,0:T(8,128)(2,1)S(1)}, u32[]{:S(2)}, u32[]{:S(2)}) collective-permute-start(bf16[32,2048]{1,0:T(8,128)(2,1)} %get-tuple-element.19), channel_id=1, source_target_pairs={{0,2},{2,0},{1,3},{3,1},{4,6},{6,4},{5,7},{7,5},{8,10},{10,8},{9,1... | collective-permute-start | bytes 393224 | tf_op jit(solution)/shard_map/ppermute | solution.py:312
  70.8 2.4 %copy-start.8 = (bf16[16,2048]{1,0:T(8,128)(2,1)}, bf16[16,2048]{1,0:T(8,128)(2,1)S(1)}, u32[]{:S(2)}) copy-start(bf16[16,2048]{1,0:T(8,128)(2,1)S(1)} %collective-permute-done.12.d3) | copy-start | bytes 196612
  70.8 2.4 %copy-start.9 = (bf16[16,2048]{1,0:T(8,128)(2,1)}, bf16[16,2048]{1,0:T(8,128)(2,1)S(1)}, u32[]{:S(2)}) copy-start(bf16[16,2048]{1,0:T(8,128)(2,1)S(1)} %collective-permute-done.11.d2) | copy-start | bytes 196612
  71.1 2.1 %copy-start.10 = (bf16[16,2048]{1,0:T(8,128)(2,1)}, bf16[16,2048]{1,0:T(8,128)(2,1)S(1)}, u32[]{:S(2)}) copy-start(bf16[16,2048]{1,0:T(8,128)(2,1)S(1)} %collective-permute-done.10.d1) | copy-start | bytes 196612
  73.2 0.6 copy-start.7

commit v2 on v0

--- a/solution.py
+++ b/solution.py
@@ -1,7 +1,365 @@
+import functools
+
 import jax
 import jax.numpy as jnp
 from jax import lax
+from jax.experimental import pallas as pl
+from jax.experimental.pallas import tpu as pltpu
 from jax.sharding import PartitionSpec as P
+
+F32 = jnp.float32
+BF16 = jnp.bfloat16
+MIB = 1024 * 1024
+VMEM = pl.BlockSpec(memory_space=pltpu.VMEM)
+SMEM = pl.BlockSpec(memory_space=pltpu.SMEM)
+HBM = pl.BlockSpec(memory_space=pltpu.HBM)
+COLUMNS = 512
+FETCH_MIB = 27
+SHARE = 8
+
+
+def params(limit):
+    return pltpu.CompilerParams(vmem_limit_bytes=limit * MIB)
+
+
+def cost(flops, moved):
+    return pl.CostEstimate(flops=int(flops), bytes_accessed=int(moved), transcendentals=0)
+
+
+def fetch_kernel(*refs, pieces):
+    count = len(pieces)
+    sources, targets, sems = refs[:count], refs[count : 2 * count], refs[2 * count]
+    copies = []
+    for source, target, (axis, start, length, cuts) in zip(sources, targets, pieces):
+        step = length // cuts
+        for cut in range(cuts):
+            if axis == 0:
+                from_ref = source.at[pl.ds(start + cut * step, step)]
+                to_ref = target.at[pl.ds(cut * step, step)]
+            else:
+                from_ref = source.at[:, pl.ds(start + cut * step, step)]
+                to_ref = target.at[:, pl.ds(cut * step, step)]
+            copies.append(pltpu.make_async_copy(from_ref, to_ref, sems.at[len(copies)]))
+    for copy in copies:
+        copy.start()
+    for copy in copies:
+        copy.wait()
+
+
+def fetch(arrays, pieces, name):
+    shapes = []
+    for array, (axis, _, length, _) in zip(arrays, pieces):
+        shape = list(array.shape)
+        shape[axis] = length
+        shapes.append(pltpu.VMEM(tuple(shape), array.dtype))
+    moved = sum(2 * s.shape[0] * s.shape[1] for s in shapes)
+    total = sum(piece[3] for piece in pieces)
+    return pl.pallas_call(
+        functools.partial(fetch_kernel, pieces=pieces),
+        in_specs=[HBM] * len(arrays),
+        out_specs=[VMEM] * len(arrays),
+        out_shape=shapes,
+        scratch_shapes=[pltpu.SemaphoreType.DMA((total,))],
+        compiler_params=params(FETCH_MIB),
+        cost_estimate=cost(0, moved),
+        name=name,
+    )(*arrays)
+
+
+def dot_nt(a, b):
+    return lax.dot_general(a, b, (((1,), (1,)), ((), ())), preferred_element_type=F32)
+
+
+def ordered(picks, blocks):
+    near, far = picks[0] == 1, picks[1] == 1
+    b0, b1, b2, b3 = [block[...] for block in blocks]
+    k0, k2 = jnp.where(near, b1, b0), jnp.where(near, b3, b2)
+    s0, s2 = jnp.where(near, b0, b1), jnp.where(near, b2, b3)
+    return jnp.concatenate(
+        [
+            jnp.where(far, k2, k0),
+            jnp.where(far, k0, k2),
+            jnp.where(far, s2, s0),
+            jnp.where(far, s0, s2),
+        ],
+        axis=0,
+    )
+
+
+def first_kernel(
+    picks, b0, b1, b2, b3, w_far, w_ref, a_ref, base_ref, low_ref, streamed, sems, *, cuts
+):
+    cut = streamed.shape[0]
+    step = cut // cuts
+    copies = []
+    for index in range(cuts):
+        rows = pl.ds(index * step, step)
+        copies.append(pltpu.make_async_copy(w_far.at[rows], streamed.at[rows], sems.at[index]))
+        copies[-1].start()
+    h = ordered(picks, (b0, b1, b2, b3))
+    depth = h.shape[1]
+    low_ref[...] = dot_nt(h, a_ref[:, :depth])
+    for start in range(0, w_ref.shape[1], COLUMNS):
+        columns = slice(start, start + COLUMNS)
+        base_ref[:, columns] = jnp.dot(h[:, cut:], w_ref[:, columns], preferred_element_type=F32)
+    for copy in copies:
+        copy.wait()
+    for start in range(0, w_ref.shape[1], COLUMNS):
+        columns = slice(start, start + COLUMNS)
+        base_ref[:, columns] += jnp.dot(
+            h[:, :cut], streamed[:, columns], preferred_element_type=F32
+        )
+
+
+def first_half(picks, blocks, w_far, w, a, cut):
+    rows, extent = blocks[0].shape
+    width, low = w.shape[1], a.shape[0]
+    cuts = 4
+    return pl.pallas_call(
+        functools.partial(first_kernel, cuts=cuts),
+        in_specs=[SMEM] + [VMEM] * 4 + [HBM] + [VMEM] * 2,
+        out_specs=[VMEM] * 2,
+        out_shape=[
+            jax.ShapeDtypeStruct((4 * rows, width), F32),
+            jax.ShapeDtypeStruct((4 * rows, low), F32),
+        ],
+        scratch_shapes=[pltpu.VMEM((cut, width), BF16), pltpu.SemaphoreType.DMA((cuts,))],
+        compiler_params=params(20),
+        cost_estimate=cost(8 * rows * extent * (width + low), 4 * MIB),
+        name="first_half",
+    )(picks, *blocks, w_far, w, a)
+
+
+def low_kernel(picks, b0, b1, b2, b3, a_ref, low_in, keep_ref, send_ref):
+    h = ordered(picks, (b0, b1, b2, b3))
+    skip = a_ref.shape[1] - h.shape[1]
+    total = low_in[...] + dot_nt(h, a_ref[:, skip:])
+    rows = keep_ref.shape[0]
+    keep_ref[...] = total[:rows]
+    send_ref[...] = total[rows:]
+
+
+def second_low(picks, blocks, a, low_in):
+    rows, extent = blocks[0].shape
+    low = a.shape[0]
+    return pl.pallas_call(
+        low_kernel,
+        in_specs=[SMEM] + [VMEM] * 6,
+        out_specs=[VMEM] * 2,
+        out_shape=[jax.ShapeDtypeStruct((2 * rows, low), F32)] * 2,
+        compiler_params=params(8),
+        cost_estimate=cost(8 * rows * extent * low, MIB),
+        name="second_low",
+    )(picks, *blocks, a, low_in)
+
+
+def base_kernel(picks, b0, b1, b2, b3, w_ref, base_in, keep_ref, send_ref):
+    h = ordered(picks, (b0, b1, b2, b3))
+    rows = keep_ref.shape[0]
+    skip = w_ref.shape[0] - h.shape[1]
+    for start in range(0, w_ref.shape[1], COLUMNS):
+        columns = slice(start, start + COLUMNS)
+        part = jnp.dot(h, w_ref[skip:, columns], preferred_element_type=F32)
+        total = base_in[:, columns] + part
+        keep_ref[:, columns] = total[:rows]
+        send_ref[:, columns] = total[rows:].astype(BF16)
+
+
+def second_base(picks, blocks, w, base_in):
+    rows, extent = blocks[0].shape
+    width = w.shape[1]
+    return pl.pallas_call(
+        base_kernel,
+        in_specs=[SMEM] + [VMEM] * 6,
+        out_specs=[VMEM] * 2,
+        out_shape=[
+            jax.ShapeDtypeStruct((2 * rows, width), F32),
+            jax.ShapeDtypeStruct((2 * rows, width), BF16),
+        ],
+        compiler_params=params(12),
+        cost_estimate=cost(8 * rows * extent * width, 4 * MIB),
+        name="second_base",
+    )(picks, *blocks, w, base_in)
+
+
+def split_kernel(keep_in, came, keep_ref, send_ref):
+    rows = keep_ref.shape[0]
+    total = keep_in[...] + came[...].astype(F32)
+    keep_ref[...] = total[:rows]
+    send_ref[...] = total[rows:].astype(send_ref.dtype)
+
+
+def split_sum(keep, came, name):
+    shape = (keep.shape[0] // 2, keep.shape[1])
+    return pl.pallas_call(
+        split_kernel,
+        in_specs=[VMEM] * 2,
+        out_specs=[VMEM] * 2,
+        out_shape=[jax.ShapeDtypeStruct(shape, F32), jax.ShapeDtypeStruct(shape, came.dtype)],
+        compiler_params=params(4),
+        cost_estimate=cost(0, MIB),
+        name=name,
+    )(keep, came)
+
+
+def plan_kernel(scalars, storage, row_ref, column_ref, into_ref, back_ref, *, stored, slots):
+    own = scalars[0]
+    rows = row_ref.shape[1]
+
+    def position(index):
+        found = jnp.zeros_like(index)
+        for adapter in range(storage.shape[0]):
+            found = jnp.where(index == adapter, storage[adapter], found)
+        return found
+
+    def owner_of(place):
+        owner = jnp.zeros_like(place)
+        for step in range(1, 4):
+            owner += (place >= step * stored).astype(jnp.int32)
+        return owner
+
+    place_row, place_column = position(row_ref[...]), position(column_ref[...])
+    owner_row, owner_column = owner_of(place_row), owner_of(place_column)
+    local_row = place_row - owner_row * stored
+    down = lax.broadcasted_iota(jnp.int32, (rows, rows), 0)
+    across = lax.broadcasted_iota(jnp.int32, (rows, rows), 1)
+    same = owner_column == owner_row
+    rank_row = jnp.sum((same & (down < across)).astype(jnp.int32), axis=0, keepdims=True)
+    rank_column = jnp.sum((same & (across < down)).astype(jnp.int32), axis=1, keepdims=True)
+    slot = lax.broadcasted_iota(jnp.int32, (slots, rows), 0)
+    here = (owner_row == own) & (rank_row == slot)
+    for index in range(stored):
+        taken = here & (local_row == index)
+        into_ref[index] = jnp.where(taken, 1.0, 0.0).astype(BF16)
+    lane = lax.broadcasted_iota(jnp.int32, (rows, 4 * slots), 1)
+    hops = lax.rem(own + 4 - owner_column, 4)
+    back_ref[...] = jnp.where(lane == hops * slots + rank_column, 1.0, 0.0).astype(BF16)
+
+
+def plan(scalars, storage, mine, stored, slots):
+    rows = mine.shape[0]
+    return pl.pallas_call(
+        functools.partial(plan_kernel, stored=stored, slots=slots),
+        in_specs=[SMEM, SMEM, VMEM, VMEM],
+        out_specs=[VMEM] * 2,
+        out_shape=[
+            jax.ShapeDtypeStruct((stored, slots, rows), BF16),
+            jax.ShapeDtypeStruct((rows, 4 * slots), BF16),
+        ],
+        compiler_params=params(2),
+        cost_estimate=cost(0, MIB),
+        name="plan",
+    )(scalars, storage, mine[None, :], mine[:, None])
+
+
+def widen_kernel(scalars, low_a, low_b, into_ref, b_ref, *outs):
+    low = (low_a[...] + low_b[...]).astype(BF16)
+    stored = into_ref.shape[0]
+    rank_extent = low.shape[1] // stored
+    terms = []
+    for index in range(stored):
+        part = low[:, index * rank_extent : (index + 1) * rank_extent]
+        terms.append(jnp.dot(into_ref[index], part, preferred_element_type=F32).astype(BF16))
+    packed = jnp.concatenate(terms, axis=1)
+    width = outs[0].shape[1]
+    for step, out in enumerate(outs):
+        start = pl.multiple_of(lax.rem(scalars[0] + step, len(outs)) * width, width)
+        columns = b_ref[:, pl.ds(start, width)]
+        out[...] = jnp.dot(packed, columns, preferred_element_type=F32).astype(BF16)
+
+
+def widen(scalars, low_a, low_b, into, b, slots, owners):
+    width = b.shape[1] // owners
+    return pl.pallas_call(
+        widen_kernel,
+        in_specs=[SMEM] + [VMEM] * 4,
+        out_specs=[VMEM] * owners,
+        out_shape=[jax.ShapeDtypeStruct((slots, width), BF16)] * owners,
+        compiler_params=params(6),
+        cost_estimate=cost(0, MIB),
+        name="widen",
+    )(scalars, low_a, low_b, into, b)
+
+
+def last_kernel(keep, came, back, d0, d1, d2, d3, out_ref):
+    deltas = jnp.concatenate([d[...] for d in (d0, d1, d2, d3)], axis=0)
+    delta = jnp.dot(back[...], deltas, preferred_element_type=F32)
+    out_ref[...] = (keep[...] + came[...].astype(F32) + delta).astype(out_ref.dtype)
+
+
+def last(keep, came, back, deltas):
+    return pl.pallas_call(
+        last_kernel,
+        in_specs=[VMEM] * 7,
+        out_specs=VMEM,
+        out_shape=jax.ShapeDtypeStruct(keep.shape, BF16),
+        compiler_params=params(4),
+        cost_estimate=cost(0, MIB),
+        name="last",
+    )(keep, came, back, *deltas)
+
+
+def small_body(
+    hidden, down_matrix, adapter_first_factors, adapter_second_factors, adapter_index_rows, storage
+):
+    owners = 4
+    rows, extent = hidden.shape
+    stored, _, rank_extent = adapter_first_factors.shape
+    slots = max(2, min(rows // 2, 2 * rows // owners))
+    own = lax.axis_index("adapter")
+    far = lax.axis_index("tensor")
+    near = lax.axis_index("seq")
+    part = far * 2 + near
+    half = 256 * (extent * SHARE // (256 * 16))
+    cut = half // 2
+    rest = extent - half
+
+    a = jnp.swapaxes(adapter_first_factors, 1, 2).reshape(stored * rank_extent, extent)
+    b = adapter_second_factors.reshape(stored * rank_extent, -1)
+    picks = jnp.stack([near ^ (own & 1), far ^ (own >> 1)]).astype(jnp.int32)
+    scalars = jnp.reshape(own, (1,)).astype(jnp.int32)
+
+    pairs = [(0, 1), (1, 0), (2, 3), (3, 2)]
+    twos = [(0, 2), (2, 0), (1, 3), (3, 1)]
+    both = [(0, 1), (1, 0)]
+    hop = functools.partial(lax.ppermute, axis_name="adapter")
+
+    mine = lax.dynamic_slice_in_dim(adapter_index_rows, part * rows, rows, 0)
+    h0a, h0b = hidden[:, :half], hidden[:, half:]
+    h2a = hop(h0a, perm=twos)
+    h1a = hop(h0a, perm=pairs)
+    into, back = plan(scalars, storage, mine, stored, slots)
+    picks, into, back, down_matrix = lax.optimization_barrier((picks, into, back, down_matrix))
+    w_a, w_b, a, b = fetch(
+        (down_matrix, down_matrix, a, b),
+        ((0, cut, half - cut, 4), (0, half, rest, 7), (1, 0, extent, 1), (1, 0, b.shape[1], 1)),
+        "fetch",
+    )
+    h1a, h2a, h0b, w_a, w_b, a, b = lax.optimization_barrier((h1a, h2a, h0b, w_a, w_b, a, b))
+    h3a = hop(h2a, perm=pairs)
+    h2b = hop(h0b, perm=twos)
+    h1b = hop(h0b, perm=pairs)
+    h3b = hop(h2b, perm=pairs)
+
+    base_a, low_a = first_half(picks, (h0a, h1a, h2a, h3a), down_matrix, w_a, a, cut)
+    h1b, h3b, base_a, low_a = lax.optimization_barrier((h1b, h3b, base_a, low_a))
+    blocks_b = (h0b, h1b, h2b, h3b)
+    low_keep, low_send = second_low(picks, blocks_b, a, low_a)
+    low_keep, low_send, h0b = lax.optimization_barrier((low_keep, low_send, h0b))
+    low_came = lax.ppermute(low_send, "seq", both)
+    base_keep, base_send = second_base(picks, (h0b, h1b, h2b, h3b), w_b, base_a)
+    base_came = lax.ppermute(base_send, "seq", both)
+    low_keep, low_send = split_sum(low_keep, low_came, "split_low")
+    low_came = lax.ppermute(low_send, "tensor", both)
+    base_keep, base_send = split_sum(base_keep, base_came, "split_base")
+    base_send, low_came = lax.optimization_barrier((base_send, low_came))
+    base_came = lax.ppermute(base_send, "tensor", both)
+    wide = widen(scalars, low_keep, low_came, into, b, slots, owners)
+    deltas = [wide[0]]
+    for step in range(1, owners):
+        deltas.append(hop(wide[step], perm=[(i, (i + step) % owners) for i in range(owners)]))
+
+    return last(base_keep, base_came, back, deltas)
 
 
 def body(
@@ -99,8 +457,9 @@
         P("groups"),
         P("groups"),
     )
+    small = mesh.shape["adapter"] == 4 and mesh.shape["tensor"] == 2 and mesh.shape["seq"] == 2
     return jax.shard_map(
-        body,
+        small_body if small else body,
         mesh=mesh,
         in_specs=placed,
         out_specs=P(("groups", "tensor", "seq"), "adapter"),

time: 189 us -> 60 us (0.32)
  other arithmetic: 47.9 us -> 0.07 us
  waiting for transfers between devices: 53.7 us -> 20.5 us
  blocking collectives: 22 us -> 0 us
  matrix products: 21.9 us -> 0 us
  Pallas kernels: 0 us -> 19.2 us
  local copies, waits for them, and re-layouts: 23 us -> 4.05 us
  between operations: 13.5 us -> 0.08 us
  starting transfers between devices: 6.33 us -> 15.9 us
    all_gather x1 -> x0, waiting for transfers between devices: 52.9 us -> none  [body(): h_all = lax.all_gather(hidden, 'adapter', axis=0, tiled=True)]
    unnamed x1 -> x0, other arithmetic: 46.6 us -> none
    dot_general x5 -> x0, matrix products: 21.9 us -> none  [the longest x1 14.9 us: body(): jnp.dot(h_all, down_matrix, preferred_element_type=jnp.float32)]
    ppermute x0 -> x13, waiting for transfers between devices: none -> 20.5 us  [the longest x1 10.2 us: small_body(): h2b = hop(h0b, perm=twos)]
    pallas_call x0 -> x9, Pallas kernels: none -> 19.2 us  [the longest x1 8.09 us: fetch(): pl.pallas_call(functools.partial(fetch_kernel, pieces=pieces), in_specs=[...]
    ppermute x0 -> x13, starting transfers between devices: none -> 15.9 us  [the longest x3 4.28 us: small_body(): hop(wide[step], perm=[(i, (i + step) % owners) for i in range(owners)])]
    psum x1 -> x0, blocking collectives: 11.4 us -> none  [body(): low_rank = lax.psum(low_part, ('tensor', 'seq')).astype(jnp.bfloat16)]
    all_to_all x1 -> x0, blocking collectives: 10.7 us -> none  [body(): lax.all_to_all(delta_rows, 'adapter', split_axis=2, concat_axis=1, tiled=...]
  transfers between devices with their start and end apart: 3 -> 13, of which waited for: 1 -> 7; matrix products, arithmetic and copies ran while one was open for 48% -> 1% of each run, Pallas kernels for 0% -> 25%
where the time goes in v2:
time: 60 us; the launch traced here: 59.9 us
  waiting for transfers between devices  20.5 us (34%)
  Pallas kernels  19.2 us (32%)
  starting transfers between devices  15.9 us (26%)
  local copies, waits for them, and re-layouts  4.05 us (7%)
    ppermute x1, waiting for transfers between devices, small_body(): h2b = hop(h0b, perm=twos)  10.2 us
    pallas_call x1, Pallas kernels, fetch(): pl.pallas_call(functools.partial(fetch_kernel, pieces=pieces), in_specs=[...  8.09 us
    pallas_call x1, Pallas kernels, first_half(): pl.pallas_call(functools.partial(first_kernel, cuts=cuts), in_specs=[SMEM...  5.19 us
    ppermute x3, starting transfers between devices, small_body(): hop(wide[step], perm=[(i, (i + step) % owners) for i in range(owners)])  4.28 us
    ppermute x1, starting transfers between devices, small_body(): h2a = hop(h0a, perm=twos)  4.1 us
    ppermute x3, waiting for transfers between devices, small_body(): hop(wide[step], perm=[(i, (i + step) % owners) for i in range(owners)])  3.25 us
    ppermute x1, waiting for transfers between devices, small_body(): h3b = hop(h2b, perm=pairs)  2.7 us
    pallas_call x1, Pallas kernels, second_base(): pl.pallas_call(base_kernel, in_specs=[SMEM] + [VMEM] * 6, out_specs=[VMEM...  2.64 us
  transfers between devices with their start and end apart: 13, of which 7 were waited for; matrix products, arithmetic and copies ran while one was open for 1% of the time, Pallas kernels for 25%

profile of v2, /device:TPU:0, one launch (start us, length us, event | category | flops | bytes accessed | tf_op | source)
XLA Modules:
  0.0 59.9 jit_solution(10683033075558533821)
XLA Ops:
  0.0 1.1 %fusion = (bf16[32,3584]{1,0:T(8,128)(2,1)S(1)}, bf16[32,3584]{1,0:T(8,128)(2,1)S(1)}) fusion(bf16[32,7168]{1,0:T(8,128)(2,1)} %param.6), kind=kLoop, calls=%fused_computation.3 | loop fusion | bytes 917504 | tf_op jit(solution)/shard_map/slice | solution.py:328
  1.1 4.1 %collective-permute-start.1 = (bf16[32,3584]{1,0:T(8,128)(2,1)S(1)}, bf16[32,3584]{1,0:T(8,128)(2,1)S(1)}, u32[]{:S(2)}, u32[]{:S(2)}) collective-permute-start(bf16[32,3584]{1,0:T(8,128)(2,1)S(1)} %get-tuple-element.86.b0), channel_id=1, source_target_pairs={{0,8},{8,0},{4,12},{12,4},{1,9},{9,1},{5,13},{13,5},{2,10},{10,2},... | collective-permute-start | bytes 688136 | tf_op jit(solution)/shard_map/ppermute | solution.py:329
  5.2 1.6 %collective-permute-start = (bf16[32,3584]{1,0:T(8,128)(2,1)S(1)}, bf16[32,3584]{1,0:T(8,128)(2,1)S(1)}, u32[]{:S(2)}, u32[]{:S(2)}) collective-permute-start(bf16[32,3584]{1,0:T(8,128)(2,1)S(1)} %get-tuple-element.86.b0), channel_id=1, source_target_pairs={{0,4},{4,0},{8,12},{12,8},{1,5},{5,1},{9,13},{13,9},{2,6},{6,2},{1... | collective-permute-start | bytes 688136 | tf_op jit(solution)/shard_map/ppermute | solution.py:330
  6.8 0.7 %dynamic-slice_bitcast_fusion = (s32[32,1]{0,1:T(1,128)S(1)}, s32[1,32]{1,0:T(1,128)S(1)}) fusion(s32[128]{0:T(128)} %param.10, s32[]{:T(128)S(6)} %select_n.3), kind=kLoop, calls=%fused_computation.1 | loop fusion | bytes 388 | tf_op jit(solution)/shard_map/broadcast_in_dim | solution.py:252
  7.5 0.1 copy.7.column_ref
  7.6 0.7 %copy-done.1 = s32[8]{0:T(128)S(1)} copy-done((s32[8]{0:T(128)S(1)}, s32[8]{0:T(128)}, u32[]{:S(2)}) %copy-start.1) | copy-done | bytes 56
  8.2 0.8 %plan.1 = (bf16[2,16,32]{2,1,0:T(8,128)(2,1)S(1)}, bf16[32,64]{1,0:T(8,128)(2,1)S(1)}) custom-call(s32[1]{0:T(128)} %bitcast.2.scalars, s32[8]{0:T(128)S(1)} %copy-done.1, s32[1,32]{1,0:T(1,128)S(1)} %get-tuple-element.88.row_ref, s32[32,1]{1,0:T(8,128)S(1)} %copy.7.column_ref), custom_call_target="tpu_custom_call" | custom-call | bytes 1048576 | tf_op jit(solution)/shard_map/plan/pallas_call | solution.py:241
  9.0 0.1 pad_add_fusion.picks
  9.1 1.5 %copy-done = bf16[2,7168,64]{1,2,0:T(8,128)(2,1)S(1)} copy-done((bf16[2,7168,64]{1,2,0:T(8,128)(2,1)S(1)}, bf16[2,7168,64]{1,2,0:T(8,128)(2,1)}, u32[]{:S(2)}) %copy-start) | copy-done | bytes 1835032
  10.6 8.1 %fetch.1 = (bf16[1792,2048]{1,0:T(8,128)(2,1)S(1)}, bf16[3584,2048]{1,0:T(8,128)(2,1)S(1)}, bf16[128,7168]{1,0:T(8,128)(2,1)S(1)}, bf16[128,8192]{1,0:T(8,128)(2,1)S(1)}) custom-call(bf16[7168,2048]{1,0:T(8,128)(2,1)} %w_far, bf16[7168,2048]{1,0:T(8,128)(2,1)} %w_far, bf16[128,7168]{1,0:T(8,128)(2,1)S(1)} %bitcast.11, bf16[128,8192]{1,0:T(8,128)(2,1)} %bitcast.12), custom_call_target="tpu_custom_call" | custom-call | bytes 25952256 | tf_op jit(solution)/shard_map/fetch/pallas_call | solution.py:57
  18.7 0.4 collective-permute-start.3
  19.1 0.7 %collective-permute-start.5 = (bf16[32,3584]{1,0:T(8,128)(2,1)S(1)}, bf16[32,3584]{1,0:T(8,128)(2,1)S(1)}, u32[]{:S(2)}, u32[]{:S(2)}) collective-permute-start(bf16[32,3584]{1,0:T(8,128)(2,1)S(1)} %collective-permute-done.1.b2), channel_id=1, source_target_pairs={{0,4},{4,0},{8,12},{12,8},{1,5},{5,1},{9,13},{13,9},{2,6},{6,2},{1... | collective-permute-start | bytes 688136 | tf_op jit(solution)/shard_map/ppermute | solution.py:339
  19.8 1.3 %collective-permute-start.2 = (bf16[32,3584]{1,0:T(8,128)(2,1)S(1)}, bf16[32,3584]{1,0:T(8,128)(2,1)S(1)}, u32[]{:S(2)}, u32[]{:S(2)}) collective-permute-start(bf16[32,3584]{1,0:T(8,128)(2,1)S(1)} %get-tuple-element.65.b0), channel_id=1, source_target_pairs={{0,4},{4,0},{8,12},{12,8},{1,5},{5,1},{9,13},{13,9},{2,6},{6,2},{1... | collective-permute-start | bytes 688136 | tf_op jit(solution)/shard_map/ppermute | solution.py:341
  21.1 10.2 %collective-permute-done.3.b2 = bf16[32,3584]{1,0:T(8,128)(2,1)S(1)} collective-permute-done((bf16[32,3584]{1,0:T(8,128)(2,1)S(1)}, bf16[32,3584]{1,0:T(8,128)(2,1)S(1)}, u32[]{:S(2)}, u32[]{:S(2)}) %collective-permute-start.3) | collective-permute-done | bytes 229408 | tf_op jit(solution)/shard_map/ppermute | solution.py:340
  31.4 1.1 %collective-permute-done.5.b3 = bf16[32,3584]{1,0:T(8,128)(2,1)S(1)} collective-permute-done((bf16[32,3584]{1,0:T(8,128)(2,1)S(1)}, bf16[32,3584]{1,0:T(8,128)(2,1)S(1)}, u32[]{:S(2)}, u32[]{:S(2)}) %collective-permute-start.5) | collective-permute-done | bytes 229408 | tf_op jit(solution)/shard_map/ppermute | solution.py:339
  32.5 5.2 %first_half.1 = (f32[128,2048]{1,0:T(8,128)S(1)}, f32[128,128]{1,0:T(8,128)S(1)}) custom-call(s32[2]{0:T(128)S(1)} %pad_add_fusion.picks, bf16[32,3584]{1,0:T(8,128)(2,1)S(1)} %get-tuple-element.86.b0, bf16[32,3584]{1,0:T(8,128)(2,1)S(1)} %collective-permute-done.b1, bf16[32,3584]{1,0:T(8,128)(2,1)S(1)} %collective-permute-done.1.b2, ...), custom_call_target="tpu_custom_call" | custom-call | flops 1996488704 | bytes 4194304 | tf_op jit(solution)/shard_map/first_half/pallas_call | solution.py:118
  37.7 2.7 %collective-permute-done.4.b3 = bf16[32,3584]{1,0:T(8,128)(2,1)S(1)} collective-permute-done((bf16[32,3584]{1,0:T(8,128)(2,1)S(1)}, bf16[32,3584]{1,0:T(8,128)(2,1)S(1)}, u32[]{:S(2)}, u32[]{:S(2)}) %collective-permute-start.4) | collective-permute-done | bytes 229408 | tf_op jit(solution)/shard_map/ppermute | solution.py:342
  40.4 1.0 %second_low.1 = (f32[64,128]{1,0:T(8,128)S(1)}, f32[64,128]{1,0:T(8,128)S(1)}) custom-call(s32[2]{0:T(128)S(1)} %pad_add_fusion.picks, bf16[32,3584]{1,0:T(8,128)(2,1)S(1)} %get-tuple-element.65.b0, bf16[32,3584]{1,0:T(8,128)(2,1)S(1)} %collective-permute-done.2.b1, bf16[32,3584]{1,0:T(8,128)(2,1)S(1)} %collective-permute-done.3.b2, ...), custom_call_target="tpu_custom_call" | custom-call | flops 117440512 | bytes 1048576 | tf_op jit(solution)/shard_map/second_low/pallas_call | solution.py:145
  41.4 2.6 %second_base.1 = (f32[64,2048]{1,0:T(8,128)S(1)}, bf16[64,2048]{1,0:T(8,128)(2,1)S(1)}) custom-call(s32[2]{0:T(128)S(1)} %pad_add_fusion.picks, bf16[32,3584]{1,0:T(8,128)(2,1)S(1)} %get-tuple-element.65.b0, bf16[32,3584]{1,0:T(8,128)(2,1)S(1)} %collective-permute-done.2.b1, bf16[32,3584]{1,0:T(8,128)(2,1)S(1)} %collective-permute-done.3.b2, ...), custom_call_target="tpu_custom_call" | custom-call | flops 1879048192 | bytes 4194304 | tf_op jit(solution)/shard_map/second_base/pallas_call | solution.py:171
  44.0 0.1 collective-permute-start.6
  44.1 0.5 collective-permute-start.7
  44.6 1.1 %collective-permute-done.7.came = f32[64,128]{1,0:T(8,128)S(1)} collective-permute-done((f32[64,128]{1,0:T(8,128)S(1)}, f32[64,128]{1,0:T(8,128)S(1)}, u32[]{:S(2)}, u32[]{:S(2)}) %collective-permute-start.7) | collective-permute-done | bytes 32800 | tf_op jit(solution)/shard_map/ppermute | solution.py:349
  45.7 1.5 %collective-permute-start.8 = (f32[32,128]{1,0:T(8,128)S(1)}, f32[32,128]{1,0:T(8,128)S(1)}, u32[]{:S(2)}, u32[]{:S(2)}) collective-permute-start(f32[32,128]{1,0:T(8,128)S(1)} %get-tuple-element.74), channel_id=1, source_target_pairs={{0,2},{2,0},{1,3},{3,1},{4,6},{6,4},{5,7},{7,5},{8,10},{10,8},{9,1... | collective-permute-start | bytes 49160 | tf_op jit(solution)/shard_map/ppermute | solution.py:353
  47.2 2.2 %collective-permute-done.8.low_b = f32[32,128]{1,0:T(8,128)S(1)} collective-permute-done((f32[32,128]{1,0:T(8,128)S(1)}, f32[32,128]{1,0:T(8,128)S(1)}, u32[]{:S(2)}, u32[]{:S(2)}) %collective-permute-start.8) | collective-permute-done | bytes 16416 | tf_op jit(solution)/shard_map/ppermute | solution.py:353
  49.4 1.5 %collective-permute-start.9 = (bf16[32,2048]{1,0:T(8,128)(2,1)S(1)}, bf16[32,2048]{1,0:T(8,128)(2,1)S(1)}, u32[]{:S(2)}, u32[]{:S(2)}) collective-permute-start(bf16[32,2048]{1,0:T(8,128)(2,1)S(1)} %get-tuple-element.75), channel_id=1, source_target_pairs={{0,2},{2,0},{1,3},{3,1},{4,6},{6,4},{5,7},{7,5},{8,10},{10,8},{9,1... | collective-permute-start | bytes 393224 | tf_op jit(solution)/shard_map/ppermute | solution.py:356
  50.9 0.6 %widen.1 = (bf16[16,2048]{1,0:T(8,128)(2,1)S(1)}, bf16[16,2048]{1,0:T(8,128)(2,1)S(1)}, bf16[16,2048]{1,0:T(8,128)(2,1)S(1)}, bf16[16,2048]{1,0:T(8,128)(2,1)S(1)}) custom-call(s32[1]{0:T(128)} %bitcast.2.scalars, f32[32,128]{1,0:T(8,128)S(1)} %get-tuple-element.77.low_a, f32[32,128]{1,0:T(8,128)S(1)} %collective-permute-done.8.low_b, ...), custom_call_target="tpu_custom_call" | custom-call | bytes 1048576 | tf_op jit(solution)/shard_map/widen/pallas_call | solution.py:273
  51.5 0.4 collective-permute-start.10
  51.9 2.6 %collective-permute-start.11 = (bf16[16,2048]{1,0:T(8,128)(2,1)S(1)}, bf16[16,2048]{1,0:T(8,128)(2,1)S(1)}, u32[]{:S(2)}, u32[]{:S(2)}) collective-permute-start(bf16[16,2048]{1,0:T(8,128)(2,1)S(1)} %get-tuple-element.83), channel_id=1, source_target_pairs={{0,8},{4,12},{8,0},{12,4},{1,9},{5,13},{9,1},{13,5},{2,10},{6,14},... | collective-permute-start | bytes 196616 | tf_op jit(solution)/shard_map/ppermute | solution.py:360
  54.4 1.4 %collective-permute-start.12 = (bf16[16,2048]{1,0:T(8,128)(2,1)S(1)}, bf16[16,2048]{1,0:T(8,128)(2,1)S(1)}, u32[]{:S(2)}, u32[]{:S(2)}) collective-permute-start(bf16[16,2048]{1,0:T(8,128)(2,1)S(1)} %get-tuple-element.84), channel_id=1, source_target_pairs={{0,12},{4,0},{8,4},{12,8},{1,13},{5,1},{9,5},{13,9},{2,14},{6,2},{... | collective-permute-start | bytes 196616 | tf_op jit(solution)/shard_map/ppermute | solution.py:360
  55.8 1.9 %collective-permute-done.10.d1 = bf16[16,2048]{1,0:T(8,128)(2,1)S(1)} collective-permute-done((bf16[16,2048]{1,0:T(8,128)(2,1)S(1)}, bf16[16,2048]{1,0:T(8,128)(2,1)S(1)}, u32[]{:S(2)}, u32[]{:S(2)}) %collective-permute-start.10) | collective-permute-done | bytes 65568 | tf_op jit(solution)/shard_map/ppermute | solution.py:360
  57.7 1.3 %collective-permute-done.11.d2 = bf16[16,2048]{1,0:T(8,128)(2,1)S(1)} collective-permute-done((bf16[16,2048]{1,0:T(8,128)(2,1)S(1)}, bf16[16,2048]{1,0:T(8,128)(2,1)S(1)}, u32[]{:S(2)}, u32[]{:S(2)}) %collective-permute-start.11) | collective-permute-done | bytes 65568 | tf_op jit(solution)/shard_map/ppermute | solution.py:360
  59.0 0.8 %last.1 = bf16[32,2048]{1,0:T(8,128)(2,1)} custom-call(f32[32,2048]{1,0:T(8,128)S(1)} %get-tuple-element.70.keep, bf16[32,2048]{1,0:T(8,128)(2,1)S(1)} %collective-permute-done.9.came, bf16[32,64]{1,0:T(8,128)(2,1)S(1)} %get-tuple-element.76.back, bf16[16,2048]{1,0:T(8,128)(2,1)S(1)} %get-tuple-element.81.d0, ...), custom_call_target="tpu_custom_call" | custom-call | bytes 1048576 | tf_op jit(solution)/shard_map/last/pallas_call | solution.py:291
  (11 shorter events, 0.1 us)
Async XLA Ops:
  1.1 17.6 %collective-permute-start.1 = (bf16[32,3584]{1,0:T(8,128)(2,1)S(1)}, bf16[32,3584]{1,0:T(8,128)(2,1)S(1)}, u32[]{:S(2)}, u32[]{:S(2)}) collective-permute-start(bf16[32,3584]{1,0:T(8,128)(2,1)S(1)} %get-tuple-element.86.b0), channel_id=1, source_target_pairs={{0,8},{8,0},{4,12},{12,4},{1,9},{9,1},{5,13},{13,5},{2,10},{10,2},... | collective-permute-start | bytes 688136 | tf_op jit(solution)/shard_map/ppermute | solution.py:329
  5.2 13.5 %collective-permute-start = (bf16[32,3584]{1,0:T(8,128)(2,1)S(1)}, bf16[32,3584]{1,0:T(8,128)(2,1)S(1)}, u32[]{:S(2)}, u32[]{:S(2)}) collective-permute-start(bf16[32,3584]{1,0:T(8,128)(2,1)S(1)} %get-tuple-element.86.b0), channel_id=1, source_target_pairs={{0,4},{4,0},{8,12},{12,8},{1,5},{5,1},{9,13},{13,9},{2,6},{6,2},{1... | collective-permute-start | bytes 688136 | tf_op jit(solution)/shard_map/ppermute | solution.py:330
  7.6 0.7 %copy-start.1 = (s32[8]{0:T(128)S(1)}, s32[8]{0:T(128)}, u32[]{:S(2)}) copy-start(s32[8]{0:T(128)} %storage.1) | copy-start | bytes 100
  9.1 1.5 %copy-start = (bf16[2,7168,64]{1,2,0:T(8,128)(2,1)S(1)}, bf16[2,7168,64]{1,2,0:T(8,128)(2,1)}, u32[]{:S(2)}) copy-start(bf16[2,7168,64]{1,2,0:T(8,128)(2,1)} %param.8) | copy-start | bytes 5505028
  18.7 12.7 %collective-permute-start.3 = (bf16[32,3584]{1,0:T(8,128)(2,1)S(1)}, bf16[32,3584]{1,0:T(8,128)(2,1)S(1)}, u32[]{:S(2)}, u32[]{:S(2)}) collective-permute-start(bf16[32,3584]{1,0:T(8,128)(2,1)S(1)} %get-tuple-element.65.b0), channel_id=1, source_target_pairs={{0,8},{8,0},{4,12},{12,4},{1,9},{9,1},{5,13},{13,5},{2,10},{10,2},... | collective-permute-start | bytes 688136 | tf_op jit(solution)/shard_map/ppermute | solution.py:340
  19.1 13.4 %collective-permute-start.5 = (bf16[32,3584]{1,0:T(8,128)(2,1)S(1)}, bf16[32,3584]{1,0:T(8,128)(2,1)S(1)}, u32[]{:S(2)}, u32[]{:S(2)}) collective-permute-start(bf16[32,3584]{1,0:T(8,128)(2,1)S(1)} %collective-permute-done.1.b2), channel_id=1, source_target_pairs={{0,4},{4,0},{8,12},{12,8},{1,5},{5,1},{9,13},{13,9},{2,6},{6,2},{1... | collective-permute-start | bytes 688136 | tf_op jit(solution)/shard_map/ppermute | solution.py:339
  19.8 17.9 %collective-permute-start.2 = (bf16[32,3584]{1,0:T(8,128)(2,1)S(1)}, bf16[32,3584]{1,0:T(8,128)(2,1)S(1)}, u32[]{:S(2)}, u32[]{:S(2)}) collective-permute-start(bf16[32,3584]{1,0:T(8,128)(2,1)S(1)} %get-tuple-element.65.b0), channel_id=1, source_target_pairs={{0,4},{4,0},{8,12},{12,8},{1,5},{5,1},{9,13},{13,9},{2,6},{6,2},{1... | collective-permute-start | bytes 688136 | tf_op jit(solution)/shard_map/ppermute | solution.py:341
  31.4 9.0 %collective-permute-start.4 = (bf16[32,3584]{1,0:T(8,128)(2,1)S(1)}, bf16[32,3584]{1,0:T(8,128)(2,1)S(1)}, u32[]{:S(2)}, u32[]{:S(2)}) collective-permute-start(bf16[32,3584]{1,0:T(8,128)(2,1)S(1)} %collective-permute-done.3.b2), channel_id=1, source_target_pairs={{0,4},{4,0},{8,12},{12,8},{1,5},{5,1},{9,13},{13,9},{2,6},{6,2},{1... | collective-permute-start | bytes 688136 | tf_op jit(solution)/shard_map/ppermute | solution.py:342
  44.0 3.2 %collective-permute-start.6 = (bf16[64,2048]{1,0:T(8,128)(2,1)S(1)}, bf16[64,2048]{1,0:T(8,128)(2,1)S(1)}, u32[]{:S(2)}, u32[]{:S(2)}) collective-permute-start(bf16[64,2048]{1,0:T(8,128)(2,1)S(1)} %get-tuple-element.69), channel_id=1, source_target_pairs={{0,1},{1,0},{2,3},{3,2},{4,5},{5,4},{6,7},{7,6},{8,9},{9,8},{10,11... | collective-permute-start | bytes 786440 | tf_op jit(solution)/shard_map/ppermute | solution.py:351
  44.1 1.6 %collective-permute-start.7 = (f32[64,128]{1,0:T(8,128)S(1)}, f32[64,128]{1,0:T(8,128)S(1)}, u32[]{:S(2)}, u32[]{:S(2)}) collective-permute-start(f32[64,128]{1,0:T(8,128)S(1)} %get-tuple-element.73), channel_id=1, source_target_pairs={{0,1},{1,0},{2,3},{3,2},{4,5},{5,4},{6,7},{7,6},{8,9},{9,8},{10,11... | collective-permute-start | bytes 98312 | tf_op jit(solution)/shard_map/ppermute | solution.py:349
  45.7 3.7 %collective-permute-start.8 = (f32[32,128]{1,0:T(8,128)S(1)}, f32[32,128]{1,0:T(8,128)S(1)}, u32[]{:S(2)}, u32[]{:S(2)}) collective-permute-start(f32[32,128]{1,0:T(8,128)S(1)} %get-tuple-element.74), channel_id=1, source_target_pairs={{0,2},{2,0},{1,3},{3,1},{4,6},{6,4},{5,7},{7,5},{8,10},{10,8},{9,1... | collective-permute-start | bytes 49160 | tf_op jit(solution)/shard_map/ppermute | solution.py:353
  49.4 9.6 %collective-permute-start.9 = (bf16[32,2048]{1,0:T(8,128)(2,1)S(1)}, bf16[32,2048]{1,0:T(8,128)(2,1)S(1)}, u32[]{:S(2)}, u32[]{:S(2)}) collective-permute-start(bf16[32,2048]{1,0:T(8,128)(2,1)S(1)} %get-tuple-element.75), channel_id=1, source_target_pairs={{0,2},{2,0},{1,3},{3,1},{4,6},{6,4},{5,7},{7,5},{8,10},{10,8},{9,1... | collective-permute-start | bytes 393224 | tf_op jit(solution)/shard_map/ppermute | solution.py:356
  51.5 6.2 %collective-permute-start.10 = (bf16[16,2048]{1,0:T(8,128)(2,1)S(1)}, bf16[16,2048]{1,0:T(8,128)(2,1)S(1)}, u32[]{:S(2)}, u32[]{:S(2)}) collective-permute-start(bf16[16,2048]{1,0:T(8,128)(2,1)S(1)} %get-tuple-element.82), channel_id=1, source_target_pairs={{0,4},{4,8},{8,12},{12,0},{1,5},{5,9},{9,13},{13,1},{2,6},{6,10},{... | collective-permute-start | bytes 196616 | tf_op jit(solution)/shard_map/ppermute | solution.py:360
  51.9 7.2 %collective-permute-start.11 = (bf16[16,2048]{1,0:T(8,128)(2,1)S(1)}, bf16[16,2048]{1,0:T(8,128)(2,1)S(1)}, u32[]{:S(2)}, u32[]{:S(2)}) collective-permute-start(bf16[16,2048]{1,0:T(8,128)(2,1)S(1)} %get-tuple-element.83), channel_id=1, source_target_pairs={{0,8},{4,12},{8,0},{12,4},{1,9},{5,13},{9,1},{13,5},{2,10},{6,14},... | collective-permute-start | bytes 196616 | tf_op jit(solution)/shard_map/ppermute | solution.py:360
  54.4 4.6 %collective-permute-start.12 = (bf16[16,2048]{1,0:T(8,128)(2,1)S(1)}, bf16[16,2048]{1,0:T(8,128)(2,1)S(1)}, u32[]{:S(2)}, u32[]{:S(2)}) collective-permute-start(bf16[16,2048]{1,0:T(8,128)(2,1)S(1)} %get-tuple-element.84), channel_id=1, source_target_pairs={{0,12},{4,0},{8,4},{12,8},{1,13},{5,1},{9,5},{13,9},{2,14},{6,2},{... | collective-permute-start | bytes 196616 | tf_op jit(solution)/shard_map/ppermute | solution.py:360

commit v3 on v2

--- a/solution.py
+++ b/solution.py
@@ -70,9 +70,13 @@
     return lax.dot_general(a, b, (((1,), (1,)), ((), ())), preferred_element_type=F32)
 
 
-def ordered(picks, blocks):
-    near, far = picks[0] == 1, picks[1] == 1
-    b0, b1, b2, b3 = [block[...] for block in blocks]
+def ordered(blocks, skip):
+    own = lax.axis_index("adapter")
+    near = (lax.axis_index("seq") ^ (own & 1)) == 1
+    far = (lax.axis_index("tensor") ^ (own >> 1)) == 1
+    depth = blocks[2].shape[1]
+    b0, b1 = [block[:, skip : skip + depth] for block in blocks[:2]]
+    b2, b3 = [block[...] for block in blocks[2:]]
     k0, k2 = jnp.where(near, b1, b0), jnp.where(near, b3, b2)
     s0, s2 = jnp.where(near, b0, b1), jnp.where(near, b2, b3)
     return jnp.concatenate(
@@ -87,7 +91,7 @@
 
 
 def first_kernel(
-    picks, b0, b1, b2, b3, w_far, w_ref, a_ref, base_ref, low_ref, streamed, sems, *, cuts
+    b0, b1, b2, b3, w_far, w_ref, a_ref, base_ref, low_ref, streamed, sems, *, cuts
 ):
     cut = streamed.shape[0]
     step = cut // cuts
@@ -96,7 +100,7 @@
         rows = pl.ds(index * step, step)
         copies.append(pltpu.make_async_copy(w_far.at[rows], streamed.at[rows], sems.at[index]))
         copies[-1].start()
-    h = ordered(picks, (b0, b1, b2, b3))
+    h = ordered((b0, b1, b2, b3), 0)
     depth = h.shape[1]
     low_ref[...] = dot_nt(h, a_ref[:, :depth])
     for start in range(0, w_ref.shape[1], COLUMNS):
@@ -111,13 +115,13 @@
         )
 
 
-def first_half(picks, blocks, w_far, w, a, cut):
-    rows, extent = blocks[0].shape
+def first_half(blocks, w_far, w, a, cut):
+    rows, extent = blocks[2].shape
     width, low = w.shape[1], a.shape[0]
     cuts = 4
     return pl.pallas_call(
         functools.partial(first_kernel, cuts=cuts),
-        in_specs=[SMEM] + [VMEM] * 4 + [HBM] + [VMEM] * 2,
+        in_specs=[VMEM] * 4 + [HBM] + [VMEM] * 2,
         out_specs=[VMEM] * 2,
         out_shape=[
             jax.ShapeDtypeStruct((4 * rows, width), F32),
@@ -127,50 +131,49 @@
         compiler_params=params(20),
         cost_estimate=cost(8 * rows * extent * (width + low), 4 * MIB),
         name="first_half",
-    )(picks, *blocks, w_far, w, a)
-
-
-def low_kernel(picks, b0, b1, b2, b3, a_ref, low_in, keep_ref, send_ref):
-    h = ordered(picks, (b0, b1, b2, b3))
-    skip = a_ref.shape[1] - h.shape[1]
+    )(*blocks, w_far, w, a)
+
+
+def low_kernel(b0, b1, b2, b3, a_ref, low_in, keep_ref, send_ref):
+    skip = a_ref.shape[1] - b2.shape[1]
+    h = ordered((b0, b1, b2, b3), skip)
     total = low_in[...] + dot_nt(h, a_ref[:, skip:])
     rows = keep_ref.shape[0]
     keep_ref[...] = total[:rows]
     send_ref[...] = total[rows:]
 
 
-def second_low(picks, blocks, a, low_in):
-    rows, extent = blocks[0].shape
+def second_low(blocks, a, low_in):
+    rows, extent = blocks[2].shape
     low = a.shape[0]
     return pl.pallas_call(
         low_kernel,
-        in_specs=[SMEM] + [VMEM] * 6,
+        in_specs=[VMEM] * 6,
         out_specs=[VMEM] * 2,
         out_shape=[jax.ShapeDtypeStruct((2 * rows, low), F32)] * 2,
         compiler_params=params(8),
         cost_estimate=cost(8 * rows * extent * low, MIB),
         name="second_low",
-    )(picks, *blocks, a, low_in)
-
-
-def base_kernel(picks, b0, b1, b2, b3, w_ref, base_in, keep_ref, send_ref):
-    h = ordered(picks, (b0, b1, b2, b3))
+    )(*blocks, a, low_in)
+
+
+def base_kernel(b0, b1, b2, b3, w_ref, base_in, keep_ref, send_ref):
+    h = ordered((b0, b1, b2, b3), b0.shape[1] - b2.shape[1])
     rows = keep_ref.shape[0]
-    skip = w_ref.shape[0] - h.shape[1]
     for start in range(0, w_ref.shape[1], COLUMNS):
         columns = slice(start, start + COLUMNS)
-        part = jnp.dot(h, w_ref[skip:, columns], preferred_element_type=F32)
+        part = jnp.dot(h, w_ref[:, columns], preferred_element_type=F32)
         total = base_in[:, columns] + part
         keep_ref[:, columns] = total[:rows]
         send_ref[:, columns] = total[rows:].astype(BF16)
 
 
-def second_base(picks, blocks, w, base_in):
-    rows, extent = blocks[0].shape
+def second_base(blocks, w, base_in):
+    rows, extent = blocks[2].shape
     width = w.shape[1]
     return pl.pallas_call(
         base_kernel,
-        in_specs=[SMEM] + [VMEM] * 6,
+        in_specs=[VMEM] * 6,
         out_specs=[VMEM] * 2,
         out_shape=[
             jax.ShapeDtypeStruct((2 * rows, width), F32),
@@ -179,7 +182,7 @@
         compiler_params=params(12),
         cost_estimate=cost(8 * rows * extent * width, 4 * MIB),
         name="second_base",
-    )(picks, *blocks, w, base_in)
+    )(*blocks, w, base_in)
 
 
 def split_kernel(keep_in, came, keep_ref, send_ref):
@@ -202,9 +205,14 @@
     )(keep, came)
 
 
-def plan_kernel(scalars, storage, row_ref, column_ref, into_ref, back_ref, *, stored, slots):
-    own = scalars[0]
-    rows = row_ref.shape[1]
+def plan_kernel(storage, index_ref, into_ref, back_ref, *, stored, slots):
+    own = lax.axis_index("adapter")
+    part = lax.axis_index("tensor") * 2 + lax.axis_index("seq")
+    rows = back_ref.shape[0]
+    shape = (rows, index_ref.shape[1])
+    spot = lax.broadcasted_iota(jnp.int32, shape, 0) + part * rows
+    chosen = lax.broadcasted_iota(jnp.int32, shape, 1) == spot
+    index = jnp.sum(jnp.where(chosen, index_ref[...], 0), axis=1, keepdims=True)
 
     def position(index):
         found = jnp.zeros_like(index)
@@ -218,11 +226,16 @@
             owner += (place >= step * stored).astype(jnp.int32)
         return owner
 
-    place_row, place_column = position(row_ref[...]), position(column_ref[...])
-    owner_row, owner_column = owner_of(place_row), owner_of(place_column)
-    local_row = place_row - owner_row * stored
     down = lax.broadcasted_iota(jnp.int32, (rows, rows), 0)
     across = lax.broadcasted_iota(jnp.int32, (rows, rows), 1)
+
+    def turned(column):
+        return jnp.sum(jnp.where(down == across, column, 0), axis=0, keepdims=True)
+
+    place_column = position(index)
+    owner_column = owner_of(place_column)
+    owner_row = turned(owner_column)
+    local_row = turned(place_column - owner_column * stored)
     same = owner_column == owner_row
     rank_row = jnp.sum((same & (down < across)).astype(jnp.int32), axis=0, keepdims=True)
     rank_column = jnp.sum((same & (across < down)).astype(jnp.int32), axis=1, keepdims=True)
@@ -236,11 +249,10 @@
     back_ref[...] = jnp.where(lane == hops * slots + rank_column, 1.0, 0.0).astype(BF16)
 
 
-def plan(scalars, storage, mine, stored, slots):
-    rows = mine.shape[0]
+def plan(storage, index, rows, stored, slots):
     return pl.pallas_call(
         functools.partial(plan_kernel, stored=stored, slots=slots),
-        in_specs=[SMEM, SMEM, VMEM, VMEM],
+        in_specs=[SMEM, VMEM],
         out_specs=[VMEM] * 2,
         out_shape=[
             jax.ShapeDtypeStruct((stored, slots, rows), BF16),
@@ -249,10 +261,10 @@
         compiler_params=params(2),
         cost_estimate=cost(0, MIB),
         name="plan",
-    )(scalars, storage, mine[None, :], mine[:, None])
-
-
-def widen_kernel(scalars, low_a, low_b, into_ref, b_ref, *outs):
+    )(storage, index[None, :])
+
+
+def widen_kernel(low_a, low_b, into_ref, b_ref, *outs):
     low = (low_a[...] + low_b[...]).astype(BF16)
     stored = into_ref.shape[0]
     rank_extent = low.shape[1] // stored
@@ -263,22 +275,22 @@
     packed = jnp.concatenate(terms, axis=1)
     width = outs[0].shape[1]
     for step, out in enumerate(outs):
-        start = pl.multiple_of(lax.rem(scalars[0] + step, len(outs)) * width, width)
+        start = pl.multiple_of(lax.rem(lax.axis_index("adapter") + step, len(outs)) * width, width)
         columns = b_ref[:, pl.ds(start, width)]
         out[...] = jnp.dot(packed, columns, preferred_element_type=F32).astype(BF16)
 
 
-def widen(scalars, low_a, low_b, into, b, slots, owners):
+def widen(low_a, low_b, into, b, slots, owners):
     width = b.shape[1] // owners
     return pl.pallas_call(
         widen_kernel,
-        in_specs=[SMEM] + [VMEM] * 4,
+        in_specs=[VMEM] * 4,
         out_specs=[VMEM] * owners,
         out_shape=[jax.ShapeDtypeStruct((slots, width), BF16)] * owners,
         compiler_params=params(6),
         cost_estimate=cost(0, MIB),
         name="widen",
-    )(scalars, low_a, low_b, into, b)
+    )(low_a, low_b, into, b)
 
 
 def last_kernel(keep, came, back, d0, d1, d2, d3, out_ref):
@@ -306,59 +318,53 @@
     rows, extent = hidden.shape
     stored, _, rank_extent = adapter_first_factors.shape
     slots = max(2, min(rows // 2, 2 * rows // owners))
-    own = lax.axis_index("adapter")
-    far = lax.axis_index("tensor")
-    near = lax.axis_index("seq")
-    part = far * 2 + near
     half = 256 * (extent * SHARE // (256 * 16))
     cut = half // 2
     rest = extent - half
 
     a = jnp.swapaxes(adapter_first_factors, 1, 2).reshape(stored * rank_extent, extent)
     b = adapter_second_factors.reshape(stored * rank_extent, -1)
-    picks = jnp.stack([near ^ (own & 1), far ^ (own >> 1)]).astype(jnp.int32)
-    scalars = jnp.reshape(own, (1,)).astype(jnp.int32)
-
     pairs = [(0, 1), (1, 0), (2, 3), (3, 2)]
     twos = [(0, 2), (2, 0), (1, 3), (3, 1)]
     both = [(0, 1), (1, 0)]
     hop = functools.partial(lax.ppermute, axis_name="adapter")
 
-    mine = lax.dynamic_slice_in_dim(adapter_index_rows, part * rows, rows, 0)
+    barrier = lax.optimization_barrier
+    h0 = hidden
+    h1 = hop(h0, perm=pairs)
     h0a, h0b = hidden[:, :half], hidden[:, half:]
     h2a = hop(h0a, perm=twos)
-    h1a = hop(h0a, perm=pairs)
-    into, back = plan(scalars, storage, mine, stored, slots)
-    picks, into, back, down_matrix = lax.optimization_barrier((picks, into, back, down_matrix))
-    w_a, w_b, a, b = fetch(
-        (down_matrix, down_matrix, a, b),
-        ((0, cut, half - cut, 4), (0, half, rest, 7), (1, 0, extent, 1), (1, 0, b.shape[1], 1)),
-        "fetch",
-    )
-    h1a, h2a, h0b, w_a, w_b, a, b = lax.optimization_barrier((h1a, h2a, h0b, w_a, w_b, a, b))
+    (w_b,) = fetch((down_matrix,), ((0, half, rest, 7),), "fetch_b")
+    w_b, h0b, a, b = barrier((w_b, h0b, a, b))
+    h2b = hop(h0b, perm=twos)
+    w_a, a, b = fetch(
+        (down_matrix, a, b),
+        ((0, cut, half - cut, 4), (1, 0, extent, 1), (1, 0, b.shape[1], 1)),
+        "fetch_a",
+    )
+    h2a, w_a, a, b, adapter_index_rows = barrier((h2a, w_a, a, b, adapter_index_rows))
     h3a = hop(h2a, perm=pairs)
-    h2b = hop(h0b, perm=twos)
-    h1b = hop(h0b, perm=pairs)
+    into, back = plan(storage, adapter_index_rows, rows, stored, slots)
+    h2b, into, back = barrier((h2b, into, back))
     h3b = hop(h2b, perm=pairs)
 
-    base_a, low_a = first_half(picks, (h0a, h1a, h2a, h3a), down_matrix, w_a, a, cut)
-    h1b, h3b, base_a, low_a = lax.optimization_barrier((h1b, h3b, base_a, low_a))
-    blocks_b = (h0b, h1b, h2b, h3b)
-    low_keep, low_send = second_low(picks, blocks_b, a, low_a)
-    low_keep, low_send, h0b = lax.optimization_barrier((low_keep, low_send, h0b))
+    base_a, low_a = first_half((h0, h1, h2a, h3a), down_matrix, w_a, a, cut)
+    h3b, base_a, low_a = barrier((h3b, base_a, low_a))
+    blocks_b = (h0, h1, h2b, h3b)
+    low_keep, low_send = second_low(blocks_b, a, low_a)
     low_came = lax.ppermute(low_send, "seq", both)
-    base_keep, base_send = second_base(picks, (h0b, h1b, h2b, h3b), w_b, base_a)
-    base_came = lax.ppermute(base_send, "seq", both)
     low_keep, low_send = split_sum(low_keep, low_came, "split_low")
     low_came = lax.ppermute(low_send, "tensor", both)
-    base_keep, base_send = split_sum(base_keep, base_came, "split_base")
-    base_send, low_came = lax.optimization_barrier((base_send, low_came))
-    base_came = lax.ppermute(base_send, "tensor", both)
-    wide = widen(scalars, low_keep, low_came, into, b, slots, owners)
+    w_b, low_keep = barrier((w_b, low_keep))
+    base_keep, base_send = second_base(blocks_b, w_b, base_a)
+    base_send, low_came = barrier((base_send, low_came))
+    base_came = lax.ppermute(base_send, "seq", both)
+    wide = widen(low_keep, low_came, into, b, slots, owners)
     deltas = [wide[0]]
     for step in range(1, owners):
         deltas.append(hop(wide[step], perm=[(i, (i + step) % owners) for i in range(owners)]))
-
+    base_keep, base_send = split_sum(base_keep, base_came, "split_base")
+    base_came = lax.ppermute(base_send, "tensor", both)
     return last(base_keep, base_came, back, deltas)
 
 

time: 60 us -> 56.7 us (0.945)
  local copies, waits for them, and re-layouts: 4.05 us -> 1.11 us
  waiting for transfers between devices: 20.5 us -> 22.5 us
  Pallas kernels: 19.2 us -> 17.9 us
  starting transfers between devices: 15.9 us -> 15 us
    ppermute x1, waiting for transfers between devices: 1.1 us -> 4.11 us  [small_body(): h3a = hop(h2a, perm=pairs)]
    ppermute x3, waiting for transfers between devices: 3.25 us -> 6.06 us  [small_body(): hop(wide[step], perm=[(i, (i + step) % owners) for i in range(owners)])]
    ppermute x1, waiting for transfers between devices: 2.7 us -> 0.01 us  [small_body(): h3b = hop(h2b, perm=pairs)]
    ppermute x1, starting transfers between devices: 0.01 us -> 2.32 us  [small_body(): h3b = hop(h2b, perm=pairs)]
    unnamed x4 -> x10, local copies, waits for them, and re-layouts: 2.16 us -> 0.03 us
    ppermute x1, waiting for transfers between devices: 2.18 us -> 0.11 us  [small_body(): low_came = lax.ppermute(low_send, 'tensor', both)]
    pallas_call x4, Pallas kernels: 9.4 us -> 7.76 us  [the longest x1 4.65 us: first_half(): pl.pallas_call(functools.partial(first_kernel, cuts=cuts), in_specs=[VMEM...]
    ppermute x1, waiting for transfers between devices: 10.2 us -> 8.66 us  [small_body(): h2b = hop(h0b, perm=twos)]
  transfers between devices with their start and end apart: 13 -> 12, of which waited for: 7 -> 8; matrix products, arithmetic and copies ran while one was open for 1% -> 0% of each run, Pallas kernels for 25% -> 29%
where the time goes in v3:
time: 56.7 us; the launch traced here: 56.6 us
  waiting for transfers between devices  22.5 us (40%)
  Pallas kernels  17.9 us (32%)
  starting transfers between devices  15 us (26%)
  local copies, waits for them, and re-layouts  1.11 us (2%)
    ppermute x1, waiting for transfers between devices, small_body(): h2b = hop(h0b, perm=twos)  8.66 us
    pallas_call x2, Pallas kernels, fetch(): pl.pallas_call(functools.partial(fetch_kernel, pieces=pieces), in_specs=[...  8.52 us
    ppermute x3, waiting for transfers between devices, small_body(): hop(wide[step], perm=[(i, (i + step) % owners) for i in range(owners)])  6.06 us
    pallas_call x1, Pallas kernels, first_half(): pl.pallas_call(functools.partial(first_kernel, cuts=cuts), in_specs=[VMEM...  4.65 us
    ppermute x1, waiting for transfers between devices, small_body(): h3a = hop(h2a, perm=pairs)  4.11 us
    ppermute x1, starting transfers between devices, small_body(): h2a = hop(h0a, perm=twos)  4.1 us
    ppermute x3, starting transfers between devices, small_body(): hop(wide[step], perm=[(i, (i + step) % owners) for i in range(owners)])  3.3 us
    ppermute x1, starting transfers between devices, small_body(): h3b = hop(h2b, perm=pairs)  2.32 us
  transfers between devices with their start and end apart: 12, of which 8 were waited for; matrix products, arithmetic and copies ran while one was open for 0% of the time, Pallas kernels for 29%

profile of v3, /device:TPU:0, one launch (start us, length us, event | category | flops | bytes accessed | tf_op | source)
XLA Modules:
  0.0 56.6 jit_solution(14751639106426741157)
XLA Ops:
  0.0 1.1 %fusion = (bf16[32,3584]{1,0:T(8,128)(2,1)S(1)}, bf16[32,3584]{1,0:T(8,128)(2,1)S(1)}) fusion(bf16[32,7168]{1,0:T(8,128)(2,1)} %b0.5), kind=kLoop, calls=%fused_computation | loop fusion | bytes 917504 | tf_op jit(solution)/shard_map/slice | solution.py:335
  1.1 0.0 copy-start.1
  1.1 0.0 copy-start.2
  1.1 4.1 %collective-permute-start.2 = (bf16[32,3584]{1,0:T(8,128)(2,1)S(1)}, bf16[32,3584]{1,0:T(8,128)(2,1)S(1)}, u32[]{:S(2)}, u32[]{:S(2)}) collective-permute-start(bf16[32,3584]{1,0:T(8,128)(2,1)S(1)} %get-tuple-element.81), channel_id=1, source_target_pairs={{0,8},{8,0},{4,12},{12,4},{1,9},{9,1},{5,13},{13,5},{2,10},{10,2},... | collective-permute-start | bytes 688136 | tf_op jit(solution)/shard_map/ppermute | solution.py:336
  5.2 1.6 %collective-permute-start = (bf16[32,7168]{1,0:T(8,128)(2,1)}, bf16[32,7168]{1,0:T(8,128)(2,1)S(1)}, u32[]{:S(2)}, u32[]{:S(2)}) collective-permute-start(bf16[32,7168]{1,0:T(8,128)(2,1)} %b0.5), channel_id=1, source_target_pairs={{0,4},{4,0},{8,12},{12,8},{1,5},{5,1},{9,13},{13,9},{2,6},{6,2},{1... | collective-permute-start | bytes 1376264 | tf_op jit(solution)/shard_map/ppermute | solution.py:334
  6.8 5.3 %fetch_b.1.w_ref = bf16[3584,2048]{1,0:T(8,128)(2,1)S(1)} custom-call(bf16[7168,2048]{1,0:T(8,128)(2,1)} %w_far.1), custom_call_target="tpu_custom_call" | custom-call | bytes 14680064 | tf_op jit(solution)/shard_map/fetch_b/pallas_call | solution.py:57
  12.1 0.0 copy-start.3
  12.1 0.0 copy-start.4
  12.1 0.0 copy-start
  12.1 0.4 collective-permute-start.1
  12.6 3.2 %fetch_a.1 = (bf16[1792,2048]{1,0:T(8,128)(2,1)S(1)}, bf16[128,7168]{1,0:T(8,128)(2,1)S(1)}, bf16[128,8192]{1,0:T(8,128)(2,1)S(1)}) custom-call(bf16[7168,2048]{1,0:T(8,128)(2,1)} %w_far.1, bf16[128,7168]{1,0:T(8,128)(2,1)S(1)} %bitcast.6, bf16[128,8192]{1,0:T(8,128)(2,1)S(1)} %bitcast.5), custom_call_target="tpu_custom_call" | custom-call | bytes 11272192 | tf_op jit(solution)/shard_map/fetch_a/pallas_call | solution.py:57
  15.8 0.8 %collective-permute-done.2.b2 = bf16[32,3584]{1,0:T(8,128)(2,1)S(1)} collective-permute-done((bf16[32,3584]{1,0:T(8,128)(2,1)S(1)}, bf16[32,3584]{1,0:T(8,128)(2,1)S(1)}, u32[]{:S(2)}, u32[]{:S(2)}) %collective-permute-start.2) | collective-permute-done | bytes 229408 | tf_op jit(solution)/shard_map/ppermute | solution.py:336
  16.6 0.0 collective-permute-start.4
  16.6 0.7 %plan.1 = (bf16[2,16,32]{2,1,0:T(8,128)(2,1)S(1)}, bf16[32,64]{1,0:T(8,128)(2,1)S(1)}) custom-call(s32[8]{0:T(128)S(1)} %copy-done.3, s32[1,128]{1,0:T(1,128)S(1)} %bitcast.7), custom_call_target="tpu_custom_call" | custom-call | bytes 1048576 | tf_op jit(solution)/shard_map/plan/pallas_call | solution.py:253
  17.3 8.7 %collective-permute-done.1.b2 = bf16[32,3584]{1,0:T(8,128)(2,1)S(1)} collective-permute-done((bf16[32,3584]{1,0:T(8,128)(2,1)S(1)}, bf16[32,3584]{1,0:T(8,128)(2,1)S(1)}, u32[]{:S(2)}, u32[]{:S(2)}) %collective-permute-start.1) | collective-permute-done | bytes 229408 | tf_op jit(solution)/shard_map/ppermute | solution.py:339
  26.0 2.3 %collective-permute-start.3 = (bf16[32,3584]{1,0:T(8,128)(2,1)S(1)}, bf16[32,3584]{1,0:T(8,128)(2,1)S(1)}, u32[]{:S(2)}, u32[]{:S(2)}) collective-permute-start(bf16[32,3584]{1,0:T(8,128)(2,1)S(1)} %collective-permute-done.1.b2), channel_id=1, source_target_pairs={{0,4},{4,0},{8,12},{12,8},{1,5},{5,1},{9,13},{13,9},{2,6},{6,2},{1... | collective-permute-start | bytes 688136 | tf_op jit(solution)/shard_map/ppermute | solution.py:349
  28.3 4.1 %collective-permute-done.4.b3 = bf16[32,3584]{1,0:T(8,128)(2,1)S(1)} collective-permute-done((bf16[32,3584]{1,0:T(8,128)(2,1)S(1)}, bf16[32,3584]{1,0:T(8,128)(2,1)S(1)}, u32[]{:S(2)}, u32[]{:S(2)}) %collective-permute-start.4) | collective-permute-done | bytes 229408 | tf_op jit(solution)/shard_map/ppermute | solution.py:346
  32.5 4.7 %first_half.1 = (f32[128,2048]{1,0:T(8,128)S(1)}, f32[128,128]{1,0:T(8,128)S(1)}) custom-call(bf16[32,7168]{1,0:T(8,128)(2,1)S(1)} %copy-done, bf16[32,7168]{1,0:T(8,128)(2,1)S(1)} %collective-permute-done.b1, bf16[32,3584]{1,0:T(8,128)(2,1)S(1)} %collective-permute-done.2.b2, bf16[32,3584]{1,0:T(8,128)(2,1)S(1)} %collective-permute-done.4.b3, ...), custom_call_target="tpu_custom_call" | custom-call | flops 1996488704 | bytes 4194304 | tf_op jit(solution)/shard_map/first_half/pallas_call | solution.py:122
  37.1 0.4 second_low.1
  37.6 0.1 collective-permute-start.5
  37.6 1.2 %collective-permute-done.5.came = f32[64,128]{1,0:T(8,128)S(1)} collective-permute-done((f32[64,128]{1,0:T(8,128)S(1)}, f32[64,128]{1,0:T(8,128)S(1)}, u32[]{:S(2)}, u32[]{:S(2)}) %collective-permute-start.5) | collective-permute-done | bytes 32800 | tf_op jit(solution)/shard_map/ppermute | solution.py:355
  38.8 1.6 %collective-permute-start.6 = (f32[32,128]{1,0:T(8,128)S(1)}, f32[32,128]{1,0:T(8,128)S(1)}, u32[]{:S(2)}, u32[]{:S(2)}) collective-permute-start(f32[32,128]{1,0:T(8,128)S(1)} %get-tuple-element.68), channel_id=1, source_target_pairs={{0,2},{2,0},{1,3},{3,1},{4,6},{6,4},{5,7},{7,5},{8,10},{10,8},{9,1... | collective-permute-start | bytes 49160 | tf_op jit(solution)/shard_map/ppermute | solution.py:357
  40.4 2.1 %second_base.1 = (f32[64,2048]{1,0:T(8,128)S(1)}, bf16[64,2048]{1,0:T(8,128)(2,1)S(1)}) custom-call(bf16[32,7168]{1,0:T(8,128)(2,1)S(1)} %copy-done, bf16[32,7168]{1,0:T(8,128)(2,1)S(1)} %collective-permute-done.b1, bf16[32,3584]{1,0:T(8,128)(2,1)S(1)} %collective-permute-done.1.b2, bf16[32,3584]{1,0:T(8,128)(2,1)S(1)} %collective-permute-done.3.b3, ...), custom_call_target="tpu_custom_call" | custom-call | flops 1879048192 | bytes 4194304 | tf_op jit(solution)/shard_map/second_base/pallas_call | solution.py:174
  42.5 0.1 collective-permute-done.6.low_b
  42.6 1.5 %collective-permute-done.7.came = bf16[64,2048]{1,0:T(8,128)(2,1)S(1)} collective-permute-done((bf16[64,2048]{1,0:T(8,128)(2,1)S(1)}, bf16[64,2048]{1,0:T(8,128)(2,1)S(1)}, u32[]{:S(2)}, u32[]{:S(2)}) %collective-permute-start.7) | collective-permute-done | bytes 262176 | tf_op jit(solution)/shard_map/ppermute | solution.py:361
  44.2 1.6 %collective-permute-start.8 = (bf16[32,2048]{1,0:T(8,128)(2,1)S(1)}, bf16[32,2048]{1,0:T(8,128)(2,1)S(1)}, u32[]{:S(2)}, u32[]{:S(2)}) collective-permute-start(bf16[32,2048]{1,0:T(8,128)(2,1)S(1)} %get-tuple-element.71), channel_id=1, source_target_pairs={{0,2},{2,0},{1,3},{3,1},{4,6},{6,4},{5,7},{7,5},{8,10},{10,8},{9,1... | collective-permute-start | bytes 393224 | tf_op jit(solution)/shard_map/ppermute | solution.py:367
  45.8 0.6 %widen.1 = (bf16[16,2048]{1,0:T(8,128)(2,1)S(1)}, bf16[16,2048]{1,0:T(8,128)(2,1)S(1)}, bf16[16,2048]{1,0:T(8,128)(2,1)S(1)}, bf16[16,2048]{1,0:T(8,128)(2,1)S(1)}) custom-call(f32[32,128]{1,0:T(8,128)S(1)} %get-tuple-element.73.low_a, f32[32,128]{1,0:T(8,128)S(1)} %collective-permute-done.6.low_b, bf16[2,16,32]{2,1,0:T(8,128)(2,1)S(1)} %get-tuple-element.75.into_ref, ...), custom_call_target="tpu_custom_call" | custom-call | bytes 1048576 | tf_op jit(solution)/shard_map/widen/pallas_call | solution.py:285
  46.4 0.8 %collective-permute-start.10 = (bf16[16,2048]{1,0:T(8,128)(2,1)S(1)}, bf16[16,2048]{1,0:T(8,128)(2,1)S(1)}, u32[]{:S(2)}, u32[]{:S(2)}) collective-permute-start(bf16[16,2048]{1,0:T(8,128)(2,1)S(1)} %get-tuple-element.79), channel_id=1, source_target_pairs={{0,8},{4,12},{8,0},{12,4},{1,9},{5,13},{9,1},{13,5},{2,10},{6,14},... | collective-permute-start | bytes 196616 | tf_op jit(solution)/shard_map/ppermute | solution.py:365
  47.2 2.5 %collective-permute-start.11 = (bf16[16,2048]{1,0:T(8,128)(2,1)S(1)}, bf16[16,2048]{1,0:T(8,128)(2,1)S(1)}, u32[]{:S(2)}, u32[]{:S(2)}) collective-permute-start(bf16[16,2048]{1,0:T(8,128)(2,1)S(1)} %get-tuple-element.80), channel_id=1, source_target_pairs={{0,12},{4,0},{8,4},{12,8},{1,13},{5,1},{9,5},{13,9},{2,14},{6,2},{... | collective-permute-start | bytes 196616 | tf_op jit(solution)/shard_map/ppermute | solution.py:365
  49.7 3.3 %collective-permute-done.10.d2 = bf16[16,2048]{1,0:T(8,128)(2,1)S(1)} collective-permute-done((bf16[16,2048]{1,0:T(8,128)(2,1)S(1)}, bf16[16,2048]{1,0:T(8,128)(2,1)S(1)}, u32[]{:S(2)}, u32[]{:S(2)}) %collective-permute-start.10) | collective-permute-done | bytes 65568 | tf_op jit(solution)/shard_map/ppermute | solution.py:365
  53.0 2.7 %collective-permute-done.9.d1 = bf16[16,2048]{1,0:T(8,128)(2,1)S(1)} collective-permute-done((bf16[16,2048]{1,0:T(8,128)(2,1)S(1)}, bf16[16,2048]{1,0:T(8,128)(2,1)S(1)}, u32[]{:S(2)}, u32[]{:S(2)}) %collective-permute-start.9) | collective-permute-done | bytes 65568 | tf_op jit(solution)/shard_map/ppermute | solution.py:365
  55.8 0.8 %last.1 = bf16[32,2048]{1,0:T(8,128)(2,1)} custom-call(f32[32,2048]{1,0:T(8,128)S(1)} %get-tuple-element.70.keep, bf16[32,2048]{1,0:T(8,128)(2,1)S(1)} %collective-permute-done.8.came, bf16[32,64]{1,0:T(8,128)(2,1)S(1)} %get-tuple-element.72.back, bf16[16,2048]{1,0:T(8,128)(2,1)S(1)} %get-tuple-element.77.d0, ...), custom_call_target="tpu_custom_call" | custom-call | bytes 1048576 | tf_op jit(solution)/shard_map/last/pallas_call | solution.py:303
  (13 shorter events, 0.1 us)
Async XLA Ops:
  1.1 11.5 %copy-start.1 = (bf16[2,64,8192]{2,1,0:T(8,128)(2,1)S(1)}, bf16[2,64,8192]{2,1,0:T(8,128)(2,1)}, u32[]{:S(2)}) copy-start(bf16[2,64,8192]{2,1,0:T(8,128)(2,1)} %param.9) | copy-start | bytes 6291460
  1.1 11.5 %copy-start.2 = (bf16[2,7168,64]{1,2,0:T(8,128)(2,1)S(1)}, bf16[2,7168,64]{1,2,0:T(8,128)(2,1)}, u32[]{:S(2)}) copy-start(bf16[2,7168,64]{1,2,0:T(8,128)(2,1)} %param.8) | copy-start | bytes 5505028
  1.1 15.5 %collective-permute-start.2 = (bf16[32,3584]{1,0:T(8,128)(2,1)S(1)}, bf16[32,3584]{1,0:T(8,128)(2,1)S(1)}, u32[]{:S(2)}, u32[]{:S(2)}) collective-permute-start(bf16[32,3584]{1,0:T(8,128)(2,1)S(1)} %get-tuple-element.81), channel_id=1, source_target_pairs={{0,8},{8,0},{4,12},{12,4},{1,9},{9,1},{5,13},{13,5},{2,10},{10,2},... | collective-permute-start | bytes 688136 | tf_op jit(solution)/shard_map/ppermute | solution.py:336
  5.2 27.2 %collective-permute-start = (bf16[32,7168]{1,0:T(8,128)(2,1)}, bf16[32,7168]{1,0:T(8,128)(2,1)S(1)}, u32[]{:S(2)}, u32[]{:S(2)}) collective-permute-start(bf16[32,7168]{1,0:T(8,128)(2,1)} %b0.5), channel_id=1, source_target_pairs={{0,4},{4,0},{8,12},{12,8},{1,5},{5,1},{9,13},{13,9},{2,6},{6,2},{1... | collective-permute-start | bytes 1376264 | tf_op jit(solution)/shard_map/ppermute | solution.py:334
  12.1 4.5 %copy-start.3 = (s32[8]{0:T(128)S(1)}, s32[8]{0:T(128)}, u32[]{:S(2)}) copy-start(s32[8]{0:T(128)} %storage.1) | copy-start | bytes 100
  12.1 4.5 %copy-start.4 = (s32[128]{0:T(128)S(1)}, s32[128]{0:T(128)}, u32[]{:S(2)}) copy-start(s32[128]{0:T(128)} %param.10) | copy-start | bytes 1540
  12.1 20.3 %copy-start = (bf16[32,7168]{1,0:T(8,128)(2,1)S(1)}, bf16[32,7168]{1,0:T(8,128)(2,1)}, u32[]{:S(2)}) copy-start(bf16[32,7168]{1,0:T(8,128)(2,1)} %b0.5) | copy-start | bytes 1376260
  12.1 13.9 %collective-permute-start.1 = (bf16[32,3584]{1,0:T(8,128)(2,1)S(1)}, bf16[32,3584]{1,0:T(8,128)(2,1)S(1)}, u32[]{:S(2)}, u32[]{:S(2)}) collective-permute-start(bf16[32,3584]{1,0:T(8,128)(2,1)S(1)} %get-tuple-element.43), channel_id=1, source_target_pairs={{0,8},{8,0},{4,12},{12,4},{1,9},{9,1},{5,13},{13,5},{2,10},{10,2},... | collective-permute-start | bytes 688136 | tf_op jit(solution)/shard_map/ppermute | solution.py:339
  16.6 15.9 %collective-permute-start.4 = (bf16[32,3584]{1,0:T(8,128)(2,1)S(1)}, bf16[32,3584]{1,0:T(8,128)(2,1)S(1)}, u32[]{:S(2)}, u32[]{:S(2)}) collective-permute-start(bf16[32,3584]{1,0:T(8,128)(2,1)S(1)} %collective-permute-done.2.b2), channel_id=1, source_target_pairs={{0,4},{4,0},{8,12},{12,8},{1,5},{5,1},{9,13},{13,9},{2,6},{6,2},{1... | collective-permute-start | bytes 688136 | tf_op jit(solution)/shard_map/ppermute | solution.py:346
  26.0 11.1 %collective-permute-start.3 = (bf16[32,3584]{1,0:T(8,128)(2,1)S(1)}, bf16[32,3584]{1,0:T(8,128)(2,1)S(1)}, u32[]{:S(2)}, u32[]{:S(2)}) collective-permute-start(bf16[32,3584]{1,0:T(8,128)(2,1)S(1)} %collective-permute-done.1.b2), channel_id=1, source_target_pairs={{0,4},{4,0},{8,12},{12,8},{1,5},{5,1},{9,13},{13,9},{2,6},{6,2},{1... | collective-permute-start | bytes 688136 | tf_op jit(solution)/shard_map/ppermute | solution.py:349
  37.6 1.3 %collective-permute-start.5 = (f32[64,128]{1,0:T(8,128)S(1)}, f32[64,128]{1,0:T(8,128)S(1)}, u32[]{:S(2)}, u32[]{:S(2)}) collective-permute-start(f32[64,128]{1,0:T(8,128)S(1)} %get-tuple-element.62), channel_id=1, source_target_pairs={{0,1},{1,0},{2,3},{3,2},{4,5},{5,4},{6,7},{7,6},{8,9},{9,8},{10,11... | collective-permute-start | bytes 98312 | tf_op jit(solution)/shard_map/ppermute | solution.py:355
  38.8 3.7 %collective-permute-start.6 = (f32[32,128]{1,0:T(8,128)S(1)}, f32[32,128]{1,0:T(8,128)S(1)}, u32[]{:S(2)}, u32[]{:S(2)}) collective-permute-start(f32[32,128]{1,0:T(8,128)S(1)} %get-tuple-element.68), channel_id=1, source_target_pairs={{0,2},{2,0},{1,3},{3,1},{4,6},{6,4},{5,7},{7,5},{8,10},{10,8},{9,1... | collective-permute-start | bytes 49160 | tf_op jit(solution)/shard_map/ppermute | solution.py:357
  42.6 1.5 %collective-permute-start.7 = (bf16[64,2048]{1,0:T(8,128)(2,1)S(1)}, bf16[64,2048]{1,0:T(8,128)(2,1)S(1)}, u32[]{:S(2)}, u32[]{:S(2)}) collective-permute-start(bf16[64,2048]{1,0:T(8,128)(2,1)S(1)} %get-tuple-element.69), channel_id=1, source_target_pairs={{0,1},{1,0},{2,3},{3,2},{4,5},{5,4},{6,7},{7,6},{8,9},{9,8},{10,11... | collective-permute-start | bytes 786440 | tf_op jit(solution)/shard_map/ppermute | solution.py:361
  44.2 11.6 %collective-permute-start.8 = (bf16[32,2048]{1,0:T(8,128)(2,1)S(1)}, bf16[32,2048]{1,0:T(8,128)(2,1)S(1)}, u32[]{:S(2)}, u32[]{:S(2)}) collective-permute-start(bf16[32,2048]{1,0:T(8,128)(2,1)S(1)} %get-tuple-element.71), channel_id=1, source_target_pairs={{0,2},{2,0},{1,3},{3,1},{4,6},{6,4},{5,7},{7,5},{8,10},{10,8},{9,1... | collective-permute-start | bytes 393224 | tf_op jit(solution)/shard_map/ppermute | solution.py:367
  46.4 6.6 %collective-permute-start.10 = (bf16[16,2048]{1,0:T(8,128)(2,1)S(1)}, bf16[16,2048]{1,0:T(8,128)(2,1)S(1)}, u32[]{:S(2)}, u32[]{:S(2)}) collective-permute-start(bf16[16,2048]{1,0:T(8,128)(2,1)S(1)} %get-tuple-element.79), channel_id=1, source_target_pairs={{0,8},{4,12},{8,0},{12,4},{1,9},{5,13},{9,1},{13,5},{2,10},{6,14},... | collective-permute-start | bytes 196616 | tf_op jit(solution)/shard_map/ppermute | solution.py:365
  47.2 5.9 %collective-permute-start.11 = (bf16[16,2048]{1,0:T(8,128)(2,1)S(1)}, bf16[16,2048]{1,0:T(8,128)(2,1)S(1)}, u32[]{:S(2)}, u32[]{:S(2)}) collective-permute-start(bf16[16,2048]{1,0:T(8,128)(2,1)S(1)} %get-tuple-element.80), channel_id=1, source_target_pairs={{0,12},{4,0},{8,4},{12,8},{1,13},{5,1},{9,5},{13,9},{2,14},{6,2},{... | collective-permute-start | bytes 196616 | tf_op jit(solution)/shard_map/ppermute | solution.py:365
  49.7 6.1 %collective-permute-start.9 = (bf16[16,2048]{1,0:T(8,128)(2,1)S(1)}, bf16[16,2048]{1,0:T(8,128)(2,1)S(1)}, u32[]{:S(2)}, u32[]{:S(2)}) collective-permute-start(bf16[16,2048]{1,0:T(8,128)(2,1)S(1)} %get-tuple-element.78), channel_id=1, source_target_pairs={{0,4},{4,8},{8,12},{12,0},{1,5},{5,9},{9,13},{13,1},{2,6},{6,10},{... | collective-permute-start | bytes 196616 | tf_op jit(solution)/shard_map/ppermute | solution.py:365

commit v4 on v3

--- a/solution.py
+++ b/solution.py
@@ -16,6 +16,8 @@
 COLUMNS = 512
 FETCH_MIB = 27
 SHARE = 8
+CUT = 14
+ADD_FLOPS = 8e9
 
 
 def params(limit):
@@ -293,22 +295,37 @@
     )(low_a, low_b, into, b)
 
 
-def last_kernel(keep, came, back, d0, d1, d2, d3, out_ref):
+def add_kernel(keep, back, d0, d1, d2, d3, out_ref):
     deltas = jnp.concatenate([d[...] for d in (d0, d1, d2, d3)], axis=0)
-    delta = jnp.dot(back[...], deltas, preferred_element_type=F32)
-    out_ref[...] = (keep[...] + came[...].astype(F32) + delta).astype(out_ref.dtype)
-
-
-def last(keep, came, back, deltas):
+    out_ref[...] = keep[...] + jnp.dot(back[...], deltas, preferred_element_type=F32)
+
+
+def add_rows(keep, back, deltas):
+    return pl.pallas_call(
+        add_kernel,
+        in_specs=[VMEM] * 6,
+        out_specs=VMEM,
+        out_shape=jax.ShapeDtypeStruct(keep.shape, F32),
+        compiler_params=params(4),
+        cost_estimate=cost(ADD_FLOPS, MIB),
+        name="add_rows",
+    )(keep, back, *deltas)
+
+
+def last_kernel(keep, came, out_ref):
+    out_ref[...] = (keep[...] + came[...].astype(F32)).astype(out_ref.dtype)
+
+
+def last(keep, came):
     return pl.pallas_call(
         last_kernel,
-        in_specs=[VMEM] * 7,
+        in_specs=[VMEM] * 2,
         out_specs=VMEM,
         out_shape=jax.ShapeDtypeStruct(keep.shape, BF16),
         compiler_params=params(4),
         cost_estimate=cost(0, MIB),
         name="last",
-    )(keep, came, back, *deltas)
+    )(keep, came)
 
 
 def small_body(
@@ -319,7 +336,7 @@
     stored, _, rank_extent = adapter_first_factors.shape
     slots = max(2, min(rows // 2, 2 * rows // owners))
     half = 256 * (extent * SHARE // (256 * 16))
-    cut = half // 2
+    cut = 128 * (extent * CUT // (128 * 56))
     rest = extent - half
 
     a = jnp.swapaxes(adapter_first_factors, 1, 2).reshape(stored * rank_extent, extent)
@@ -357,15 +374,16 @@
     low_came = lax.ppermute(low_send, "tensor", both)
     w_b, low_keep = barrier((w_b, low_keep))
     base_keep, base_send = second_base(blocks_b, w_b, base_a)
-    base_send, low_came = barrier((base_send, low_came))
+    base_keep, low_came = barrier((base_keep, low_came))
+    wide = widen(low_keep, low_came, into, b, slots, owners)
+    base_send, wide = barrier((base_send, wide))
     base_came = lax.ppermute(base_send, "seq", both)
-    wide = widen(low_keep, low_came, into, b, slots, owners)
     deltas = [wide[0]]
     for step in range(1, owners):
         deltas.append(hop(wide[step], perm=[(i, (i + step) % owners) for i in range(owners)]))
     base_keep, base_send = split_sum(base_keep, base_came, "split_base")
     base_came = lax.ppermute(base_send, "tensor", both)
-    return last(base_keep, base_came, back, deltas)
+    return last(add_rows(base_keep, back, deltas), base_came)
 
 
 def body(

time: 56.7 us -> 54.7 us (0.965)
  waiting for transfers between devices: 22.5 us -> 20.6 us
    ppermute x1, waiting for transfers between devices: 1.53 us -> 0.01 us  [small_body(): base_came = lax.ppermute(base_send, 'seq', both)]
  transfers between devices with their start and end apart: 12 -> 12, of which waited for: 8 -> 8; matrix products, arithmetic and copies ran while one was open for 0% -> 0% of each run, Pallas kernels for 29% -> 30%
where the time goes in v4:
time: 54.7 us; the launch traced here: 54.6 us
  waiting for transfers between devices  20.6 us (38%)
  Pallas kernels  17.9 us (33%)
  starting transfers between devices  14.8 us (27%)
  local copies, waits for them, and re-layouts  1.11 us (2%)
    ppermute x1, waiting for transfers between devices, small_body(): h2b = hop(h0b, perm=twos)  8.66 us
    pallas_call x2, Pallas kernels, fetch(): pl.pallas_call(functools.partial(fetch_kernel, pieces=pieces), in_specs=[...  8.52 us
    ppermute x3, waiting for transfers between devices, small_body(): hop(wide[step], perm=[(i, (i + step) % owners) for i in range(owners)])  5.74 us
    pallas_call x1, Pallas kernels, first_half(): pl.pallas_call(functools.partial(first_kernel, cuts=cuts), in_specs=[VMEM...  4.65 us
    ppermute x1, waiting for transfers between devices, small_body(): h3a = hop(h2a, perm=pairs)  4.11 us
    ppermute x1, starting transfers between devices, small_body(): h2a = hop(h0a, perm=twos)  4.1 us
    ppermute x3, starting transfers between devices, small_body(): hop(wide[step], perm=[(i, (i + step) % owners) for i in range(owners)])  3.15 us
    ppermute x1, starting transfers between devices, small_body(): h3b = hop(h2b, perm=pairs)  2.32 us
  transfers between devices with their start and end apart: 12, of which 8 were waited for; matrix products, arithmetic and copies ran while one was open for 0% of the time, Pallas kernels for 30%

profile of v4, /device:TPU:0, one launch (start us, length us, event | category | flops | bytes accessed | tf_op | source)
XLA Modules:
  0.0 54.6 jit_solution(17978761116452794380)
XLA Ops:
  0.0 1.1 %fusion = (bf16[32,3584]{1,0:T(8,128)(2,1)S(1)}, bf16[32,3584]{1,0:T(8,128)(2,1)S(1)}) fusion(bf16[32,7168]{1,0:T(8,128)(2,1)} %b0.5), kind=kLoop, calls=%fused_computation | loop fusion | bytes 917504 | tf_op jit(solution)/shard_map/slice | solution.py:352
  1.1 0.0 copy-start.1
  1.1 0.0 copy-start.2
  1.1 4.1 %collective-permute-start.2 = (bf16[32,3584]{1,0:T(8,128)(2,1)S(1)}, bf16[32,3584]{1,0:T(8,128)(2,1)S(1)}, u32[]{:S(2)}, u32[]{:S(2)}) collective-permute-start(bf16[32,3584]{1,0:T(8,128)(2,1)S(1)} %get-tuple-element.91), channel_id=1, source_target_pairs={{0,8},{8,0},{4,12},{12,4},{1,9},{9,1},{5,13},{13,5},{2,10},{10,2},... | collective-permute-start | bytes 688136 | tf_op jit(solution)/shard_map/ppermute | solution.py:353
  5.2 1.6 %collective-permute-start = (bf16[32,7168]{1,0:T(8,128)(2,1)}, bf16[32,7168]{1,0:T(8,128)(2,1)S(1)}, u32[]{:S(2)}, u32[]{:S(2)}) collective-permute-start(bf16[32,7168]{1,0:T(8,128)(2,1)} %b0.5), channel_id=1, source_target_pairs={{0,4},{4,0},{8,12},{12,8},{1,5},{5,1},{9,13},{13,9},{2,6},{6,2},{1... | collective-permute-start | bytes 1376264 | tf_op jit(solution)/shard_map/ppermute | solution.py:351
  6.8 5.3 %fetch_b.1.w_ref = bf16[3584,2048]{1,0:T(8,128)(2,1)S(1)} custom-call(bf16[7168,2048]{1,0:T(8,128)(2,1)} %w_far.1), custom_call_target="tpu_custom_call" | custom-call | bytes 14680064 | tf_op jit(solution)/shard_map/fetch_b/pallas_call | solution.py:59
  12.1 0.0 copy-start
  12.1 0.4 collective-permute-start.1
  12.6 3.2 %fetch_a.1 = (bf16[1792,2048]{1,0:T(8,128)(2,1)S(1)}, bf16[128,7168]{1,0:T(8,128)(2,1)S(1)}, bf16[128,8192]{1,0:T(8,128)(2,1)S(1)}) custom-call(bf16[7168,2048]{1,0:T(8,128)(2,1)} %w_far.1, bf16[128,7168]{1,0:T(8,128)(2,1)S(1)} %bitcast.6, bf16[128,8192]{1,0:T(8,128)(2,1)S(1)} %bitcast.5), custom_call_target="tpu_custom_call" | custom-call | bytes 11272192 | tf_op jit(solution)/shard_map/fetch_a/pallas_call | solution.py:59
  15.8 0.8 %collective-permute-done.2.b2 = bf16[32,3584]{1,0:T(8,128)(2,1)S(1)} collective-permute-done((bf16[32,3584]{1,0:T(8,128)(2,1)S(1)}, bf16[32,3584]{1,0:T(8,128)(2,1)S(1)}, u32[]{:S(2)}, u32[]{:S(2)}) %collective-permute-start.2) | collective-permute-done | bytes 229408 | tf_op jit(solution)/shard_map/ppermute | solution.py:353
  16.6 0.0 collective-permute-start.4
  16.6 0.7 %plan.1 = (bf16[2,16,32]{2,1,0:T(8,128)(2,1)S(1)}, bf16[32,64]{1,0:T(8,128)(2,1)S(1)}) custom-call(s32[8]{0:T(128)S(1)} %copy-done.3, s32[1,128]{1,0:T(1,128)S(1)} %bitcast.7), custom_call_target="tpu_custom_call" | custom-call | bytes 1048576 | tf_op jit(solution)/shard_map/plan/pallas_call | solution.py:255
  17.3 8.7 %collective-permute-done.1.b2 = bf16[32,3584]{1,0:T(8,128)(2,1)S(1)} collective-permute-done((bf16[32,3584]{1,0:T(8,128)(2,1)S(1)}, bf16[32,3584]{1,0:T(8,128)(2,1)S(1)}, u32[]{:S(2)}, u32[]{:S(2)}) %collective-permute-start.1) | collective-permute-done | bytes 229408 | tf_op jit(solution)/shard_map/ppermute | solution.py:356
  26.0 2.3 %collective-permute-start.3 = (bf16[32,3584]{1,0:T(8,128)(2,1)S(1)}, bf16[32,3584]{1,0:T(8,128)(2,1)S(1)}, u32[]{:S(2)}, u32[]{:S(2)}) collective-permute-start(bf16[32,3584]{1,0:T(8,128)(2,1)S(1)} %collective-permute-done.1.b2), channel_id=1, source_target_pairs={{0,4},{4,0},{8,12},{12,8},{1,5},{5,1},{9,13},{13,9},{2,6},{6,2},{1... | collective-permute-start | bytes 688136 | tf_op jit(solution)/shard_map/ppermute | solution.py:366
  28.3 4.1 %collective-permute-done.4.b3 = bf16[32,3584]{1,0:T(8,128)(2,1)S(1)} collective-permute-done((bf16[32,3584]{1,0:T(8,128)(2,1)S(1)}, bf16[32,3584]{1,0:T(8,128)(2,1)S(1)}, u32[]{:S(2)}, u32[]{:S(2)}) %collective-permute-start.4) | collective-permute-done | bytes 229408 | tf_op jit(solution)/shard_map/ppermute | solution.py:363
  32.5 4.7 %first_half.1 = (f32[128,2048]{1,0:T(8,128)S(1)}, f32[128,128]{1,0:T(8,128)S(1)}) custom-call(bf16[32,7168]{1,0:T(8,128)(2,1)S(1)} %copy-done, bf16[32,7168]{1,0:T(8,128)(2,1)S(1)} %collective-permute-done.b1, bf16[32,3584]{1,0:T(8,128)(2,1)S(1)} %collective-permute-done.2.b2, bf16[32,3584]{1,0:T(8,128)(2,1)S(1)} %collective-permute-done.4.b3, ...), custom_call_target="tpu_custom_call" | custom-call | flops 1996488704 | bytes 4194304 | tf_op jit(solution)/shard_map/first_half/pallas_call | solution.py:124
  37.1 0.4 second_low.1
  37.6 0.1 collective-permute-start.5
  37.6 1.2 %collective-permute-done.5.came = f32[64,128]{1,0:T(8,128)S(1)} collective-permute-done((f32[64,128]{1,0:T(8,128)S(1)}, f32[64,128]{1,0:T(8,128)S(1)}, u32[]{:S(2)}, u32[]{:S(2)}) %collective-permute-start.5) | collective-permute-done | bytes 32800 | tf_op jit(solution)/shard_map/ppermute | solution.py:372
  38.8 1.6 %collective-permute-start.6 = (f32[32,128]{1,0:T(8,128)S(1)}, f32[32,128]{1,0:T(8,128)S(1)}, u32[]{:S(2)}, u32[]{:S(2)}) collective-permute-start(f32[32,128]{1,0:T(8,128)S(1)} %get-tuple-element.72), channel_id=1, source_target_pairs={{0,2},{2,0},{1,3},{3,1},{4,6},{6,4},{5,7},{7,5},{8,10},{10,8},{9,1... | collective-permute-start | bytes 49160 | tf_op jit(solution)/shard_map/ppermute | solution.py:374
  40.4 2.1 %second_base.1 = (f32[64,2048]{1,0:T(8,128)S(1)}, bf16[64,2048]{1,0:T(8,128)(2,1)S(1)}) custom-call(bf16[32,7168]{1,0:T(8,128)(2,1)S(1)} %copy-done, bf16[32,7168]{1,0:T(8,128)(2,1)S(1)} %collective-permute-done.b1, bf16[32,3584]{1,0:T(8,128)(2,1)S(1)} %collective-permute-done.1.b2, bf16[32,3584]{1,0:T(8,128)(2,1)S(1)} %collective-permute-done.3.b3, ...), custom_call_target="tpu_custom_call" | custom-call | flops 1879048192 | bytes 4194304 | tf_op jit(solution)/shard_map/second_base/pallas_call | solution.py:176
  42.5 0.1 collective-permute-done.6.low_b
  42.6 0.6 %widen.1 = (bf16[16,2048]{1,0:T(8,128)(2,1)S(1)}, bf16[16,2048]{1,0:T(8,128)(2,1)S(1)}, bf16[16,2048]{1,0:T(8,128)(2,1)S(1)}, bf16[16,2048]{1,0:T(8,128)(2,1)S(1)}) custom-call(f32[32,128]{1,0:T(8,128)S(1)} %get-tuple-element.75.low_a, f32[32,128]{1,0:T(8,128)S(1)} %collective-permute-done.6.low_b, bf16[2,16,32]{2,1,0:T(8,128)(2,1)S(1)} %get-tuple-element.77.into_ref, ...), custom_call_target="tpu_custom_call" | custom-call | bytes 1048576 | tf_op jit(solution)/shard_map/widen/pallas_call | solution.py:287
  43.2 0.1 collective-permute-start.7
  43.3 2.5 %collective-permute-start.10 = (bf16[16,2048]{1,0:T(8,128)(2,1)S(1)}, bf16[16,2048]{1,0:T(8,128)(2,1)S(1)}, u32[]{:S(2)}, u32[]{:S(2)}) collective-permute-start(bf16[16,2048]{1,0:T(8,128)(2,1)S(1)} %get-tuple-element.89), channel_id=1, source_target_pairs={{0,12},{4,0},{8,4},{12,8},{1,13},{5,1},{9,5},{13,9},{2,14},{6,2},{... | collective-permute-start | bytes 196616 | tf_op jit(solution)/shard_map/ppermute | solution.py:383
  45.8 0.6 %collective-permute-start.9 = (bf16[16,2048]{1,0:T(8,128)(2,1)S(1)}, bf16[16,2048]{1,0:T(8,128)(2,1)S(1)}, u32[]{:S(2)}, u32[]{:S(2)}) collective-permute-start(bf16[16,2048]{1,0:T(8,128)(2,1)S(1)} %get-tuple-element.88), channel_id=1, source_target_pairs={{0,8},{4,12},{8,0},{12,4},{1,9},{5,13},{9,1},{13,5},{2,10},{6,14},... | collective-permute-start | bytes 196616 | tf_op jit(solution)/shard_map/ppermute | solution.py:383
  46.5 1.5 %collective-permute-start.11 = (bf16[32,2048]{1,0:T(8,128)(2,1)S(1)}, bf16[32,2048]{1,0:T(8,128)(2,1)S(1)}, u32[]{:S(2)}, u32[]{:S(2)}) collective-permute-start(bf16[32,2048]{1,0:T(8,128)(2,1)S(1)} %get-tuple-element.90), channel_id=1, source_target_pairs={{0,2},{2,0},{1,3},{3,1},{4,6},{6,4},{5,7},{7,5},{8,10},{10,8},{9,1... | collective-permute-start | bytes 393224 | tf_op jit(solution)/shard_map/ppermute | solution.py:385
  48.0 0.2 collective-permute-done.10.d3
  48.2 4.3 %collective-permute-done.8.d1 = bf16[16,2048]{1,0:T(8,128)(2,1)S(1)} collective-permute-done((bf16[16,2048]{1,0:T(8,128)(2,1)S(1)}, bf16[16,2048]{1,0:T(8,128)(2,1)S(1)}, u32[]{:S(2)}, u32[]{:S(2)}) %collective-permute-start.8) | collective-permute-done | bytes 65568 | tf_op jit(solution)/shard_map/ppermute | solution.py:383
  52.5 1.2 %collective-permute-done.9.d2 = bf16[16,2048]{1,0:T(8,128)(2,1)S(1)} collective-permute-done((bf16[16,2048]{1,0:T(8,128)(2,1)S(1)}, bf16[16,2048]{1,0:T(8,128)(2,1)S(1)}, u32[]{:S(2)}, u32[]{:S(2)}) %collective-permute-start.9) | collective-permute-done | bytes 65568 | tf_op jit(solution)/shard_map/ppermute | solution.py:383
  53.7 0.2 add_rows.1.keep
  53.9 0.7 %last.1 = bf16[32,2048]{1,0:T(8,128)(2,1)} custom-call(f32[32,2048]{1,0:T(8,128)S(1)} %add_rows.1.keep, bf16[32,2048]{1,0:T(8,128)(2,1)S(1)} %collective-permute-done.11.came), custom_call_target="tpu_custom_call" | custom-call | bytes 1048576 | tf_op jit(solution)/shard_map/last/pallas_call | solution.py:320
  (14 shorter events, 0.1 us)
Async XLA Ops:
  1.1 11.5 %copy-start.1 = (bf16[2,64,8192]{2,1,0:T(8,128)(2,1)S(1)}, bf16[2,64,8192]{2,1,0:T(8,128)(2,1)}, u32[]{:S(2)}) copy-start(bf16[2,64,8192]{2,1,0:T(8,128)(2,1)} %param.9) | copy-start | bytes 6291460
  1.1 11.5 %copy-start.2 = (bf16[2,7168,64]{1,2,0:T(8,128)(2,1)S(1)}, bf16[2,7168,64]{1,2,0:T(8,128)(2,1)}, u32[]{:S(2)}) copy-start(bf16[2,7168,64]{1,2,0:T(8,128)(2,1)} %param.8) | copy-start | bytes 5505028
  1.1 15.5 %collective-permute-start.2 = (bf16[32,3584]{1,0:T(8,128)(2,1)S(1)}, bf16[32,3584]{1,0:T(8,128)(2,1)S(1)}, u32[]{:S(2)}, u32[]{:S(2)}) collective-permute-start(bf16[32,3584]{1,0:T(8,128)(2,1)S(1)} %get-tuple-element.91), channel_id=1, source_target_pairs={{0,8},{8,0},{4,12},{12,4},{1,9},{9,1},{5,13},{13,5},{2,10},{10,2},... | collective-permute-start | bytes 688136 | tf_op jit(solution)/shard_map/ppermute | solution.py:353
  5.2 27.2 %collective-permute-start = (bf16[32,7168]{1,0:T(8,128)(2,1)}, bf16[32,7168]{1,0:T(8,128)(2,1)S(1)}, u32[]{:S(2)}, u32[]{:S(2)}) collective-permute-start(bf16[32,7168]{1,0:T(8,128)(2,1)} %b0.5), channel_id=1, source_target_pairs={{0,4},{4,0},{8,12},{12,8},{1,5},{5,1},{9,13},{13,9},{2,6},{6,2},{1... | collective-permute-start | bytes 1376264 | tf_op jit(solution)/shard_map/ppermute | solution.py:351
  12.1 4.5 %copy-start.3 = (s32[8]{0:T(128)S(1)}, s32[8]{0:T(128)}, u32[]{:S(2)}) copy-start(s32[8]{0:T(128)} %storage.1) | copy-start | bytes 100
  12.1 4.5 %copy-start.4 = (s32[128]{0:T(128)S(1)}, s32[128]{0:T(128)}, u32[]{:S(2)}) copy-start(s32[128]{0:T(128)} %param.10) | copy-start | bytes 1540
  12.1 20.3 %copy-start = (bf16[32,7168]{1,0:T(8,128)(2,1)S(1)}, bf16[32,7168]{1,0:T(8,128)(2,1)}, u32[]{:S(2)}) copy-start(bf16[32,7168]{1,0:T(8,128)(2,1)} %b0.5) | copy-start | bytes 1376260
  12.1 13.9 %collective-permute-start.1 = (bf16[32,3584]{1,0:T(8,128)(2,1)S(1)}, bf16[32,3584]{1,0:T(8,128)(2,1)S(1)}, u32[]{:S(2)}, u32[]{:S(2)}) collective-permute-start(bf16[32,3584]{1,0:T(8,128)(2,1)S(1)} %get-tuple-element.48), channel_id=1, source_target_pairs={{0,8},{8,0},{4,12},{12,4},{1,9},{9,1},{5,13},{13,5},{2,10},{10,2},... | collective-permute-start | bytes 688136 | tf_op jit(solution)/shard_map/ppermute | solution.py:356
  16.6 15.9 %collective-permute-start.4 = (bf16[32,3584]{1,0:T(8,128)(2,1)S(1)}, bf16[32,3584]{1,0:T(8,128)(2,1)S(1)}, u32[]{:S(2)}, u32[]{:S(2)}) collective-permute-start(bf16[32,3584]{1,0:T(8,128)(2,1)S(1)} %collective-permute-done.2.b2), channel_id=1, source_target_pairs={{0,4},{4,0},{8,12},{12,8},{1,5},{5,1},{9,13},{13,9},{2,6},{6,2},{1... | collective-permute-start | bytes 688136 | tf_op jit(solution)/shard_map/ppermute | solution.py:363
  26.0 11.1 %collective-permute-start.3 = (bf16[32,3584]{1,0:T(8,128)(2,1)S(1)}, bf16[32,3584]{1,0:T(8,128)(2,1)S(1)}, u32[]{:S(2)}, u32[]{:S(2)}) collective-permute-start(bf16[32,3584]{1,0:T(8,128)(2,1)S(1)} %collective-permute-done.1.b2), channel_id=1, source_target_pairs={{0,4},{4,0},{8,12},{12,8},{1,5},{5,1},{9,13},{13,9},{2,6},{6,2},{1... | collective-permute-start | bytes 688136 | tf_op jit(solution)/shard_map/ppermute | solution.py:366
  37.6 1.3 %collective-permute-start.5 = (f32[64,128]{1,0:T(8,128)S(1)}, f32[64,128]{1,0:T(8,128)S(1)}, u32[]{:S(2)}, u32[]{:S(2)}) collective-permute-start(f32[64,128]{1,0:T(8,128)S(1)} %get-tuple-element.67), channel_id=1, source_target_pairs={{0,1},{1,0},{2,3},{3,2},{4,5},{5,4},{6,7},{7,6},{8,9},{9,8},{10,11... | collective-permute-start | bytes 98312 | tf_op jit(solution)/shard_map/ppermute | solution.py:372
  38.8 3.7 %collective-permute-start.6 = (f32[32,128]{1,0:T(8,128)S(1)}, f32[32,128]{1,0:T(8,128)S(1)}, u32[]{:S(2)}, u32[]{:S(2)}) collective-permute-start(f32[32,128]{1,0:T(8,128)S(1)} %get-tuple-element.72), channel_id=1, source_target_pairs={{0,2},{2,0},{1,3},{3,1},{4,6},{6,4},{5,7},{7,5},{8,10},{10,8},{9,1... | collective-permute-start | bytes 49160 | tf_op jit(solution)/shard_map/ppermute | solution.py:374
  43.2 3.2 %collective-permute-start.7 = (bf16[64,2048]{1,0:T(8,128)(2,1)S(1)}, bf16[64,2048]{1,0:T(8,128)(2,1)S(1)}, u32[]{:S(2)}, u32[]{:S(2)}) collective-permute-start(bf16[64,2048]{1,0:T(8,128)(2,1)S(1)} %get-tuple-element.83), channel_id=1, source_target_pairs={{0,1},{1,0},{2,3},{3,2},{4,5},{5,4},{6,7},{7,6},{8,9},{9,8},{10,11... | collective-permute-start | bytes 786440 | tf_op jit(solution)/shard_map/ppermute | solution.py:380
  43.3 4.9 %collective-permute-start.10 = (bf16[16,2048]{1,0:T(8,128)(2,1)S(1)}, bf16[16,2048]{1,0:T(8,128)(2,1)S(1)}, u32[]{:S(2)}, u32[]{:S(2)}) collective-permute-start(bf16[16,2048]{1,0:T(8,128)(2,1)S(1)} %get-tuple-element.89), channel_id=1, source_target_pairs={{0,12},{4,0},{8,4},{12,8},{1,13},{5,1},{9,5},{13,9},{2,14},{6,2},{... | collective-permute-start | bytes 196616 | tf_op jit(solution)/shard_map/ppermute | solution.py:383
  45.8 6.8 %collective-permute-start.8 = (bf16[16,2048]{1,0:T(8,128)(2,1)S(1)}, bf16[16,2048]{1,0:T(8,128)(2,1)S(1)}, u32[]{:S(2)}, u32[]{:S(2)}) collective-permute-start(bf16[16,2048]{1,0:T(8,128)(2,1)S(1)} %get-tuple-element.87), channel_id=1, source_target_pairs={{0,4},{4,8},{8,12},{12,0},{1,5},{5,9},{9,13},{13,1},{2,6},{6,10},{... | collective-permute-start | bytes 196616 | tf_op jit(solution)/shard_map/ppermute | solution.py:383
  45.8 8.0 %collective-permute-start.9 = (bf16[16,2048]{1,0:T(8,128)(2,1)S(1)}, bf16[16,2048]{1,0:T(8,128)(2,1)S(1)}, u32[]{:S(2)}, u32[]{:S(2)}) collective-permute-start(bf16[16,2048]{1,0:T(8,128)(2,1)S(1)} %get-tuple-element.88), channel_id=1, source_target_pairs={{0,8},{4,12},{8,0},{12,4},{1,9},{5,13},{9,1},{13,5},{2,10},{6,14},... | collective-permute-start | bytes 196616 | tf_op jit(solution)/shard_map/ppermute | solution.py:383
  46.5 7.4 %collective-permute-start.11 = (bf16[32,2048]{1,0:T(8,128)(2,1)S(1)}, bf16[32,2048]{1,0:T(8,128)(2,1)S(1)}, u32[]{:S(2)}, u32[]{:S(2)}) collective-permute-start(bf16[32,2048]{1,0:T(8,128)(2,1)S(1)} %get-tuple-element.90), channel_id=1, source_target_pairs={{0,2},{2,0},{1,3},{3,1},{4,6},{6,4},{5,7},{7,5},{8,10},{10,8},{9,1... | collective-permute-start | bytes 393224 | tf_op jit(solution)/shard_map/ppermute | solution.py:385

commit v5 on v4

--- a/solution.py
+++ b/solution.py
@@ -16,7 +16,9 @@
 COLUMNS = 512
 FETCH_MIB = 27
 SHARE = 8
-CUT = 14
+FETCH_A = 0.01
+FETCH_B = 1.0
+CUT = 7
 ADD_FLOPS = 8e9
 
 
@@ -48,7 +50,7 @@
         copy.wait()
 
 
-def fetch(arrays, pieces, name):
+def fetch(arrays, pieces, name, weight=1.0):
     shapes = []
     for array, (axis, _, length, _) in zip(arrays, pieces):
         shape = list(array.shape)
@@ -63,7 +65,7 @@
         out_shape=shapes,
         scratch_shapes=[pltpu.SemaphoreType.DMA((total,))],
         compiler_params=params(FETCH_MIB),
-        cost_estimate=cost(0, moved),
+        cost_estimate=cost(0, weight * moved),
         name=name,
     )(*arrays)
 
@@ -295,7 +297,7 @@
     )(low_a, low_b, into, b)
 
 
-def add_kernel(keep, back, d0, d1, d2, d3, out_ref):
+def add_kernel(keep, back, d0, d1, d3, d2, out_ref):
     deltas = jnp.concatenate([d[...] for d in (d0, d1, d2, d3)], axis=0)
     out_ref[...] = keep[...] + jnp.dot(back[...], deltas, preferred_element_type=F32)
 
@@ -309,7 +311,7 @@
         compiler_params=params(4),
         cost_estimate=cost(ADD_FLOPS, MIB),
         name="add_rows",
-    )(keep, back, *deltas)
+    )(keep, back, deltas[0], deltas[1], deltas[3], deltas[2])
 
 
 def last_kernel(keep, came, out_ref):
@@ -335,7 +337,7 @@
     rows, extent = hidden.shape
     stored, _, rank_extent = adapter_first_factors.shape
     slots = max(2, min(rows // 2, 2 * rows // owners))
-    half = 256 * (extent * SHARE // (256 * 16))
+    half = 128 * (extent * SHARE // (128 * 16))
     cut = 128 * (extent * CUT // (128 * 56))
     rest = extent - half
 
@@ -349,17 +351,19 @@
     barrier = lax.optimization_barrier
     h0 = hidden
     h1 = hop(h0, perm=pairs)
-    h0a, h0b = hidden[:, :half], hidden[:, half:]
+    h0a = hidden[:, :half]
     h2a = hop(h0a, perm=twos)
-    (w_b,) = fetch((down_matrix,), ((0, half, rest, 7),), "fetch_b")
-    w_b, h0b, a, b = barrier((w_b, h0b, a, b))
+    (w_b,) = fetch((down_matrix,), ((0, half, rest, 7),), "fetch_b", FETCH_B)
+    w_b, hidden, down_matrix = barrier((w_b, hidden, down_matrix))
+    (h0b,) = fetch((hidden,), ((1, half, rest, 1),), "half_b")
     h2b = hop(h0b, perm=twos)
-    w_a, a, b = fetch(
-        (down_matrix, a, b),
-        ((0, cut, half - cut, 4), (1, 0, extent, 1), (1, 0, b.shape[1], 1)),
+    (w_a,) = fetch(
+        (down_matrix,),
+        ((0, cut, half - cut, 4),),
         "fetch_a",
-    )
-    h2a, w_a, a, b, adapter_index_rows = barrier((h2a, w_a, a, b, adapter_index_rows))
+        FETCH_A,
+    )
+    h2a, w_a, adapter_index_rows = barrier((h2a, w_a, adapter_index_rows))
     h3a = hop(h2a, perm=pairs)
     into, back = plan(storage, adapter_index_rows, rows, stored, slots)
     h2b, into, back = barrier((h2b, into, back))
@@ -378,9 +382,10 @@
     wide = widen(low_keep, low_came, into, b, slots, owners)
     base_send, wide = barrier((base_send, wide))
     base_came = lax.ppermute(base_send, "seq", both)
-    deltas = [wide[0]]
-    for step in range(1, owners):
-        deltas.append(hop(wide[step], perm=[(i, (i + step) % owners) for i in range(owners)]))
+    deltas = {0: wide[0]}
+    for step in (1, 2, 3):
+        deltas[step] = hop(wide[step], perm=[(i, (i + step) % owners) for i in range(owners)])
+    deltas = [deltas[step] for step in range(owners)]
     base_keep, base_send = split_sum(base_keep, base_came, "split_base")
     base_came = lax.ppermute(base_send, "tensor", both)
     return last(add_rows(base_keep, back, deltas), base_came)

time: 54.7 us -> 52.9 us (0.967)
  waiting for transfers between devices: 20.6 us -> 16.8 us
  starting transfers between devices: 14.8 us -> 16.8 us
    ppermute x3, waiting for transfers between devices: 5.74 us -> 2.49 us  [small_body(): hop(wide[step], perm=[(i, (i + step) % owners) for i in range(owners)])]
    ppermute x3, starting transfers between devices: 3.15 us -> 4.95 us  [small_body(): hop(wide[step], perm=[(i, (i + step) % owners) for i in range(owners)])]
    pallas_call x2 -> x3, Pallas kernels: 8.52 us -> 9.78 us  [fetch(): pl.pallas_call(functools.partial(fetch_kernel, pieces=pieces), in_specs=[...]
    pallas_call x1, Pallas kernels: 4.65 us -> 3.5 us  [first_half(): pl.pallas_call(functools.partial(first_kernel, cuts=cuts), in_specs=[VMEM...]
    ppermute x1, waiting for transfers between devices: 0.01 us -> 0.86 us  [small_body(): base_came = lax.ppermute(base_send, 'tensor', both)]
    ppermute x1, waiting for transfers between devices: 0.79 us -> 0.01 us  [small_body(): h2a = hop(h0a, perm=twos)]
    ppermute x1, waiting for transfers between devices: 8.66 us -> 7.98 us  [small_body(): h2b = hop(h0b, perm=twos)]
  transfers between devices with their start and end apart: 12 -> 12, of which waited for: 8 -> 7; matrix products, arithmetic and copies ran while one was open for 0% -> 0% of each run, Pallas kernels for 30% -> 31%
where the time goes in v5:
time: 52.9 us; the launch traced here: 52.7 us
  Pallas kernels  18 us (34%)
  starting transfers between devices  16.8 us (32%)
  waiting for transfers between devices  16.8 us (32%)
  local copies, waits for them, and re-layouts  0.98 us (2%)
    pallas_call x3, Pallas kernels, fetch(): pl.pallas_call(functools.partial(fetch_kernel, pieces=pieces), in_specs=[...  9.78 us
    ppermute x1, waiting for transfers between devices, small_body(): h2b = hop(h0b, perm=twos)  7.98 us
    ppermute x3, starting transfers between devices, small_body(): hop(wide[step], perm=[(i, (i + step) % owners) for i in range(owners)])  4.95 us
    ppermute x1, waiting for transfers between devices, small_body(): h3a = hop(h2a, perm=pairs)  4.11 us
    ppermute x1, starting transfers between devices, small_body(): h2a = hop(h0a, perm=twos)  4.1 us
    pallas_call x1, Pallas kernels, first_half(): pl.pallas_call(functools.partial(first_kernel, cuts=cuts), in_specs=[VMEM...  3.5 us
    ppermute x3, waiting for transfers between devices, small_body(): hop(wide[step], perm=[(i, (i + step) % owners) for i in range(owners)])  2.49 us
    ppermute x1, starting transfers between devices, small_body(): h3b = hop(h2b, perm=pairs)  2.32 us
  transfers between devices with their start and end apart: 12, of which 7 were waited for; matrix products, arithmetic and copies ran while one was open for 0% of the time, Pallas kernels for 31%

profile of v5, /device:TPU:0, one launch (start us, length us, event | category | flops | bytes accessed | tf_op | source)
XLA Modules:
  0.0 52.7 jit_solution(16945332537171450856)
XLA Ops:
  0.0 1.0 %slice.3 = bf16[32,3584]{1,0:T(8,128)(2,1)S(1)} slice(bf16[32,7168]{1,0:T(8,128)(2,1)} %b0.5), slice={[0:32], [0:3584]} | slice | bytes 458752 | tf_op jit(solution)/shard_map/slice | solution.py:354
  1.0 4.1 %collective-permute-start.2 = (bf16[32,3584]{1,0:T(8,128)(2,1)S(1)}, bf16[32,3584]{1,0:T(8,128)(2,1)S(1)}, u32[]{:S(2)}, u32[]{:S(2)}) collective-permute-start(bf16[32,3584]{1,0:T(8,128)(2,1)S(1)} %slice.3), channel_id=1, source_target_pairs={{0,8},{8,0},{4,12},{12,4},{1,9},{9,1},{5,13},{13,5},{2,10},{10,2},... | collective-permute-start | bytes 688136 | tf_op jit(solution)/shard_map/ppermute | solution.py:355
  5.1 1.6 %collective-permute-start = (bf16[32,7168]{1,0:T(8,128)(2,1)}, bf16[32,7168]{1,0:T(8,128)(2,1)S(1)}, u32[]{:S(2)}, u32[]{:S(2)}) collective-permute-start(bf16[32,7168]{1,0:T(8,128)(2,1)} %b0.5), channel_id=1, source_target_pairs={{0,4},{4,0},{8,12},{12,8},{1,5},{5,1},{9,13},{13,9},{2,6},{6,2},{1... | collective-permute-start | bytes 1376264 | tf_op jit(solution)/shard_map/ppermute | solution.py:353
  6.6 5.3 %fetch_b.1.w_ref = bf16[3584,2048]{1,0:T(8,128)(2,1)S(1)} custom-call(bf16[7168,2048]{1,0:T(8,128)(2,1)} %w_far), custom_call_target="tpu_custom_call" | custom-call | bytes 14680064 | tf_op jit(solution)/shard_map/fetch_b/pallas_call | solution.py:61
  12.0 0.1 half_b.1
  12.1 0.0 copy-start.4
  12.1 0.0 copy-start.1
  12.1 0.4 collective-permute-start.1
  12.5 4.4 %fetch_a.1.w_ref = bf16[2688,2048]{1,0:T(8,128)(2,1)S(1)} custom-call(bf16[7168,2048]{1,0:T(8,128)(2,1)} %w_far), custom_call_target="tpu_custom_call" | custom-call | bytes 110100 | tf_op jit(solution)/shard_map/fetch_a/pallas_call | solution.py:61
  16.9 0.2 collective-permute-start.4
  17.1 0.7 %plan.1 = (bf16[2,16,32]{2,1,0:T(8,128)(2,1)S(1)}, bf16[32,64]{1,0:T(8,128)(2,1)S(1)}) custom-call(s32[8]{0:T(128)S(1)} %copy-done.3, s32[1,128]{1,0:T(1,128)S(1)} %bitcast.8), custom_call_target="tpu_custom_call" | custom-call | bytes 1048576 | tf_op jit(solution)/shard_map/plan/pallas_call | solution.py:257
  17.9 8.0 %collective-permute-done.1.b2 = bf16[32,3584]{1,0:T(8,128)(2,1)S(1)} collective-permute-done((bf16[32,3584]{1,0:T(8,128)(2,1)S(1)}, bf16[32,3584]{1,0:T(8,128)(2,1)S(1)}, u32[]{:S(2)}, u32[]{:S(2)}) %collective-permute-start.1) | collective-permute-done | bytes 229408 | tf_op jit(solution)/shard_map/ppermute | solution.py:359
  25.9 2.3 %collective-permute-start.3 = (bf16[32,3584]{1,0:T(8,128)(2,1)S(1)}, bf16[32,3584]{1,0:T(8,128)(2,1)S(1)}, u32[]{:S(2)}, u32[]{:S(2)}) collective-permute-start(bf16[32,3584]{1,0:T(8,128)(2,1)S(1)} %collective-permute-done.1.b2), channel_id=1, source_target_pairs={{0,4},{4,0},{8,12},{12,8},{1,5},{5,1},{9,13},{13,9},{2,6},{6,2},{1... | collective-permute-start | bytes 688136 | tf_op jit(solution)/shard_map/ppermute | solution.py:370
  28.2 4.1 %collective-permute-done.4.b3 = bf16[32,3584]{1,0:T(8,128)(2,1)S(1)} collective-permute-done((bf16[32,3584]{1,0:T(8,128)(2,1)S(1)}, bf16[32,3584]{1,0:T(8,128)(2,1)S(1)}, u32[]{:S(2)}, u32[]{:S(2)}) %collective-permute-start.4) | collective-permute-done | bytes 229408 | tf_op jit(solution)/shard_map/ppermute | solution.py:367
  32.3 3.5 %first_half.1 = (f32[128,2048]{1,0:T(8,128)S(1)}, f32[128,128]{1,0:T(8,128)S(1)}) custom-call(bf16[32,7168]{1,0:T(8,128)(2,1)S(1)} %copy-done, bf16[32,7168]{1,0:T(8,128)(2,1)S(1)} %collective-permute-done.b1, bf16[32,3584]{1,0:T(8,128)(2,1)S(1)} %collective-permute-done.2.b2, bf16[32,3584]{1,0:T(8,128)(2,1)S(1)} %collective-permute-done.4.b3, ...), custom_call_target="tpu_custom_call" | custom-call | flops 1996488704 | bytes 4194304 | tf_op jit(solution)/shard_map/first_half/pallas_call | solution.py:126
  35.8 0.4 second_low.1
  36.3 0.1 collective-permute-start.5
  36.4 1.2 %collective-permute-done.5.came = f32[64,128]{1,0:T(8,128)S(1)} collective-permute-done((f32[64,128]{1,0:T(8,128)S(1)}, f32[64,128]{1,0:T(8,128)S(1)}, u32[]{:S(2)}, u32[]{:S(2)}) %collective-permute-start.5) | collective-permute-done | bytes 32800 | tf_op jit(solution)/shard_map/ppermute | solution.py:376
  37.6 1.5 %collective-permute-start.6 = (f32[32,128]{1,0:T(8,128)S(1)}, f32[32,128]{1,0:T(8,128)S(1)}, u32[]{:S(2)}, u32[]{:S(2)}) collective-permute-start(f32[32,128]{1,0:T(8,128)S(1)} %get-tuple-element.61), channel_id=1, source_target_pairs={{0,2},{2,0},{1,3},{3,1},{4,6},{6,4},{5,7},{7,5},{8,10},{10,8},{9,1... | collective-permute-start | bytes 49160 | tf_op jit(solution)/shard_map/ppermute | solution.py:378
  39.1 2.1 %second_base.1 = (f32[64,2048]{1,0:T(8,128)S(1)}, bf16[64,2048]{1,0:T(8,128)(2,1)S(1)}) custom-call(bf16[32,7168]{1,0:T(8,128)(2,1)S(1)} %copy-done, bf16[32,7168]{1,0:T(8,128)(2,1)S(1)} %collective-permute-done.b1, bf16[32,3584]{1,0:T(8,128)(2,1)S(1)} %collective-permute-done.1.b2, bf16[32,3584]{1,0:T(8,128)(2,1)S(1)} %collective-permute-done.3.b3, ...), custom_call_target="tpu_custom_call" | custom-call | flops 1879048192 | bytes 4194304 | tf_op jit(solution)/shard_map/second_base/pallas_call | solution.py:178
  41.2 0.1 collective-permute-done.6.low_b
  41.3 0.6 %widen.1 = (bf16[16,2048]{1,0:T(8,128)(2,1)S(1)}, bf16[16,2048]{1,0:T(8,128)(2,1)S(1)}, bf16[16,2048]{1,0:T(8,128)(2,1)S(1)}, bf16[16,2048]{1,0:T(8,128)(2,1)S(1)}) custom-call(f32[32,128]{1,0:T(8,128)S(1)} %get-tuple-element.64.low_a, f32[32,128]{1,0:T(8,128)S(1)} %collective-permute-done.6.low_b, bf16[2,16,32]{2,1,0:T(8,128)(2,1)S(1)} %get-tuple-element.66.into_ref, ...), custom_call_target="tpu_custom_call" | custom-call | bytes 1048576 | tf_op jit(solution)/shard_map/widen/pallas_call | solution.py:289
  41.9 0.1 collective-permute-start.7
  42.0 1.1 %collective-permute-start.10 = (bf16[16,2048]{1,0:T(8,128)(2,1)S(1)}, bf16[16,2048]{1,0:T(8,128)(2,1)S(1)}, u32[]{:S(2)}, u32[]{:S(2)}) collective-permute-start(bf16[16,2048]{1,0:T(8,128)(2,1)S(1)} %get-tuple-element.77), channel_id=1, source_target_pairs={{0,8},{4,12},{8,0},{12,4},{1,9},{5,13},{9,1},{13,5},{2,10},{6,14},... | collective-permute-start | bytes 196616 | tf_op jit(solution)/shard_map/ppermute | solution.py:387
  43.1 1.9 %collective-permute-start.8 = (bf16[16,2048]{1,0:T(8,128)(2,1)S(1)}, bf16[16,2048]{1,0:T(8,128)(2,1)S(1)}, u32[]{:S(2)}, u32[]{:S(2)}) collective-permute-start(bf16[16,2048]{1,0:T(8,128)(2,1)S(1)} %get-tuple-element.75), channel_id=1, source_target_pairs={{0,4},{4,8},{8,12},{12,0},{1,5},{5,9},{9,13},{13,1},{2,6},{6,10},{... | collective-permute-start | bytes 196616 | tf_op jit(solution)/shard_map/ppermute | solution.py:387
  45.0 1.9 %collective-permute-start.9 = (bf16[16,2048]{1,0:T(8,128)(2,1)S(1)}, bf16[16,2048]{1,0:T(8,128)(2,1)S(1)}, u32[]{:S(2)}, u32[]{:S(2)}) collective-permute-start(bf16[16,2048]{1,0:T(8,128)(2,1)S(1)} %get-tuple-element.76), channel_id=1, source_target_pairs={{0,12},{4,0},{8,4},{12,8},{1,13},{5,1},{9,5},{13,9},{2,14},{6,2},{... | collective-permute-start | bytes 196616 | tf_op jit(solution)/shard_map/ppermute | solution.py:387
  47.0 1.5 %collective-permute-start.11 = (bf16[32,2048]{1,0:T(8,128)(2,1)S(1)}, bf16[32,2048]{1,0:T(8,128)(2,1)S(1)}, u32[]{:S(2)}, u32[]{:S(2)}) collective-permute-start(bf16[32,2048]{1,0:T(8,128)(2,1)S(1)} %get-tuple-element.78), channel_id=1, source_target_pairs={{0,2},{2,0},{1,3},{3,1},{4,6},{6,4},{5,7},{7,5},{8,10},{10,8},{9,1... | collective-permute-start | bytes 393224 | tf_op jit(solution)/shard_map/ppermute | solution.py:390
  48.5 2.2 %collective-permute-done.10.d2 = bf16[16,2048]{1,0:T(8,128)(2,1)S(1)} collective-permute-done((bf16[16,2048]{1,0:T(8,128)(2,1)S(1)}, bf16[16,2048]{1,0:T(8,128)(2,1)S(1)}, u32[]{:S(2)}, u32[]{:S(2)}) %collective-permute-start.10) | collective-permute-done | bytes 65568 | tf_op jit(solution)/shard_map/ppermute | solution.py:387
  50.7 0.3 collective-permute-done.9.d3
  51.0 0.2 add_rows.1.keep
  51.2 0.9 %collective-permute-done.11.came = bf16[32,2048]{1,0:T(8,128)(2,1)S(1)} collective-permute-done((bf16[32,2048]{1,0:T(8,128)(2,1)S(1)}, bf16[32,2048]{1,0:T(8,128)(2,1)S(1)}, u32[]{:S(2)}, u32[]{:S(2)}) %collective-permute-start.11) | collective-permute-done | bytes 131104 | tf_op jit(solution)/shard_map/ppermute | solution.py:390
  52.1 0.7 %last.1 = bf16[32,2048]{1,0:T(8,128)(2,1)} custom-call(f32[32,2048]{1,0:T(8,128)S(1)} %add_rows.1.keep, bf16[32,2048]{1,0:T(8,128)(2,1)S(1)} %collective-permute-done.11.came), custom_call_target="tpu_custom_call" | custom-call | bytes 1048576 | tf_op jit(solution)/shard_map/last/pallas_call | solution.py:322
  (15 shorter events, 0.1 us)
Async XLA Ops:
  1.0 11.0 %copy-start = (bf16[32,7168]{1,0:T(8,128)(2,1)S(1)}, bf16[32,7168]{1,0:T(8,128)(2,1)}, u32[]{:S(2)}) copy-start(bf16[32,7168]{1,0:T(8,128)(2,1)} %b0.5) | copy-start | bytes 1376260
  1.0 15.9 %collective-permute-start.2 = (bf16[32,3584]{1,0:T(8,128)(2,1)S(1)}, bf16[32,3584]{1,0:T(8,128)(2,1)S(1)}, u32[]{:S(2)}, u32[]{:S(2)}) collective-permute-start(bf16[32,3584]{1,0:T(8,128)(2,1)S(1)} %slice.3), channel_id=1, source_target_pairs={{0,8},{8,0},{4,12},{12,4},{1,9},{9,1},{5,13},{13,5},{2,10},{10,2},... | collective-permute-start | bytes 688136 | tf_op jit(solution)/shard_map/ppermute | solution.py:355
  5.1 27.2 %collective-permute-start = (bf16[32,7168]{1,0:T(8,128)(2,1)}, bf16[32,7168]{1,0:T(8,128)(2,1)S(1)}, u32[]{:S(2)}, u32[]{:S(2)}) collective-permute-start(bf16[32,7168]{1,0:T(8,128)(2,1)} %b0.5), channel_id=1, source_target_pairs={{0,4},{4,0},{8,12},{12,8},{1,5},{5,1},{9,13},{13,9},{2,6},{6,2},{1... | collective-permute-start | bytes 1376264 | tf_op jit(solution)/shard_map/ppermute | solution.py:353
  12.1 5.1 %copy-start.3 = (s32[8]{0:T(128)S(1)}, s32[8]{0:T(128)}, u32[]{:S(2)}) copy-start(s32[8]{0:T(128)} %storage.1) | copy-start | bytes 100
  12.1 5.0 %copy-start.4 = (s32[128]{0:T(128)S(1)}, s32[128]{0:T(128)}, u32[]{:S(2)}) copy-start(s32[128]{0:T(128)} %param.10) | copy-start | bytes 1540
  12.1 20.2 %copy-start.1 = (bf16[2,7168,64]{1,2,0:T(8,128)(2,1)S(1)}, bf16[2,7168,64]{1,2,0:T(8,128)(2,1)}, u32[]{:S(2)}) copy-start(bf16[2,7168,64]{1,2,0:T(8,128)(2,1)} %param.8) | copy-start | bytes 5505028
  12.1 13.8 %collective-permute-start.1 = (bf16[32,3584]{1,0:T(8,128)(2,1)S(1)}, bf16[32,3584]{1,0:T(8,128)(2,1)S(1)}, u32[]{:S(2)}, u32[]{:S(2)}) collective-permute-start(bf16[32,3584]{1,0:T(8,128)(2,1)S(1)} %half_b.1), channel_id=1, source_target_pairs={{0,8},{8,0},{4,12},{12,4},{1,9},{9,1},{5,13},{13,5},{2,10},{10,2},... | collective-permute-start | bytes 688136 | tf_op jit(solution)/shard_map/ppermute | solution.py:359
  16.9 15.4 %collective-permute-start.4 = (bf16[32,3584]{1,0:T(8,128)(2,1)S(1)}, bf16[32,3584]{1,0:T(8,128)(2,1)S(1)}, u32[]{:S(2)}, u32[]{:S(2)}) collective-permute-start(bf16[32,3584]{1,0:T(8,128)(2,1)S(1)} %collective-permute-done.2.b2), channel_id=1, source_target_pairs={{0,4},{4,0},{8,12},{12,8},{1,5},{5,1},{9,13},{13,9},{2,6},{6,2},{1... | collective-permute-start | bytes 688136 | tf_op jit(solution)/shard_map/ppermute | solution.py:367
  25.9 10.0 %collective-permute-start.3 = (bf16[32,3584]{1,0:T(8,128)(2,1)S(1)}, bf16[32,3584]{1,0:T(8,128)(2,1)S(1)}, u32[]{:S(2)}, u32[]{:S(2)}) collective-permute-start(bf16[32,3584]{1,0:T(8,128)(2,1)S(1)} %collective-permute-done.1.b2), channel_id=1, source_target_pairs={{0,4},{4,0},{8,12},{12,8},{1,5},{5,1},{9,13},{13,9},{2,6},{6,2},{1... | collective-permute-start | bytes 688136 | tf_op jit(solution)/shard_map/ppermute | solution.py:370
  35.8 5.5 %copy-start.2 = (bf16[2,64,8192]{2,1,0:T(8,128)(2,1)S(1)}, bf16[2,64,8192]{2,1,0:T(8,128)(2,1)}, u32[]{:S(2)}) copy-start(bf16[2,64,8192]{2,1,0:T(8,128)(2,1)} %param.9) | copy-start | bytes 6291460
  36.3 1.3 %collective-permute-start.5 = (f32[64,128]{1,0:T(8,128)S(1)}, f32[64,128]{1,0:T(8,128)S(1)}, u32[]{:S(2)}, u32[]{:S(2)}) collective-permute-start(f32[64,128]{1,0:T(8,128)S(1)} %get-tuple-element.56), channel_id=1, source_target_pairs={{0,1},{1,0},{2,3},{3,2},{4,5},{5,4},{6,7},{7,6},{8,9},{9,8},{10,11... | collective-permute-start | bytes 98312 | tf_op jit(solution)/shard_map/ppermute | solution.py:376
  37.6 3.7 %collective-permute-start.6 = (f32[32,128]{1,0:T(8,128)S(1)}, f32[32,128]{1,0:T(8,128)S(1)}, u32[]{:S(2)}, u32[]{:S(2)}) collective-permute-start(f32[32,128]{1,0:T(8,128)S(1)} %get-tuple-element.61), channel_id=1, source_target_pairs={{0,2},{2,0},{1,3},{3,1},{4,6},{6,4},{5,7},{7,5},{8,10},{10,8},{9,1... | collective-permute-start | bytes 49160 | tf_op jit(solution)/shard_map/ppermute | solution.py:378
  41.9 5.0 %collective-permute-start.7 = (bf16[64,2048]{1,0:T(8,128)(2,1)S(1)}, bf16[64,2048]{1,0:T(8,128)(2,1)S(1)}, u32[]{:S(2)}, u32[]{:S(2)}) collective-permute-start(bf16[64,2048]{1,0:T(8,128)(2,1)S(1)} %get-tuple-element.71), channel_id=1, source_target_pairs={{0,1},{1,0},{2,3},{3,2},{4,5},{5,4},{6,7},{7,6},{8,9},{9,8},{10,11... | collective-permute-start | bytes 786440 | tf_op jit(solution)/shard_map/ppermute | solution.py:384
  42.0 8.7 %collective-permute-start.10 = (bf16[16,2048]{1,0:T(8,128)(2,1)S(1)}, bf16[16,2048]{1,0:T(8,128)(2,1)S(1)}, u32[]{:S(2)}, u32[]{:S(2)}) collective-permute-start(bf16[16,2048]{1,0:T(8,128)(2,1)S(1)} %get-tuple-element.77), channel_id=1, source_target_pairs={{0,8},{4,12},{8,0},{12,4},{1,9},{5,13},{9,1},{13,5},{2,10},{6,14},... | collective-permute-start | bytes 196616 | tf_op jit(solution)/shard_map/ppermute | solution.py:387
  43.1 7.6 %collective-permute-start.8 = (bf16[16,2048]{1,0:T(8,128)(2,1)S(1)}, bf16[16,2048]{1,0:T(8,128)(2,1)S(1)}, u32[]{:S(2)}, u32[]{:S(2)}) collective-permute-start(bf16[16,2048]{1,0:T(8,128)(2,1)S(1)} %get-tuple-element.75), channel_id=1, source_target_pairs={{0,4},{4,8},{8,12},{12,0},{1,5},{5,9},{9,13},{13,1},{2,6},{6,10},{... | collective-permute-start | bytes 196616 | tf_op jit(solution)/shard_map/ppermute | solution.py:387
  45.0 6.0 %collective-permute-start.9 = (bf16[16,2048]{1,0:T(8,128)(2,1)S(1)}, bf16[16,2048]{1,0:T(8,128)(2,1)S(1)}, u32[]{:S(2)}, u32[]{:S(2)}) collective-permute-start(bf16[16,2048]{1,0:T(8,128)(2,1)S(1)} %get-tuple-element.76), channel_id=1, source_target_pairs={{0,12},{4,0},{8,4},{12,8},{1,13},{5,1},{9,5},{13,9},{2,14},{6,2},{... | collective-permute-start | bytes 196616 | tf_op jit(solution)/shard_map/ppermute | solution.py:387
  47.0 5.1 %collective-permute-start.11 = (bf16[32,2048]{1,0:T(8,128)(2,1)S(1)}, bf16[32,2048]{1,0:T(8,128)(2,1)S(1)}, u32[]{:S(2)}, u32[]{:S(2)}) collective-permute-start(bf16[32,2048]{1,0:T(8,128)(2,1)S(1)} %get-tuple-element.78), channel_id=1, source_target_pairs={{0,2},{2,0},{1,3},{3,1},{4,6},{6,4},{5,7},{7,5},{8,10},{10,8},{9,1... | collective-permute-start | bytes 393224 | tf_op jit(solution)/shard_map/ppermute | solution.py:390

commit v6 on v5

--- a/solution.py
+++ b/solution.py
@@ -16,6 +16,7 @@
 COLUMNS = 512
 FETCH_MIB = 27
 SHARE = 8
+MIDDLE = 12
 FETCH_A = 0.01
 FETCH_B = 1.0
 CUT = 7
@@ -79,8 +80,10 @@
     near = (lax.axis_index("seq") ^ (own & 1)) == 1
     far = (lax.axis_index("tensor") ^ (own >> 1)) == 1
     depth = blocks[2].shape[1]
-    b0, b1 = [block[:, skip : skip + depth] for block in blocks[:2]]
-    b2, b3 = [block[...] for block in blocks[2:]]
+    b0, b1, b2, b3 = [
+        block[...] if block.shape[1] == depth else block[:, skip : skip + depth]
+        for block in blocks
+    ]
     k0, k2 = jnp.where(near, b1, b0), jnp.where(near, b3, b2)
     s0, s2 = jnp.where(near, b0, b1), jnp.where(near, b2, b3)
     return jnp.concatenate(
@@ -95,7 +98,7 @@
 
 
 def first_kernel(
-    b0, b1, b2, b3, w_far, w_ref, a_ref, base_ref, low_ref, streamed, sems, *, cuts
+    b0, b1, b2, b3, w_far, w_ref, a_ref, base_ref, low_ref, streamed, sems, *, cuts, stop
 ):
     cut = streamed.shape[0]
     step = cut // cuts
@@ -109,7 +112,9 @@
     low_ref[...] = dot_nt(h, a_ref[:, :depth])
     for start in range(0, w_ref.shape[1], COLUMNS):
         columns = slice(start, start + COLUMNS)
-        base_ref[:, columns] = jnp.dot(h[:, cut:], w_ref[:, columns], preferred_element_type=F32)
+        base_ref[:, columns] = jnp.dot(
+            h[:, cut:stop], w_ref[: stop - cut, columns], preferred_element_type=F32
+        )
     for copy in copies:
         copy.wait()
     for start in range(0, w_ref.shape[1], COLUMNS):
@@ -119,12 +124,12 @@
         )
 
 
-def first_half(blocks, w_far, w, a, cut):
+def first_half(blocks, w_far, w, a, cut, stop):
     rows, extent = blocks[2].shape
     width, low = w.shape[1], a.shape[0]
     cuts = 4
     return pl.pallas_call(
-        functools.partial(first_kernel, cuts=cuts),
+        functools.partial(first_kernel, cuts=cuts, stop=stop),
         in_specs=[VMEM] * 4 + [HBM] + [VMEM] * 2,
         out_specs=[VMEM] * 2,
         out_shape=[
@@ -161,8 +166,30 @@
     )(*blocks, a, low_in)
 
 
+def middle_kernel(b0, b1, b2, b3, w_ref, base_in, base_ref, *, depth):
+    h = ordered((b0, b1, b2, b3), 0)
+    taken, held = h.shape[1] - depth, w_ref.shape[0] - depth
+    for start in range(0, w_ref.shape[1], COLUMNS):
+        columns = slice(start, start + COLUMNS)
+        part = jnp.dot(h[:, taken:], w_ref[held:, columns], preferred_element_type=F32)
+        base_ref[:, columns] = base_in[:, columns] + part
+
+
+def middle_base(blocks, w, base_in, depth):
+    rows = blocks[2].shape[0]
+    return pl.pallas_call(
+        functools.partial(middle_kernel, depth=depth),
+        in_specs=[VMEM] * 6,
+        out_specs=VMEM,
+        out_shape=jax.ShapeDtypeStruct(base_in.shape, F32),
+        compiler_params=params(8),
+        cost_estimate=cost(8 * rows * depth * w.shape[1], 4 * MIB),
+        name="middle_base",
+    )(*blocks, w, base_in)
+
+
 def base_kernel(b0, b1, b2, b3, w_ref, base_in, keep_ref, send_ref):
-    h = ordered((b0, b1, b2, b3), b0.shape[1] - b2.shape[1])
+    h = ordered((b0, b1, b2, b3), b1.shape[1] - b2.shape[1])
     rows = keep_ref.shape[0]
     for start in range(0, w_ref.shape[1], COLUMNS):
         columns = slice(start, start + COLUMNS)
@@ -249,7 +276,7 @@
         taken = here & (local_row == index)
         into_ref[index] = jnp.where(taken, 1.0, 0.0).astype(BF16)
     lane = lax.broadcasted_iota(jnp.int32, (rows, 4 * slots), 1)
-    hops = lax.rem(own + 4 - owner_column, 4)
+    hops = owner_column ^ own
     back_ref[...] = jnp.where(lane == hops * slots + rank_column, 1.0, 0.0).astype(BF16)
 
 
@@ -279,7 +306,7 @@
     packed = jnp.concatenate(terms, axis=1)
     width = outs[0].shape[1]
     for step, out in enumerate(outs):
-        start = pl.multiple_of(lax.rem(lax.axis_index("adapter") + step, len(outs)) * width, width)
+        start = pl.multiple_of((lax.axis_index("adapter") ^ step) * width, width)
         columns = b_ref[:, pl.ds(start, width)]
         out[...] = jnp.dot(packed, columns, preferred_element_type=F32).astype(BF16)
 
@@ -297,7 +324,7 @@
     )(low_a, low_b, into, b)
 
 
-def add_kernel(keep, back, d0, d1, d3, d2, out_ref):
+def add_kernel(keep, back, d0, d3, d1, d2, out_ref):
     deltas = jnp.concatenate([d[...] for d in (d0, d1, d2, d3)], axis=0)
     out_ref[...] = keep[...] + jnp.dot(back[...], deltas, preferred_element_type=F32)
 
@@ -311,7 +338,7 @@
         compiler_params=params(4),
         cost_estimate=cost(ADD_FLOPS, MIB),
         name="add_rows",
-    )(keep, back, deltas[0], deltas[1], deltas[3], deltas[2])
+    )(keep, back, deltas[0], deltas[3], deltas[1], deltas[2])
 
 
 def last_kernel(keep, came, out_ref):
@@ -339,6 +366,7 @@
     slots = max(2, min(rows // 2, 2 * rows // owners))
     half = 128 * (extent * SHARE // (128 * 16))
     cut = 128 * (extent * CUT // (128 * 56))
+    middle = 128 * (extent * MIDDLE // (128 * 56))
     rest = extent - half
 
     a = jnp.swapaxes(adapter_first_factors, 1, 2).reshape(stored * rank_extent, extent)
@@ -369,11 +397,15 @@
     h2b, into, back = barrier((h2b, into, back))
     h3b = hop(h2b, perm=pairs)
 
-    base_a, low_a = first_half((h0, h1, h2a, h3a), down_matrix, w_a, a, cut)
+    blocks_a = (h0, h1, h2a, h3a)
+    base_a, low_a = first_half(blocks_a, down_matrix, w_a, a, cut, half - middle)
     h3b, base_a, low_a = barrier((h3b, base_a, low_a))
     blocks_b = (h0, h1, h2b, h3b)
     low_keep, low_send = second_low(blocks_b, a, low_a)
+    w_a, low_keep = barrier((w_a, low_keep))
     low_came = lax.ppermute(low_send, "seq", both)
+    base_a = middle_base(blocks_a, w_a, base_a, middle)
+    low_came, base_a = barrier((low_came, base_a))
     low_keep, low_send = split_sum(low_keep, low_came, "split_low")
     low_came = lax.ppermute(low_send, "tensor", both)
     w_b, low_keep = barrier((w_b, low_keep))
@@ -384,7 +416,7 @@
     base_came = lax.ppermute(base_send, "seq", both)
     deltas = {0: wide[0]}
     for step in (1, 2, 3):
-        deltas[step] = hop(wide[step], perm=[(i, (i + step) % owners) for i in range(owners)])
+        deltas[step] = hop(wide[step], perm=[(i, i ^ step) for i in range(owners)])
     deltas = [deltas[step] for step in range(owners)]
     base_keep, base_send = split_sum(base_keep, base_came, "split_base")
     base_came = lax.ppermute(base_send, "tensor", both)

time: 52.9 us -> 52.3 us (0.989)
  waiting for transfers between devices: 16.8 us -> 16.2 us
    ppermute x1, waiting for transfers between devices: 1.19 us -> 0.18 us  [small_body(): low_came = lax.ppermute(low_send, 'seq', both)]
    ppermute x1, waiting for transfers between devices: 0.86 us -> 0.01 us  [small_body(): base_came = lax.ppermute(base_send, 'tensor', both)]
    ppermute x3, waiting for transfers between devices: 2.49 us -> 3.32 us  [small_body(): deltas[step] = hop(wide[step], perm=[(i, i ^ step) for i in range(owners)])]
    ppermute x3, starting transfers between devices: 4.95 us -> 4.42 us  [small_body(): deltas[step] = hop(wide[step], perm=[(i, i ^ step) for i in range(owners)])]
    pallas_call x1 -> x2, Pallas kernels: 3.5 us -> 4 us  [the longest x1 3 us: first_half(): pl.pallas_call(functools.partial(first_kernel, cuts=cuts, stop=stop), in_...]
  transfers between devices with their start and end apart: 12 -> 12, of which waited for: 7 -> 8; matrix products, arithmetic and copies ran while one was open for 0% -> 0% of each run, Pallas kernels for 31% -> 32%
where the time goes in v6:
time: 52.3 us; the launch traced here: 52.2 us
  Pallas kernels  18.5 us (35%)
  starting transfers between devices  16.4 us (31%)
  waiting for transfers between devices  16.2 us (31%)
  local copies, waits for them, and re-layouts  0.98 us (2%)
    pallas_call x3, Pallas kernels, fetch(): pl.pallas_call(functools.partial(fetch_kernel, pieces=pieces), in_specs=[...  9.78 us
    ppermute x1, waiting for transfers between devices, small_body(): h2b = hop(h0b, perm=twos)  7.98 us
    ppermute x3, starting transfers between devices, small_body(): deltas[step] = hop(wide[step], perm=[(i, i ^ step) for i in range(owners)])  4.42 us
    ppermute x1, waiting for transfers between devices, small_body(): h3a = hop(h2a, perm=pairs)  4.11 us
    ppermute x1, starting transfers between devices, small_body(): h2a = hop(h0a, perm=twos)  4.1 us
    ppermute x3, waiting for transfers between devices, small_body(): deltas[step] = hop(wide[step], perm=[(i, i ^ step) for i in range(owners)])  3.32 us
    pallas_call x1, Pallas kernels, first_half(): pl.pallas_call(functools.partial(first_kernel, cuts=cuts, stop=stop), in_...  3 us
    ppermute x1, starting transfers between devices, small_body(): h3b = hop(h2b, perm=pairs)  2.32 us
  transfers between devices with their start and end apart: 12, of which 8 were waited for; matrix products, arithmetic and copies ran while one was open for 0% of the time, Pallas kernels for 32%

profile of v6, /device:TPU:0, one launch (start us, length us, event | category | flops | bytes accessed | tf_op | source)
XLA Modules:
  0.0 52.2 jit_solution(13269087881916197714)
XLA Ops:
  0.0 1.0 %slice.3 = bf16[32,3584]{1,0:T(8,128)(2,1)S(1)} slice(bf16[32,7168]{1,0:T(8,128)(2,1)} %b0.7), slice={[0:32], [0:3584]} | slice | bytes 458752 | tf_op jit(solution)/shard_map/slice | solution.py:382
  1.0 4.1 %collective-permute-start.2 = (bf16[32,3584]{1,0:T(8,128)(2,1)S(1)}, bf16[32,3584]{1,0:T(8,128)(2,1)S(1)}, u32[]{:S(2)}, u32[]{:S(2)}) collective-permute-start(bf16[32,3584]{1,0:T(8,128)(2,1)S(1)} %slice.3), channel_id=1, source_target_pairs={{0,8},{8,0},{4,12},{12,4},{1,9},{9,1},{5,13},{13,5},{2,10},{10,2},... | collective-permute-start | bytes 688136 | tf_op jit(solution)/shard_map/ppermute | solution.py:383
  5.1 1.6 %collective-permute-start = (bf16[32,7168]{1,0:T(8,128)(2,1)}, bf16[32,7168]{1,0:T(8,128)(2,1)S(1)}, u32[]{:S(2)}, u32[]{:S(2)}) collective-permute-start(bf16[32,7168]{1,0:T(8,128)(2,1)} %b0.7), channel_id=1, source_target_pairs={{0,4},{4,0},{8,12},{12,8},{1,5},{5,1},{9,13},{13,9},{2,6},{6,2},{1... | collective-permute-start | bytes 1376264 | tf_op jit(solution)/shard_map/ppermute | solution.py:381
  6.6 5.3 %fetch_b.1.w_ref = bf16[3584,2048]{1,0:T(8,128)(2,1)S(1)} custom-call(bf16[7168,2048]{1,0:T(8,128)(2,1)} %w_far), custom_call_target="tpu_custom_call" | custom-call | bytes 14680064 | tf_op jit(solution)/shard_map/fetch_b/pallas_call | solution.py:62
  12.0 0.1 half_b.1
  12.1 0.0 copy-start.4
  12.1 0.4 collective-permute-start.1
  12.5 4.4 %fetch_a.1.w_ref = bf16[2688,2048]{1,0:T(8,128)(2,1)S(1)} custom-call(bf16[7168,2048]{1,0:T(8,128)(2,1)} %w_far), custom_call_target="tpu_custom_call" | custom-call | bytes 110100 | tf_op jit(solution)/shard_map/fetch_a/pallas_call | solution.py:62
  16.9 0.2 collective-permute-start.4
  17.1 0.7 %plan.1 = (bf16[2,16,32]{2,1,0:T(8,128)(2,1)S(1)}, bf16[32,64]{1,0:T(8,128)(2,1)S(1)}) custom-call(s32[8]{0:T(128)S(1)} %copy-done.3, s32[1,128]{1,0:T(1,128)S(1)} %bitcast.8), custom_call_target="tpu_custom_call" | custom-call | bytes 1048576 | tf_op jit(solution)/shard_map/plan/pallas_call | solution.py:284
  17.9 8.0 %collective-permute-done.1.b2 = bf16[32,3584]{1,0:T(8,128)(2,1)S(1)} collective-permute-done((bf16[32,3584]{1,0:T(8,128)(2,1)S(1)}, bf16[32,3584]{1,0:T(8,128)(2,1)S(1)}, u32[]{:S(2)}, u32[]{:S(2)}) %collective-permute-start.1) | collective-permute-done | bytes 229408 | tf_op jit(solution)/shard_map/ppermute | solution.py:387
  25.9 2.3 %collective-permute-start.3 = (bf16[32,3584]{1,0:T(8,128)(2,1)S(1)}, bf16[32,3584]{1,0:T(8,128)(2,1)S(1)}, u32[]{:S(2)}, u32[]{:S(2)}) collective-permute-start(bf16[32,3584]{1,0:T(8,128)(2,1)S(1)} %collective-permute-done.1.b2), channel_id=1, source_target_pairs={{0,4},{4,0},{8,12},{12,8},{1,5},{5,1},{9,13},{13,9},{2,6},{6,2},{1... | collective-permute-start | bytes 688136 | tf_op jit(solution)/shard_map/ppermute | solution.py:398
  28.2 4.1 %collective-permute-done.4.b3 = bf16[32,3584]{1,0:T(8,128)(2,1)S(1)} collective-permute-done((bf16[32,3584]{1,0:T(8,128)(2,1)S(1)}, bf16[32,3584]{1,0:T(8,128)(2,1)S(1)}, u32[]{:S(2)}, u32[]{:S(2)}) %collective-permute-start.4) | collective-permute-done | bytes 229408 | tf_op jit(solution)/shard_map/ppermute | solution.py:395
  32.3 3.0 %first_half.1 = (f32[128,2048]{1,0:T(8,128)S(1)}, f32[128,128]{1,0:T(8,128)S(1)}) custom-call(bf16[32,7168]{1,0:T(8,128)(2,1)S(1)} %copy-done, bf16[32,7168]{1,0:T(8,128)(2,1)S(1)} %collective-permute-done.b1, bf16[32,3584]{1,0:T(8,128)(2,1)S(1)} %collective-permute-done.2.b2, bf16[32,3584]{1,0:T(8,128)(2,1)S(1)} %collective-permute-done.4.b3, ...), custom_call_target="tpu_custom_call" | custom-call | flops 1996488704 | bytes 4194304 | tf_op jit(solution)/shard_map/first_half/pallas_call | solution.py:131
  35.3 0.4 collective-permute-done.3.b3
  35.8 0.4 second_low.1
  36.2 0.1 collective-permute-start.5
  36.3 1.0 %middle_base.1.base_in = f32[128,2048]{1,0:T(8,128)S(1)} custom-call(bf16[32,7168]{1,0:T(8,128)(2,1)S(1)} %copy-done, bf16[32,7168]{1,0:T(8,128)(2,1)S(1)} %collective-permute-done.b1, bf16[32,3584]{1,0:T(8,128)(2,1)S(1)} %collective-permute-done.2.b2, bf16[32,3584]{1,0:T(8,128)(2,1)S(1)} %collective-permute-done.4.b3, bf16[2688,2048]{1,0:T(8,128)(2,1)S(1)} %fetch_a.1.w_ref, ...), custom_call_target="tpu_custom_call" | custom-call | flops 805306368 | bytes 4194304 | tf_op jit(solution)/shard_map/middle_base/pallas_call | solution.py:180
  37.3 0.2 collective-permute-done.5.came
  37.5 1.5 %collective-permute-start.6 = (f32[32,128]{1,0:T(8,128)S(1)}, f32[32,128]{1,0:T(8,128)S(1)}, u32[]{:S(2)}, u32[]{:S(2)}) collective-permute-start(f32[32,128]{1,0:T(8,128)S(1)} %get-tuple-element.69), channel_id=1, source_target_pairs={{0,2},{2,0},{1,3},{3,1},{4,6},{6,4},{5,7},{7,5},{8,10},{10,8},{9,1... | collective-permute-start | bytes 49160 | tf_op jit(solution)/shard_map/ppermute | solution.py:410
  39.0 2.1 %second_base.1 = (f32[64,2048]{1,0:T(8,128)S(1)}, bf16[64,2048]{1,0:T(8,128)(2,1)S(1)}) custom-call(bf16[32,7168]{1,0:T(8,128)(2,1)S(1)} %copy-done, bf16[32,7168]{1,0:T(8,128)(2,1)S(1)} %collective-permute-done.b1, bf16[32,3584]{1,0:T(8,128)(2,1)S(1)} %collective-permute-done.1.b2, bf16[32,3584]{1,0:T(8,128)(2,1)S(1)} %collective-permute-done.3.b3, ...), custom_call_target="tpu_custom_call" | custom-call | flops 1879048192 | bytes 4194304 | tf_op jit(solution)/shard_map/second_base/pallas_call | solution.py:205
  41.1 0.1 collective-permute-done.6.low_b
  41.2 0.6 %widen.1 = (bf16[16,2048]{1,0:T(8,128)(2,1)S(1)}, bf16[16,2048]{1,0:T(8,128)(2,1)S(1)}, bf16[16,2048]{1,0:T(8,128)(2,1)S(1)}, bf16[16,2048]{1,0:T(8,128)(2,1)S(1)}) custom-call(f32[32,128]{1,0:T(8,128)S(1)} %get-tuple-element.72.low_a, f32[32,128]{1,0:T(8,128)S(1)} %collective-permute-done.6.low_b, bf16[2,16,32]{2,1,0:T(8,128)(2,1)S(1)} %get-tuple-element.74.into_ref, ...), custom_call_target="tpu_custom_call" | custom-call | bytes 1048576 | tf_op jit(solution)/shard_map/widen/pallas_call | solution.py:316
  41.8 0.1 collective-permute-start.7
  41.9 2.6 %collective-permute-start.8 = (bf16[16,2048]{1,0:T(8,128)(2,1)S(1)}, bf16[16,2048]{1,0:T(8,128)(2,1)S(1)}, u32[]{:S(2)}, u32[]{:S(2)}) collective-permute-start(bf16[16,2048]{1,0:T(8,128)(2,1)S(1)} %get-tuple-element.83), channel_id=1, source_target_pairs={{0,12},{4,8},{8,4},{12,0},{1,13},{5,9},{9,5},{13,1},{2,14},{6,10},... | collective-permute-start | bytes 196616 | tf_op jit(solution)/shard_map/ppermute | solution.py:419
  44.5 1.9 %collective-permute-start.10 = (bf16[16,2048]{1,0:T(8,128)(2,1)S(1)}, bf16[16,2048]{1,0:T(8,128)(2,1)S(1)}, u32[]{:S(2)}, u32[]{:S(2)}) collective-permute-start(bf16[16,2048]{1,0:T(8,128)(2,1)S(1)} %get-tuple-element.85), channel_id=1, source_target_pairs={{0,8},{4,12},{8,0},{12,4},{1,9},{5,13},{9,1},{13,5},{2,10},{6,14},... | collective-permute-start | bytes 196616 | tf_op jit(solution)/shard_map/ppermute | solution.py:419
  46.4 1.6 %collective-permute-start.11 = (bf16[32,2048]{1,0:T(8,128)(2,1)S(1)}, bf16[32,2048]{1,0:T(8,128)(2,1)S(1)}, u32[]{:S(2)}, u32[]{:S(2)}) collective-permute-start(bf16[32,2048]{1,0:T(8,128)(2,1)S(1)} %get-tuple-element.86), channel_id=1, source_target_pairs={{0,2},{2,0},{1,3},{3,1},{4,6},{6,4},{5,7},{7,5},{8,10},{10,8},{9,1... | collective-permute-start | bytes 393224 | tf_op jit(solution)/shard_map/ppermute | solution.py:422
  48.0 0.7 %collective-permute-done.8.d3 = bf16[16,2048]{1,0:T(8,128)(2,1)S(1)} collective-permute-done((bf16[16,2048]{1,0:T(8,128)(2,1)S(1)}, bf16[16,2048]{1,0:T(8,128)(2,1)S(1)}, u32[]{:S(2)}, u32[]{:S(2)}) %collective-permute-start.8) | collective-permute-done | bytes 65568 | tf_op jit(solution)/shard_map/ppermute | solution.py:419
  48.7 2.2 %collective-permute-done.9.d1 = bf16[16,2048]{1,0:T(8,128)(2,1)S(1)} collective-permute-done((bf16[16,2048]{1,0:T(8,128)(2,1)S(1)}, bf16[16,2048]{1,0:T(8,128)(2,1)S(1)}, u32[]{:S(2)}, u32[]{:S(2)}) %collective-permute-start.9) | collective-permute-done | bytes 65568 | tf_op jit(solution)/shard_map/ppermute | solution.py:419
  50.9 0.4 collective-permute-done.10.d2
  51.3 0.2 add_rows.1.keep
  51.5 0.7 %last.1 = bf16[32,2048]{1,0:T(8,128)(2,1)} custom-call(f32[32,2048]{1,0:T(8,128)S(1)} %add_rows.1.keep, bf16[32,2048]{1,0:T(8,128)(2,1)S(1)} %collective-permute-done.11.came), custom_call_target="tpu_custom_call" | custom-call | bytes 1048576 | tf_op jit(solution)/shard_map/last/pallas_call | solution.py:349
  (16 shorter events, 0.1 us)
Async XLA Ops:
  1.0 11.0 %copy-start = (bf16[32,7168]{1,0:T(8,128)(2,1)S(1)}, bf16[32,7168]{1,0:T(8,128)(2,1)}, u32[]{:S(2)}) copy-start(bf16[32,7168]{1,0:T(8,128)(2,1)} %b0.7) | copy-start | bytes 1376260
  1.0 15.9 %collective-permute-start.2 = (bf16[32,3584]{1,0:T(8,128)(2,1)S(1)}, bf16[32,3584]{1,0:T(8,128)(2,1)S(1)}, u32[]{:S(2)}, u32[]{:S(2)}) collective-permute-start(bf16[32,3584]{1,0:T(8,128)(2,1)S(1)} %slice.3), channel_id=1, source_target_pairs={{0,8},{8,0},{4,12},{12,4},{1,9},{9,1},{5,13},{13,5},{2,10},{10,2},... | collective-permute-start | bytes 688136 | tf_op jit(solution)/shard_map/ppermute | solution.py:383
  5.1 23.1 %collective-permute-start = (bf16[32,7168]{1,0:T(8,128)(2,1)}, bf16[32,7168]{1,0:T(8,128)(2,1)S(1)}, u32[]{:S(2)}, u32[]{:S(2)}) collective-permute-start(bf16[32,7168]{1,0:T(8,128)(2,1)} %b0.7), channel_id=1, source_target_pairs={{0,4},{4,0},{8,12},{12,8},{1,5},{5,1},{9,13},{13,9},{2,6},{6,2},{1... | collective-permute-start | bytes 1376264 | tf_op jit(solution)/shard_map/ppermute | solution.py:381
  12.1 5.1 %copy-start.3 = (s32[8]{0:T(128)S(1)}, s32[8]{0:T(128)}, u32[]{:S(2)}) copy-start(s32[8]{0:T(128)} %storage.1) | copy-start | bytes 100
  12.1 5.0 %copy-start.4 = (s32[128]{0:T(128)S(1)}, s32[128]{0:T(128)}, u32[]{:S(2)}) copy-start(s32[128]{0:T(128)} %param.10) | copy-start | bytes 1540
  12.1 20.2 %copy-start.1 = (bf16[2,7168,64]{1,2,0:T(8,128)(2,1)S(1)}, bf16[2,7168,64]{1,2,0:T(8,128)(2,1)}, u32[]{:S(2)}) copy-start(bf16[2,7168,64]{1,2,0:T(8,128)(2,1)} %param.8) | copy-start | bytes 5505028
  12.1 13.8 %collective-permute-start.1 = (bf16[32,3584]{1,0:T(8,128)(2,1)S(1)}, bf16[32,3584]{1,0:T(8,128)(2,1)S(1)}, u32[]{:S(2)}, u32[]{:S(2)}) collective-permute-start(bf16[32,3584]{1,0:T(8,128)(2,1)S(1)} %half_b.1), channel_id=1, source_target_pairs={{0,8},{8,0},{4,12},{12,4},{1,9},{9,1},{5,13},{13,5},{2,10},{10,2},... | collective-permute-start | bytes 688136 | tf_op jit(solution)/shard_map/ppermute | solution.py:387
  16.9 15.4 %collective-permute-start.4 = (bf16[32,3584]{1,0:T(8,128)(2,1)S(1)}, bf16[32,3584]{1,0:T(8,128)(2,1)S(1)}, u32[]{:S(2)}, u32[]{:S(2)}) collective-permute-start(bf16[32,3584]{1,0:T(8,128)(2,1)S(1)} %collective-permute-done.2.b2), channel_id=1, source_target_pairs={{0,4},{4,0},{8,12},{12,8},{1,5},{5,1},{9,13},{13,9},{2,6},{6,2},{1... | collective-permute-start | bytes 688136 | tf_op jit(solution)/shard_map/ppermute | solution.py:395
  25.9 9.9 %collective-permute-start.3 = (bf16[32,3584]{1,0:T(8,128)(2,1)S(1)}, bf16[32,3584]{1,0:T(8,128)(2,1)S(1)}, u32[]{:S(2)}, u32[]{:S(2)}) collective-permute-start(bf16[32,3584]{1,0:T(8,128)(2,1)S(1)} %collective-permute-done.1.b2), channel_id=1, source_target_pairs={{0,4},{4,0},{8,12},{12,8},{1,5},{5,1},{9,13},{13,9},{2,6},{6,2},{1... | collective-permute-start | bytes 688136 | tf_op jit(solution)/shard_map/ppermute | solution.py:398
  36.2 1.3 %collective-permute-start.5 = (f32[64,128]{1,0:T(8,128)S(1)}, f32[64,128]{1,0:T(8,128)S(1)}, u32[]{:S(2)}, u32[]{:S(2)}) collective-permute-start(f32[64,128]{1,0:T(8,128)S(1)} %get-tuple-element.61), channel_id=1, source_target_pairs={{0,1},{1,0},{2,3},{3,2},{4,5},{5,4},{6,7},{7,6},{8,9},{9,8},{10,11... | collective-permute-start | bytes 98312 | tf_op jit(solution)/shard_map/ppermute | solution.py:406
  37.3 3.9 %copy-start.2 = (bf16[2,64,8192]{2,1,0:T(8,128)(2,1)S(1)}, bf16[2,64,8192]{2,1,0:T(8,128)(2,1)}, u32[]{:S(2)}) copy-start(bf16[2,64,8192]{2,1,0:T(8,128)(2,1)} %param.9) | copy-start | bytes 6291460
  37.5 3.7 %collective-permute-start.6 = (f32[32,128]{1,0:T(8,128)S(1)}, f32[32,128]{1,0:T(8,128)S(1)}, u32[]{:S(2)}, u32[]{:S(2)}) collective-permute-start(f32[32,128]{1,0:T(8,128)S(1)} %get-tuple-element.69), channel_id=1, source_target_pairs={{0,2},{2,0},{1,3},{3,1},{4,6},{6,4},{5,7},{7,5},{8,10},{10,8},{9,1... | collective-permute-start | bytes 49160 | tf_op jit(solution)/shard_map/ppermute | solution.py:410
  41.8 4.5 %collective-permute-start.7 = (bf16[64,2048]{1,0:T(8,128)(2,1)S(1)}, bf16[64,2048]{1,0:T(8,128)(2,1)S(1)}, u32[]{:S(2)}, u32[]{:S(2)}) collective-permute-start(bf16[64,2048]{1,0:T(8,128)(2,1)S(1)} %get-tuple-element.79), channel_id=1, source_target_pairs={{0,1},{1,0},{2,3},{3,2},{4,5},{5,4},{6,7},{7,6},{8,9},{9,8},{10,11... | collective-permute-start | bytes 786440 | tf_op jit(solution)/shard_map/ppermute | solution.py:416
  41.9 6.8 %collective-permute-start.8 = (bf16[16,2048]{1,0:T(8,128)(2,1)S(1)}, bf16[16,2048]{1,0:T(8,128)(2,1)S(1)}, u32[]{:S(2)}, u32[]{:S(2)}) collective-permute-start(bf16[16,2048]{1,0:T(8,128)(2,1)S(1)} %get-tuple-element.83), channel_id=1, source_target_pairs={{0,12},{4,8},{8,4},{12,0},{1,13},{5,9},{9,5},{13,1},{2,14},{6,10},... | collective-permute-start | bytes 196616 | tf_op jit(solution)/shard_map/ppermute | solution.py:419
  44.5 6.4 %collective-permute-start.9 = (bf16[16,2048]{1,0:T(8,128)(2,1)S(1)}, bf16[16,2048]{1,0:T(8,128)(2,1)S(1)}, u32[]{:S(2)}, u32[]{:S(2)}) collective-permute-start(bf16[16,2048]{1,0:T(8,128)(2,1)S(1)} %get-tuple-element.84), channel_id=1, source_target_pairs={{0,4},{4,0},{8,12},{12,8},{1,5},{5,1},{9,13},{13,9},{2,6},{6,2},{1... | collective-permute-start | bytes 196616 | tf_op jit(solution)/shard_map/ppermute | solution.py:419
  44.5 6.8 %collective-permute-start.10 = (bf16[16,2048]{1,0:T(8,128)(2,1)S(1)}, bf16[16,2048]{1,0:T(8,128)(2,1)S(1)}, u32[]{:S(2)}, u32[]{:S(2)}) collective-permute-start(bf16[16,2048]{1,0:T(8,128)(2,1)S(1)} %get-tuple-element.85), channel_id=1, source_target_pairs={{0,8},{4,12},{8,0},{12,4},{1,9},{5,13},{9,1},{13,5},{2,10},{6,14},... | collective-permute-start | bytes 196616 | tf_op jit(solution)/shard_map/ppermute | solution.py:419
  46.4 5.1 %collective-permute-start.11 = (bf16[32,2048]{1,0:T(8,128)(2,1)S(1)}, bf16[32,2048]{1,0:T(8,128)(2,1)S(1)}, u32[]{:S(2)}, u32[]{:S(2)}) collective-permute-start(bf16[32,2048]{1,0:T(8,128)(2,1)S(1)} %get-tuple-element.86), channel_id=1, source_target_pairs={{0,2},{2,0},{1,3},{3,1},{4,6},{6,4},{5,7},{7,5},{8,10},{10,8},{9,1... | collective-permute-start | bytes 393224 | tf_op jit(solution)/shard_map/ppermute | solution.py:422

commit v7 on v6

--- a/solution.py
+++ b/solution.py
@@ -15,7 +15,7 @@
 HBM = pl.BlockSpec(memory_space=pltpu.HBM)
 COLUMNS = 512
 FETCH_MIB = 27
-SHARE = 8
+SHARE = 26
 MIDDLE = 12
 FETCH_A = 0.01
 FETCH_B = 1.0
@@ -364,7 +364,7 @@
     rows, extent = hidden.shape
     stored, _, rank_extent = adapter_first_factors.shape
     slots = max(2, min(rows // 2, 2 * rows // owners))
-    half = 128 * (extent * SHARE // (128 * 16))
+    half = 128 * (extent * SHARE // (128 * 56))
     cut = 128 * (extent * CUT // (128 * 56))
     middle = 128 * (extent * MIDDLE // (128 * 56))
     rest = extent - half
@@ -381,20 +381,21 @@
     h1 = hop(h0, perm=pairs)
     h0a = hidden[:, :half]
     h2a = hop(h0a, perm=twos)
-    (w_b,) = fetch((down_matrix,), ((0, half, rest, 7),), "fetch_b", FETCH_B)
-    w_b, hidden, down_matrix = barrier((w_b, hidden, down_matrix))
     (h0b,) = fetch((hidden,), ((1, half, rest, 1),), "half_b")
+    h0b, down_matrix = barrier((h0b, down_matrix))
+    (w_b,) = fetch((down_matrix,), ((0, half, rest, 8),), "fetch_b", FETCH_B)
+    w_b, down_matrix = barrier((w_b, down_matrix))
     h2b = hop(h0b, perm=twos)
+    h2a, w_b, down_matrix, adapter_index_rows = barrier((h2a, w_b, down_matrix, adapter_index_rows))
+    h3a = hop(h2a, perm=pairs)
     (w_a,) = fetch(
         (down_matrix,),
         ((0, cut, half - cut, 4),),
         "fetch_a",
         FETCH_A,
     )
-    h2a, w_a, adapter_index_rows = barrier((h2a, w_a, adapter_index_rows))
-    h3a = hop(h2a, perm=pairs)
     into, back = plan(storage, adapter_index_rows, rows, stored, slots)
-    h2b, into, back = barrier((h2b, into, back))
+    h2b, into, back, w_a = barrier((h2b, into, back, w_a))
     h3b = hop(h2b, perm=pairs)
 
     blocks_a = (h0, h1, h2a, h3a)

time: 52.3 us -> 50.4 us (0.964)
  waiting for transfers between devices: 16.2 us -> 10.9 us
  starting transfers between devices: 16.4 us -> 17.9 us
  local copies, waits for them, and re-layouts: 0.98 us -> 2.02 us
  Pallas kernels: 18.5 us -> 19.1 us
    ppermute x1, waiting for transfers between devices: 7.98 us -> 0.01 us  [small_body(): h2b = hop(h0b, perm=twos)]
    ppermute x1, waiting for transfers between devices: 0.01 us -> 4.94 us  [small_body(): h2a = hop(h0a, perm=twos)]
    ppermute x1, starting transfers between devices: 0.22 us -> 3.55 us  [small_body(): h3a = hop(h2a, perm=pairs)]
    ppermute x1, waiting for transfers between devices: 4.11 us -> 1.49 us  [small_body(): h3a = hop(h2a, perm=pairs)]
    ppermute x1, starting transfers between devices: 2.32 us -> 0.47 us  [small_body(): h3b = hop(h2b, perm=pairs)]
    ppermute x1, starting transfers between devices: 4.1 us -> 2.65 us  [small_body(): h2a = hop(h0a, perm=twos)]
    ppermute x1, starting transfers between devices: 1.58 us -> 3.02 us  [small_body(): h1 = hop(h0, perm=pairs)]
    unnamed x10, local copies, waits for them, and re-layouts: 0.03 us -> 1.04 us
  transfers between devices with their start and end apart: 12 -> 12, of which waited for: 8 -> 7; matrix products, arithmetic and copies ran while one was open for 0% -> 2% of each run, Pallas kernels for 32% -> 35%
where the time goes in v7:
time: 50.4 us; the launch traced here: 50.2 us
  Pallas kernels  19.1 us (38%)
  starting transfers between devices  17.9 us (36%)
  waiting for transfers between devices  10.9 us (22%)
  local copies, waits for them, and re-layouts  2.02 us (4%)
    pallas_call x3, Pallas kernels, fetch(): pl.pallas_call(functools.partial(fetch_kernel, pieces=pieces), in_specs=[...  9.64 us
    ppermute x1, waiting for transfers between devices, small_body(): h2a = hop(h0a, perm=twos)  4.94 us
    ppermute x3, starting transfers between devices, small_body(): deltas[step] = hop(wide[step], perm=[(i, i ^ step) for i in range(owners)])  4.4 us
    pallas_call x1, Pallas kernels, first_half(): pl.pallas_call(functools.partial(first_kernel, cuts=cuts, stop=stop), in_...  3.59 us
    ppermute x1, starting transfers between devices, small_body(): h3a = hop(h2a, perm=pairs)  3.55 us
    ppermute x3, waiting for transfers between devices, small_body(): deltas[step] = hop(wide[step], perm=[(i, i ^ step) for i in range(owners)])  3.54 us
    ppermute x1, starting transfers between devices, small_body(): h1 = hop(h0, perm=pairs)  3.02 us
    ppermute x1, starting transfers between devices, small_body(): h2a = hop(h0a, perm=twos)  2.65 us
  transfers between devices with their start and end apart: 12, of which 7 were waited for; matrix products, arithmetic and copies ran while one was open for 2% of the time, Pallas kernels for 35%

profile of v7, /device:TPU:0, one launch (start us, length us, event | category | flops | bytes accessed | tf_op | source)
XLA Modules:
  0.0 50.2 jit_solution(10482524735230651329)
XLA Ops:
  0.0 3.0 %collective-permute-start = (bf16[32,7168]{1,0:T(8,128)(2,1)}, bf16[32,7168]{1,0:T(8,128)(2,1)S(1)}, u32[]{:S(2)}, u32[]{:S(2)}) collective-permute-start(bf16[32,7168]{1,0:T(8,128)(2,1)} %b0.7), channel_id=1, source_target_pairs={{0,4},{4,0},{8,12},{12,8},{1,5},{5,1},{9,13},{13,9},{2,6},{6,2},{1... | collective-permute-start | bytes 1376264 | tf_op jit(solution)/shard_map/ppermute | solution.py:381
  3.0 1.0 %slice.3 = bf16[32,3328]{1,0:T(8,128)(2,1)S(1)} slice(bf16[32,7168]{1,0:T(8,128)(2,1)} %b0.7), slice={[0:32], [0:3328]} | slice | bytes 425984 | tf_op jit(solution)/shard_map/slice | solution.py:382
  4.0 2.7 %collective-permute-start.2 = (bf16[32,3328]{1,0:T(8,128)(2,1)S(1)}, bf16[32,3328]{1,0:T(8,128)(2,1)S(1)}, u32[]{:S(2)}, u32[]{:S(2)}) collective-permute-start(bf16[32,3328]{1,0:T(8,128)(2,1)S(1)} %slice.3), channel_id=1, source_target_pairs={{0,8},{8,0},{4,12},{12,4},{1,9},{9,1},{5,13},{13,5},{2,10},{10,2},... | collective-permute-start | bytes 638984 | tf_op jit(solution)/shard_map/ppermute | solution.py:383
  6.7 1.0 %copy-done = bf16[32,7168]{1,0:T(8,128)(2,1)S(1)} copy-done((bf16[32,7168]{1,0:T(8,128)(2,1)S(1)}, bf16[32,7168]{1,0:T(8,128)(2,1)}, u32[]{:S(2)}) %copy-start) | copy-done | bytes 458776
  7.7 0.1 half_b.1
  7.8 0.4 collective-permute-start.1
  8.2 5.6 %fetch_b.1.w_ref = bf16[3840,2048]{1,0:T(8,128)(2,1)S(1)} custom-call(bf16[7168,2048]{1,0:T(8,128)(2,1)} %w_far), custom_call_target="tpu_custom_call" | custom-call | bytes 15728640 | tf_op jit(solution)/shard_map/fetch_b/pallas_call | solution.py:62
  13.8 0.0 copy-start.3
  13.8 4.9 %collective-permute-done.2.b2 = bf16[32,3328]{1,0:T(8,128)(2,1)S(1)} collective-permute-done((bf16[32,3328]{1,0:T(8,128)(2,1)S(1)}, bf16[32,3328]{1,0:T(8,128)(2,1)S(1)}, u32[]{:S(2)}, u32[]{:S(2)}) %collective-permute-start.2) | collective-permute-done | bytes 213024 | tf_op jit(solution)/shard_map/ppermute | solution.py:383
  18.8 3.5 %collective-permute-start.4 = (bf16[32,3328]{1,0:T(8,128)(2,1)S(1)}, bf16[32,3328]{1,0:T(8,128)(2,1)S(1)}, u32[]{:S(2)}, u32[]{:S(2)}) collective-permute-start(bf16[32,3328]{1,0:T(8,128)(2,1)S(1)} %collective-permute-done.2.b2), channel_id=1, source_target_pairs={{0,4},{4,0},{8,12},{12,8},{1,5},{5,1},{9,13},{13,9},{2,6},{6,2},{1... | collective-permute-start | bytes 638984 | tf_op jit(solution)/shard_map/ppermute | solution.py:390
  22.3 3.9 %fetch_a.1.w_ref = bf16[2432,2048]{1,0:T(8,128)(2,1)S(1)} custom-call(bf16[7168,2048]{1,0:T(8,128)(2,1)} %w_far), custom_call_target="tpu_custom_call" | custom-call | bytes 99614 | tf_op jit(solution)/shard_map/fetch_a/pallas_call | solution.py:62
  26.3 0.7 %plan.1 = (bf16[2,16,32]{2,1,0:T(8,128)(2,1)S(1)}, bf16[32,64]{1,0:T(8,128)(2,1)S(1)}) custom-call(s32[8]{0:T(128)S(1)} %copy-done.3, s32[1,128]{1,0:T(1,128)S(1)} %bitcast.8), custom_call_target="tpu_custom_call" | custom-call | bytes 1048576 | tf_op jit(solution)/shard_map/plan/pallas_call | solution.py:284
  27.1 0.5 collective-permute-start.3
  27.5 1.5 %collective-permute-done.4.b3 = bf16[32,3328]{1,0:T(8,128)(2,1)S(1)} collective-permute-done((bf16[32,3328]{1,0:T(8,128)(2,1)S(1)}, bf16[32,3328]{1,0:T(8,128)(2,1)S(1)}, u32[]{:S(2)}, u32[]{:S(2)}) %collective-permute-start.4) | collective-permute-done | bytes 213024 | tf_op jit(solution)/shard_map/ppermute | solution.py:390
  29.0 3.6 %first_half.1 = (f32[128,2048]{1,0:T(8,128)S(1)}, f32[128,128]{1,0:T(8,128)S(1)}) custom-call(bf16[32,7168]{1,0:T(8,128)(2,1)S(1)} %copy-done, bf16[32,7168]{1,0:T(8,128)(2,1)S(1)} %collective-permute-done.b1, bf16[32,3328]{1,0:T(8,128)(2,1)S(1)} %collective-permute-done.2.b2, bf16[32,3328]{1,0:T(8,128)(2,1)S(1)} %collective-permute-done.4.b3, ...), custom_call_target="tpu_custom_call" | custom-call | flops 1853882368 | bytes 4194304 | tf_op jit(solution)/shard_map/first_half/pallas_call | solution.py:131
  32.6 0.8 %collective-permute-done.3.b3 = bf16[32,3840]{1,0:T(8,128)(2,1)S(1)} collective-permute-done((bf16[32,3840]{1,0:T(8,128)(2,1)S(1)}, bf16[32,3840]{1,0:T(8,128)(2,1)S(1)}, u32[]{:S(2)}, u32[]{:S(2)}) %collective-permute-start.3) | collective-permute-done | bytes 245792 | tf_op jit(solution)/shard_map/ppermute | solution.py:399
  33.4 0.4 second_low.1
  33.9 0.1 collective-permute-start.5
  33.9 1.0 %middle_base.1.base_in = f32[128,2048]{1,0:T(8,128)S(1)} custom-call(bf16[32,7168]{1,0:T(8,128)(2,1)S(1)} %copy-done, bf16[32,7168]{1,0:T(8,128)(2,1)S(1)} %collective-permute-done.b1, bf16[32,3328]{1,0:T(8,128)(2,1)S(1)} %collective-permute-done.2.b2, bf16[32,3328]{1,0:T(8,128)(2,1)S(1)} %collective-permute-done.4.b3, bf16[2432,2048]{1,0:T(8,128)(2,1)S(1)} %fetch_a.1.w_ref, ...), custom_call_target="tpu_custom_call" | custom-call | flops 805306368 | bytes 4194304 | tf_op jit(solution)/shard_map/middle_base/pallas_call | solution.py:180
  34.9 0.2 collective-permute-done.5.came
  35.1 1.7 %collective-permute-start.6 = (f32[32,128]{1,0:T(8,128)S(1)}, f32[32,128]{1,0:T(8,128)S(1)}, u32[]{:S(2)}, u32[]{:S(2)}) collective-permute-start(f32[32,128]{1,0:T(8,128)S(1)} %get-tuple-element.75), channel_id=1, source_target_pairs={{0,2},{2,0},{1,3},{3,1},{4,6},{6,4},{5,7},{7,5},{8,10},{10,8},{9,1... | collective-permute-start | bytes 49160 | tf_op jit(solution)/shard_map/ppermute | solution.py:411
  36.8 2.2 %second_base.1 = (f32[64,2048]{1,0:T(8,128)S(1)}, bf16[64,2048]{1,0:T(8,128)(2,1)S(1)}) custom-call(bf16[32,7168]{1,0:T(8,128)(2,1)S(1)} %copy-done, bf16[32,7168]{1,0:T(8,128)(2,1)S(1)} %collective-permute-done.b1, bf16[32,3840]{1,0:T(8,128)(2,1)S(1)} %collective-permute-done.1.b2, bf16[32,3840]{1,0:T(8,128)(2,1)S(1)} %collective-permute-done.3.b3, ...), custom_call_target="tpu_custom_call" | custom-call | flops 2013265920 | bytes 4194304 | tf_op jit(solution)/shard_map/second_base/pallas_call | solution.py:205
  39.0 0.6 %widen.1 = (bf16[16,2048]{1,0:T(8,128)(2,1)S(1)}, bf16[16,2048]{1,0:T(8,128)(2,1)S(1)}, bf16[16,2048]{1,0:T(8,128)(2,1)S(1)}, bf16[16,2048]{1,0:T(8,128)(2,1)S(1)}) custom-call(f32[32,128]{1,0:T(8,128)S(1)} %get-tuple-element.78.low_a, f32[32,128]{1,0:T(8,128)S(1)} %collective-permute-done.6.low_b, bf16[2,16,32]{2,1,0:T(8,128)(2,1)S(1)} %get-tuple-element.80.into_ref, ...), custom_call_target="tpu_custom_call" | custom-call | bytes 1048576 | tf_op jit(solution)/shard_map/widen/pallas_call | solution.py:316
  39.6 0.2 collective-permute-start.7
  39.8 3.6 %collective-permute-start.8 = (bf16[16,2048]{1,0:T(8,128)(2,1)S(1)}, bf16[16,2048]{1,0:T(8,128)(2,1)S(1)}, u32[]{:S(2)}, u32[]{:S(2)}) collective-permute-start(bf16[16,2048]{1,0:T(8,128)(2,1)S(1)} %get-tuple-element.89), channel_id=1, source_target_pairs={{0,12},{4,8},{8,4},{12,0},{1,13},{5,9},{9,5},{13,1},{2,14},{6,10},... | collective-permute-start | bytes 196616 | tf_op jit(solution)/shard_map/ppermute | solution.py:420
  43.5 0.8 %collective-permute-start.10 = (bf16[16,2048]{1,0:T(8,128)(2,1)S(1)}, bf16[16,2048]{1,0:T(8,128)(2,1)S(1)}, u32[]{:S(2)}, u32[]{:S(2)}) collective-permute-start(bf16[16,2048]{1,0:T(8,128)(2,1)S(1)} %get-tuple-element.91), channel_id=1, source_target_pairs={{0,8},{4,12},{8,0},{12,4},{1,9},{5,13},{9,1},{13,5},{2,10},{6,14},... | collective-permute-start | bytes 196616 | tf_op jit(solution)/shard_map/ppermute | solution.py:420
  44.3 1.5 %collective-permute-start.11 = (bf16[32,2048]{1,0:T(8,128)(2,1)S(1)}, bf16[32,2048]{1,0:T(8,128)(2,1)S(1)}, u32[]{:S(2)}, u32[]{:S(2)}) collective-permute-start(bf16[32,2048]{1,0:T(8,128)(2,1)S(1)} %get-tuple-element.92), channel_id=1, source_target_pairs={{0,2},{2,0},{1,3},{3,1},{4,6},{6,4},{5,7},{7,5},{8,10},{10,8},{9,1... | collective-permute-start | bytes 393224 | tf_op jit(solution)/shard_map/ppermute | solution.py:423
  45.8 0.8 %collective-permute-done.8.d3 = bf16[16,2048]{1,0:T(8,128)(2,1)S(1)} collective-permute-done((bf16[16,2048]{1,0:T(8,128)(2,1)S(1)}, bf16[16,2048]{1,0:T(8,128)(2,1)S(1)}, u32[]{:S(2)}, u32[]{:S(2)}) %collective-permute-start.8) | collective-permute-done | bytes 65568 | tf_op jit(solution)/shard_map/ppermute | solution.py:420
  46.5 2.3 %collective-permute-done.9.d1 = bf16[16,2048]{1,0:T(8,128)(2,1)S(1)} collective-permute-done((bf16[16,2048]{1,0:T(8,128)(2,1)S(1)}, bf16[16,2048]{1,0:T(8,128)(2,1)S(1)}, u32[]{:S(2)}, u32[]{:S(2)}) %collective-permute-start.9) | collective-permute-done | bytes 65568 | tf_op jit(solution)/shard_map/ppermute | solution.py:420
  48.8 0.5 collective-permute-done.10.d2
  49.3 0.2 add_rows.1.keep
  49.5 0.7 %last.1 = bf16[32,2048]{1,0:T(8,128)(2,1)} custom-call(f32[32,2048]{1,0:T(8,128)S(1)} %add_rows.1.keep, bf16[32,2048]{1,0:T(8,128)(2,1)S(1)} %collective-permute-done.11.came), custom_call_target="tpu_custom_call" | custom-call | bytes 1048576 | tf_op jit(solution)/shard_map/last/pallas_call | solution.py:349
  (16 shorter events, 0.1 us)
Async XLA Ops:
  0.0 29.0 %collective-permute-start = (bf16[32,7168]{1,0:T(8,128)(2,1)}, bf16[32,7168]{1,0:T(8,128)(2,1)S(1)}, u32[]{:S(2)}, u32[]{:S(2)}) collective-permute-start(bf16[32,7168]{1,0:T(8,128)(2,1)} %b0.7), channel_id=1, source_target_pairs={{0,4},{4,0},{8,12},{12,8},{1,5},{5,1},{9,13},{13,9},{2,6},{6,2},{1... | collective-permute-start | bytes 1376264 | tf_op jit(solution)/shard_map/ppermute | solution.py:381
  4.0 14.8 %collective-permute-start.2 = (bf16[32,3328]{1,0:T(8,128)(2,1)S(1)}, bf16[32,3328]{1,0:T(8,128)(2,1)S(1)}, u32[]{:S(2)}, u32[]{:S(2)}) collective-permute-start(bf16[32,3328]{1,0:T(8,128)(2,1)S(1)} %slice.3), channel_id=1, source_target_pairs={{0,8},{8,0},{4,12},{12,4},{1,9},{9,1},{5,13},{13,5},{2,10},{10,2},... | collective-permute-start | bytes 638984 | tf_op jit(solution)/shard_map/ppermute | solution.py:383
  6.7 1.0 %copy-start = (bf16[32,7168]{1,0:T(8,128)(2,1)S(1)}, bf16[32,7168]{1,0:T(8,128)(2,1)}, u32[]{:S(2)}) copy-start(bf16[32,7168]{1,0:T(8,128)(2,1)} %b0.7) | copy-start | bytes 1376260
  7.8 19.3 %collective-permute-start.1 = (bf16[32,3840]{1,0:T(8,128)(2,1)S(1)}, bf16[32,3840]{1,0:T(8,128)(2,1)S(1)}, u32[]{:S(2)}, u32[]{:S(2)}) collective-permute-start(bf16[32,3840]{1,0:T(8,128)(2,1)S(1)} %half_b.1), channel_id=1, source_target_pairs={{0,8},{8,0},{4,12},{12,4},{1,9},{9,1},{5,13},{13,5},{2,10},{10,2},... | collective-permute-start | bytes 737288 | tf_op jit(solution)/shard_map/ppermute | solution.py:388
  13.8 12.5 %copy-start.3 = (s32[8]{0:T(128)S(1)}, s32[8]{0:T(128)}, u32[]{:S(2)}) copy-start(s32[8]{0:T(128)} %storage.1) | copy-start | bytes 100
  13.8 12.5 %copy-start.4 = (s32[128]{0:T(128)S(1)}, s32[128]{0:T(128)}, u32[]{:S(2)}) copy-start(s32[128]{0:T(128)} %param.10) | copy-start | bytes 1540
  13.8 15.2 %copy-start.1 = (bf16[2,7168,64]{1,2,0:T(8,128)(2,1)S(1)}, bf16[2,7168,64]{1,2,0:T(8,128)(2,1)}, u32[]{:S(2)}) copy-start(bf16[2,7168,64]{1,2,0:T(8,128)(2,1)} %param.8) | copy-start | bytes 5505028
  18.8 10.3 %collective-permute-start.4 = (bf16[32,3328]{1,0:T(8,128)(2,1)S(1)}, bf16[32,3328]{1,0:T(8,128)(2,1)S(1)}, u32[]{:S(2)}, u32[]{:S(2)}) collective-permute-start(bf16[32,3328]{1,0:T(8,128)(2,1)S(1)} %collective-permute-done.2.b2), channel_id=1, source_target_pairs={{0,4},{4,0},{8,12},{12,8},{1,5},{5,1},{9,13},{13,9},{2,6},{6,2},{1... | collective-permute-start | bytes 638984 | tf_op jit(solution)/shard_map/ppermute | solution.py:390
  27.1 6.4 %collective-permute-start.3 = (bf16[32,3840]{1,0:T(8,128)(2,1)S(1)}, bf16[32,3840]{1,0:T(8,128)(2,1)S(1)}, u32[]{:S(2)}, u32[]{:S(2)}) collective-permute-start(bf16[32,3840]{1,0:T(8,128)(2,1)S(1)} %collective-permute-done.1.b2), channel_id=1, source_target_pairs={{0,4},{4,0},{8,12},{12,8},{1,5},{5,1},{9,13},{13,9},{2,6},{6,2},{1... | collective-permute-start | bytes 737288 | tf_op jit(solution)/shard_map/ppermute | solution.py:399
  33.9 1.3 %collective-permute-start.5 = (f32[64,128]{1,0:T(8,128)S(1)}, f32[64,128]{1,0:T(8,128)S(1)}, u32[]{:S(2)}, u32[]{:S(2)}) collective-permute-start(f32[64,128]{1,0:T(8,128)S(1)} %get-tuple-element.67), channel_id=1, source_target_pairs={{0,1},{1,0},{2,3},{3,2},{4,5},{5,4},{6,7},{7,6},{8,9},{9,8},{10,11... | collective-permute-start | bytes 98312 | tf_op jit(solution)/shard_map/ppermute | solution.py:407
  34.9 4.1 %copy-start.2 = (bf16[2,64,8192]{2,1,0:T(8,128)(2,1)S(1)}, bf16[2,64,8192]{2,1,0:T(8,128)(2,1)}, u32[]{:S(2)}) copy-start(bf16[2,64,8192]{2,1,0:T(8,128)(2,1)} %param.9) | copy-start | bytes 6291460
  35.1 3.9 %collective-permute-start.6 = (f32[32,128]{1,0:T(8,128)S(1)}, f32[32,128]{1,0:T(8,128)S(1)}, u32[]{:S(2)}, u32[]{:S(2)}) collective-permute-start(f32[32,128]{1,0:T(8,128)S(1)} %get-tuple-element.75), channel_id=1, source_target_pairs={{0,2},{2,0},{1,3},{3,1},{4,6},{6,4},{5,7},{7,5},{8,10},{10,8},{9,1... | collective-permute-start | bytes 49160 | tf_op jit(solution)/shard_map/ppermute | solution.py:411
  39.6 4.6 %collective-permute-start.7 = (bf16[64,2048]{1,0:T(8,128)(2,1)S(1)}, bf16[64,2048]{1,0:T(8,128)(2,1)S(1)}, u32[]{:S(2)}, u32[]{:S(2)}) collective-permute-start(bf16[64,2048]{1,0:T(8,128)(2,1)S(1)} %get-tuple-element.85), channel_id=1, source_target_pairs={{0,1},{1,0},{2,3},{3,2},{4,5},{5,4},{6,7},{7,6},{8,9},{9,8},{10,11... | collective-permute-start | bytes 786440 | tf_op jit(solution)/shard_map/ppermute | solution.py:417
  39.8 6.7 %collective-permute-start.8 = (bf16[16,2048]{1,0:T(8,128)(2,1)S(1)}, bf16[16,2048]{1,0:T(8,128)(2,1)S(1)}, u32[]{:S(2)}, u32[]{:S(2)}) collective-permute-start(bf16[16,2048]{1,0:T(8,128)(2,1)S(1)} %get-tuple-element.89), channel_id=1, source_target_pairs={{0,12},{4,8},{8,4},{12,0},{1,13},{5,9},{9,5},{13,1},{2,14},{6,10},... | collective-permute-start | bytes 196616 | tf_op jit(solution)/shard_map/ppermute | solution.py:420
  43.5 5.4 %collective-permute-start.9 = (bf16[16,2048]{1,0:T(8,128)(2,1)S(1)}, bf16[16,2048]{1,0:T(8,128)(2,1)S(1)}, u32[]{:S(2)}, u32[]{:S(2)}) collective-permute-start(bf16[16,2048]{1,0:T(8,128)(2,1)S(1)} %get-tuple-element.90), channel_id=1, source_target_pairs={{0,4},{4,0},{8,12},{12,8},{1,5},{5,1},{9,13},{13,9},{2,6},{6,2},{1... | collective-permute-start | bytes 196616 | tf_op jit(solution)/shard_map/ppermute | solution.py:420
  43.5 5.9 %collective-permute-start.10 = (bf16[16,2048]{1,0:T(8,128)(2,1)S(1)}, bf16[16,2048]{1,0:T(8,128)(2,1)S(1)}, u32[]{:S(2)}, u32[]{:S(2)}) collective-permute-start(bf16[16,2048]{1,0:T(8,128)(2,1)S(1)} %get-tuple-element.91), channel_id=1, source_target_pairs={{0,8},{4,12},{8,0},{12,4},{1,9},{5,13},{9,1},{13,5},{2,10},{6,14},... | collective-permute-start | bytes 196616 | tf_op jit(solution)/shard_map/ppermute | solution.py:420
  44.3 5.2 %collective-permute-start.11 = (bf16[32,2048]{1,0:T(8,128)(2,1)S(1)}, bf16[32,2048]{1,0:T(8,128)(2,1)S(1)}, u32[]{:S(2)}, u32[]{:S(2)}) collective-permute-start(bf16[32,2048]{1,0:T(8,128)(2,1)S(1)} %get-tuple-element.92), channel_id=1, source_target_pairs={{0,2},{2,0},{1,3},{3,1},{4,6},{6,4},{5,7},{7,5},{8,10},{10,8},{9,1... | collective-permute-start | bytes 393224 | tf_op jit(solution)/shard_map/ppermute | solution.py:423
